TPU v7x, 32 devices: a whole 2x2x4 slice. The times are simulated.
32 devices in a mesh: grp: 2 (over y), ep: 4 (over z), tp: 4 (over x, core).
Axes of the slice: x: 2, y: 2, z: 4, core: 2. Of those that a mesh axis runs over, the one named last changes fastest.
Arguments:
- tokens: bfloat16 [1536, 5120], P(('grp', 'ep'), 'tp'), parts along dimension 0, may hold values from -6 to 6
- expert_ids: int32 [1536, 6], P(('grp', 'ep')), parts along dimension 0, may hold values from 0 to 31, all different within a row; in each aligned block of 192 rows (0 to 191, 192 to 383, ...) at most 48 rows name the same one
- gate_weights: bfloat16 [1536, 6], P(('grp', 'ep')), parts along dimension 0, may hold values from 0.049804688 to 1
- gu_weight: bfloat16 [32, 1024, 2, 5120], P('ep', None, None, 'tp'), may hold values from -0.078125 to 0.078125
- down_weight: bfloat16 [32, 1024, 5120], P('ep', None, 'tp'), may hold values from -0.1875 to 0.1875
Outputs:
- mixed: bfloat16 [1536, 5120], P(('grp', 'ep'), 'tp'), parts along dimension 0
There are 2 independent parts, one for each index of `grp`. A program takes and returns all parts, laid end to end along the dimension named above; an argument that names none is the same for every part. Nothing has to cross between parts.
Inputs may be any that keep to these rules, and one draw needn't show every extreme that they name: `expert_ids`: each token names 6 different experts. Among the 192 tokens of one block no expert is named more than 48 times, and in every draw some expert is named exactly 48 times in some block.
All inputs are finite; a program needn't handle non-finite values.
Results may differ from a plain program's by a relative error of at most 0.019.
Values may be sent and summed in bfloat16 or wider, within the bound.
No kernel may reach another device: no remote copies, remote signals or barrier semaphores. Data moves between devices by JAX's collectives and lax.ppermute only.
A program may use at most 192 MiB of HBM per device.

v0:
```python
import functools

import jax
import jax.numpy as jnp
from jax import lax
from jax.experimental import pallas as pl
from jax.experimental.pallas import tpu as pltpu
from jax.sharding import PartitionSpec as P

EXPERTS = 32
TOPK = 6
CAP = 48
LANES = 128
BF16, F32 = jnp.bfloat16, jnp.float32
NT = (((1,), (1,)), ((), ()))
TN = (((0,), (0,)), ((), ()))
NN = (((1,), (0,)), ((), ()))

PAIR = [(0, 1), (1, 0), (2, 3), (3, 2)]
MIDDLE = [(1, 2), (2, 1)]
OUTWARD = [(1, 0), (2, 3)]
INWARD = [(0, 1), (3, 2)]
ACROSS_X = [(0, 2), (1, 3), (2, 0), (3, 1)]
ACROSS_CORE = [(0, 1), (1, 0), (2, 3), (3, 2)]


QUICK = pl.CostEstimate(flops=1024, bytes_accessed=1024, transcendentals=0)


SLOW = pl.CostEstimate(flops=20_000_000_000, bytes_accessed=1024, transcendentals=0)


def params(mib):
    return pltpu.CompilerParams(vmem_limit_bytes=mib << 20)


def route_kernel(ids_ref, gates_ref, out_ref):
    count = ids_ref.shape[1]
    expert = lax.broadcasted_iota(jnp.int32, (EXPERTS, count), 0)
    weight = jnp.zeros((EXPERTS, count), F32)
    chosen = jnp.zeros((EXPERTS, count), F32)
    for k in range(TOPK):
        hit = ids_ref[k : k + 1, :] == expert
        chosen = jnp.where(hit, 1.0, chosen)
        weight = jnp.where(hit, gates_ref[k : k + 1, :], weight)
    first = lax.broadcasted_iota(jnp.int32, (count, count), 0)
    second = lax.broadcasted_iota(jnp.int32, (count, count), 1)
    before = jnp.where(first < second, 1.0, 0.0).astype(BF16)
    position = lax.dot_general(chosen.astype(BF16), before, NN, preferred_element_type=F32)
    out_ref[:EXPERTS, :] = jnp.where(chosen > 0.0, position, -1.0)
    out_ref[EXPERTS:, :] = weight


def route(expert_ids, gate_weights):
    return pl.pallas_call(
        route_kernel,
        out_shape=jax.ShapeDtypeStruct((2 * EXPERTS, expert_ids.shape[0]), F32),
        name="route",
    )(expert_ids.T, gate_weights.T.astype(F32))


def place_kernel(experts, where_ref, *refs):
    *token_refs, table_ref, out_ref = refs
    count = table_ref.shape[1]
    slot_of = lax.broadcasted_iota(jnp.int32, (CAP, count), 0).astype(F32)
    table = [
        jnp.where(table_ref[pl.ds(where_ref[0] + e, 1), :] == slot_of, 1.0, 0.0)
        for e in range(experts)
    ]
    tokens = token_refs[0][...]
    for extra in token_refs[1:]:
        tokens = tokens + extra[...]
    table = jnp.concatenate(table, axis=0).astype(BF16)
    rows = lax.dot_general(table, tokens, NN, preferred_element_type=F32).astype(BF16)
    for e in range(experts):
        out_ref[e] = rows[e * CAP : (e + 1) * CAP]


def place(where, tokens, table, experts):
    whole = pl.BlockSpec(memory_space=pltpu.VMEM)
    return pl.pallas_call(
        functools.partial(place_kernel, experts),
        out_shape=jax.ShapeDtypeStruct((experts, CAP, tokens[0].shape[1]), BF16),
        in_specs=[pl.BlockSpec(memory_space=pltpu.SMEM)] + [whole] * (len(tokens) + 1),
        out_specs=whole,
        compiler_params=params(24),
        cost_estimate=QUICK,
        name="place",
    )(where, *tokens, table)


def gate_up_kernel(n_blocks, where_ref, *refs):
    row_refs = refs[:n_blocks]
    w_ref, _, send_ref, keep_ref, rows_ref, carry = refs[n_blocks:]
    step = pl.program_id(0)
    rows = n_blocks * CAP
    spare = 2 * LANES - rows
    x, core = where_ref[1], where_ref[2]
    quarter = w_ref.shape[1] // 4

    @pl.when(step == 0)
    def _():
        rows_ref[...] = jnp.zeros_like(rows_ref)

    def product(parity):
        for i in range(n_blocks):
            at = parity * spare + i * CAP
            rows_ref[parity, at : at + CAP, :] = row_refs[i][0]
        w = w_ref[0].reshape(8 * quarter, w_ref.shape[3])
        return lax.dot_general(w, rows_ref[parity], NT, preferred_element_type=F32)

    def store(tile, lane):
        tile = tile.astype(BF16)
        for q in range(4):
            piece = tile[2 * q * quarter : 2 * (q + 1) * quarter]
            at = jnp.where(x == q // 2, 1, 0)

            @pl.when(core == q % 2)
            def _():
                keep_ref[at, :, lane : lane + LANES] = piece

            @pl.when(core != q % 2)
            def _():
                send_ref[at, :, lane : lane + LANES] = piece

    @pl.when(lax.rem(step, 2) == 0)
    def _():
        out = product(0)
        store(out[:, :LANES], 0)
        carry[...] = out[:, LANES:]

    @pl.when(lax.rem(step, 2) == 1)
    def _():
        out = product(1)
        store(carry[...] + out[:, :LANES], LANES)
        store(out[:, LANES:], 2 * LANES)


def gate_up(where, placed, gu_weight, chunk, group, after):
    _, units, _, width = gu_weight.shape
    n_blocks = len(placed)
    lanes = 2 * n_blocks * CAP
    half = jax.ShapeDtypeStruct((2, units // 2, group // 2 * lanes), BF16)
    pair = pl.BlockSpec((2, units // 2, lanes), lambda i: (0, 0, i // 2))
    return pl.pallas_call(
        functools.partial(gate_up_kernel, n_blocks),
        grid=(group,),
        out_shape=(half, half),
        in_specs=[pl.BlockSpec(memory_space=pltpu.SMEM)]
        + [pl.BlockSpec((1, CAP, width), lambda i: (chunk * group + i, 0, 0))] * n_blocks
        + [pl.BlockSpec((1, units, 2, width), lambda i: (chunk * group + i, 0, 0, 0))]
        + [pl.BlockSpec(memory_space=pl.ANY)],
        out_specs=(pair, pair),
        scratch_shapes=[
            pltpu.VMEM((2, 2 * LANES, width), BF16),
            pltpu.VMEM((2 * units, LANES), F32),
        ],
        compiler_params=params(48),
        cost_estimate=QUICK,
        name="gate_up",
    )(where, *placed, gu_weight, after)


def hidden_kernel(keep_ref, near_ref, far_ref, _, out_ref, sums):
    units = out_ref.shape[1]
    for n in range(sums.shape[0]):
        lanes = slice(n * LANES, (n + 1) * LANES)
        total = keep_ref[0, :, lanes].astype(F32) + near_ref[0, :, lanes].astype(F32)
        sums[n] = total + far_ref[:, lanes].astype(F32)
        gate = sums[n, pl.ds(0, units, stride=2), :]
        up = sums[n, pl.ds(1, units, stride=2), :]
        out_ref[lanes, :] = (gate / (1.0 + jnp.exp(-gate)) * up).T.astype(BF16)


def hidden_quarter(keep, near, far, after):
    _, doubled, columns = keep.shape
    mine = pl.BlockSpec((1, doubled, columns), lambda i: (1, 0, 0))
    return pl.pallas_call(
        hidden_kernel,
        grid=(1,),
        out_shape=jax.ShapeDtypeStruct((columns, doubled // 2), BF16),
        in_specs=[
            mine,
            mine,
            pl.BlockSpec((doubled, columns), lambda i: (0, 0)),
            pl.BlockSpec(memory_space=pl.ANY),
        ],
        out_specs=pl.BlockSpec((columns, doubled // 2), lambda i: (0, 0)),
        scratch_shapes=[pltpu.VMEM((columns // LANES, doubled, LANES), F32)],
        compiler_params=params(24),
        cost_estimate=SLOW,
        name="hidden",
    )(keep, near, far, after)


def add_kernel(keep_ref, near_ref, _, out_ref):
    out_ref[...] = (keep_ref[0].astype(F32) + near_ref[0].astype(F32)).astype(BF16)


def chip_sum(keep, near, after):
    _, doubled, columns = keep.shape
    other = pl.BlockSpec((1, doubled, columns), lambda i: (0, 0, 0))
    return pl.pallas_call(
        add_kernel,
        grid=(1,),
        out_shape=jax.ShapeDtypeStruct((doubled, columns), BF16),
        in_specs=[other, other, pl.BlockSpec(memory_space=pl.ANY)],
        out_specs=pl.BlockSpec((doubled, columns), lambda i: (0, 0)),
        compiler_params=params(24),
        cost_estimate=QUICK,
        name="chip_sum",
    )(keep, near, after)


def down_kernel(group, n_blocks, chunk, has_carry, where_ref, *refs):
    hidden_refs, refs = refs[:4], refs[4:]
    route_refs, refs = refs[:n_blocks], refs[n_blocks:]
    w_hbm, refs = refs[0], refs[2:]
    carry_ref, refs = (refs[0], refs[1:]) if has_carry else (None, refs)
    out_refs, (held, w_buf, sems) = refs[:-3], refs[-3:]
    rows = n_blocks * CAP
    quarter = w_hbm.shape[1] // 4
    count = route_refs[0].shape[1]
    expert0 = where_ref[0]
    x, core = where_ref[1], where_ref[2]
    order = [(x, core), (1 - x, core), (x, 1 - core), (1 - x, 1 - core)]

    def fetch(e):
        copies = []
        for j in range(4):
            f0 = pl.multiple_of((order[j][0] * 2 + order[j][1]) * quarter, quarter)
            copies.append(
                pltpu.make_async_copy(
                    w_hbm.at[chunk * group + e, pl.ds(f0, quarter)],
                    w_buf.at[e, pl.ds(j * quarter, quarter)],
                    sems.at[e, j],
                )
            )
        return copies

    def start(e):
        for copy in fetch(e):
            copy.start()

    start(0)
    start(1)
    for e in range(group):
        for copy in fetch(e):
            copy.wait()
        if e + 2 < group:
            start(e + 2)
        units = jnp.concatenate([h[e * rows : (e + 1) * rows, :] for h in hidden_refs], axis=1)
        out = lax.dot_general(units, w_buf[e], NN, preferred_element_type=F32).astype(BF16)
        for i in range(n_blocks):
            held[i, e * CAP : (e + 1) * CAP, :] = out[i * CAP : (i + 1) * CAP]
    slot_of = lax.broadcasted_iota(jnp.int32, (CAP, count), 0).astype(F32)
    for i in range(n_blocks):
        table = [
            jnp.where(
                route_refs[i][pl.ds(expert0 + e, 1), :] == slot_of,
                route_refs[i][pl.ds(EXPERTS + expert0 + e, 1), :],
                0.0,
            )
            for e in range(group)
        ]
        table = jnp.concatenate(table, axis=0).astype(BF16)
        total = lax.dot_general(table, held[i], TN, preferred_element_type=F32)
        if has_carry:
            out_refs[i][...] = (total + carry_ref[i]).astype(BF16)
        else:
            out_refs[0][i] = total


def down(where, hidden, routes, down_weight, chunk, group, carry, after):
    n_blocks = len(routes)
    units = hidden[0].shape[1]
    count = routes[0].shape[1]
    width = down_weight.shape[2]
    whole = pl.BlockSpec(memory_space=pltpu.VMEM)
    carried = [] if carry is None else [carry]
    if carry is None:
        out_shape = (jax.ShapeDtypeStruct((n_blocks, count, width), F32),)
    else:
        out_shape = tuple(jax.ShapeDtypeStruct((count, width), BF16) for _ in routes)
    return pl.pallas_call(
        functools.partial(down_kernel, group, n_blocks, chunk, carry is not None),
        out_shape=out_shape,
        in_specs=[pl.BlockSpec(memory_space=pltpu.SMEM)]
        + [whole] * (4 + n_blocks)
        + [pl.BlockSpec(memory_space=pl.ANY)] * 2
        + [whole] * len(carried),
        out_specs=tuple(whole for _ in out_shape),
        scratch_shapes=[
            pltpu.VMEM((n_blocks, group * CAP, width), BF16),
            pltpu.VMEM((group, 4 * units, width), BF16),
            pltpu.SemaphoreType.DMA((group, 4)),
        ],
        compiler_params=params(40),
        cost_estimate=QUICK,
        name="down",
    )(where, *hidden, *routes, down_weight, after, *carried)


def plus_kernel(a_ref, b_ref, _, out_ref, __):
    out_ref[...] = (a_ref[...].astype(F32) + b_ref[...].astype(F32)).astype(BF16)


def plus_then(a, b, other):
    whole = pl.BlockSpec(memory_space=pltpu.VMEM)
    free = pl.BlockSpec(memory_space=pl.ANY)
    return pl.pallas_call(
        plus_kernel,
        out_shape=(jax.ShapeDtypeStruct(a.shape, a.dtype), jax.ShapeDtypeStruct(a.shape, a.dtype)),
        in_specs=[whole, whole, free],
        out_specs=(whole, free),
        input_output_aliases={2: 1},
        compiler_params=params(16),
        cost_estimate=QUICK,
        name="plus",
    )(a, b, other)


def local_square(tokens, expert_ids, gate_weights, gu_weight, down_weight):
    z, t = lax.axis_index("ep"), lax.axis_index("tp")
    x, core = t // 2, t % 2
    local = gu_weight.shape[0]
    group = local // 2
    wheres = [jnp.stack([z * local + n * group, x, core]).astype(jnp.int32) for n in range(2)]

    def hop(array, pairs):
        return lax.ppermute(array, "ep", pairs)

    table = route(expert_ids, gate_weights)
    neighbour = hop(tokens, PAIR)
    table_1 = hop(table, PAIR)
    middle_1 = hop(tokens, MIDDLE)
    table_2 = hop(table, [(i, i ^ 2) for i in range(4)])
    table_3 = hop(table, [(i, i ^ 3) for i in range(4)])
    inner = (z == 1) | (z == 2)
    table_in = jnp.where(inner, table_3, table_2)
    table_out = jnp.where(inner, table_2, table_3)
    middle_2 = hop(neighbour, MIDDLE)
    end_1 = hop(middle_1, OUTWARD)
    end_2 = hop(middle_2, OUTWARD)

    tables = [table, table_1, table_in, table_out]
    blocks = [(tokens,), (neighbour,), (middle_1, end_1), (middle_2, end_2)]
    placed = [place(wheres[0], b, t, local) for b, t in zip(blocks, tables)]

    def sums(n, after):
        send, keep = gate_up(wheres[n], placed, gu_weight, n, group, after)
        return keep, lax.ppermute(send, "tp", ACROSS_CORE)

    def across(keep, near, after):
        total = chip_sum(keep, near, after)
        return total, lax.ppermute(total, "tp", ACROSS_X)

    def gathered(own):
        own_x = lax.ppermute(own, "tp", ACROSS_X)
        own_core = lax.ppermute(own, "tp", ACROSS_CORE)
        return own, own_x, own_core, lax.ppermute(own_x, "tp", ACROSS_CORE)

    keep_0, near_0 = sums(0, placed[3])
    turn, far_0 = across(keep_0, near_0, keep_0)
    keep_1, near_1 = sums(1, turn)
    own_0 = hidden_quarter(keep_0, near_0, far_0, keep_1)
    hidden_0 = gathered(own_0)
    turn, far_1 = across(keep_1, near_1, own_0)
    (carry,) = down(wheres[0], hidden_0, tables, down_weight, 0, group, None, turn)
    own_1 = hidden_quarter(keep_1, near_1, far_1, carry)
    hidden_1 = gathered(own_1)
    own, other, far_in, far_out = down(
        wheres[1], hidden_1, tables, down_weight, 1, group, carry, own_1
    )

    def plus(a, b):
        return (a.astype(F32) + b.astype(F32)).astype(BF16)

    out_inner = hop(far_out, INWARD)
    far_out, far_in = plus_then(far_out, out_inner, far_in)
    out_mid = hop(far_out, MIDDLE)
    in_inner = hop(far_in, INWARD)
    last = hop(plus(other, out_mid), PAIR)
    in_mid = hop(plus(far_in, in_inner), MIDDLE)
    return (own.astype(F32) + in_mid.astype(F32) + last.astype(F32)).astype(BF16)


def local_general(tokens, expert_ids, gate_weights, gu_weight, down_weight):
    tok_rows, local_width = tokens.shape
    table = route(expert_ids, gate_weights)
    slots = jnp.arange(CAP, dtype=jnp.int32).astype(F32)
    matches = table[:EXPERTS, None, :] == slots[None, :, None]
    dispatch_table = matches.astype(BF16).reshape(EXPERTS * CAP, tok_rows)
    outgoing = jnp.dot(dispatch_table, tokens, preferred_element_type=F32)
    outgoing = outgoing.astype(BF16).reshape(EXPERTS, CAP, local_width)
    received = lax.all_to_all(outgoing, "ep", split_axis=0, concat_axis=1, tiled=True)
    terms = jnp.einsum("efgd,esd->fegs", gu_weight, received, preferred_element_type=F32)
    totals = lax.psum(terms.astype(BF16), "tp").astype(F32)
    hidden = (jax.nn.silu(totals[:, :, 0]) * totals[:, :, 1]).astype(BF16)
    expert_out = jnp.einsum("fes,efd->esd", hidden, down_weight, preferred_element_type=F32)
    returned = lax.all_to_all(
        expert_out.astype(BF16), "ep", split_axis=1, concat_axis=0, tiled=True
    )
    combine_table = jnp.where(matches, table[EXPERTS:, None, :], 0.0).astype(BF16)
    mixed = lax.dot_general(
        combine_table.reshape(EXPERTS * CAP, tok_rows),
        returned.reshape(EXPERTS * CAP, local_width),
        TN,
        preferred_element_type=F32,
    )
    return mixed.astype(BF16)


def solution(mesh):
    placed = (
        P(("grp", "ep"), "tp"),
        P(("grp", "ep"), None),
        P(("grp", "ep"), None),
        P("ep", None, None, "tp"),
        P("ep", None, "tp"),
    )
    square = mesh.shape["ep"] == 4 and mesh.shape["tp"] == 4
    return jax.shard_map(
        local_square if square else local_general,
        mesh=mesh,
        in_specs=placed,
        out_specs=P(("grp", "ep"), "tp"),
        check_vma=False,
    )
```

profile of v0, /device:TPU:0, one launch (start us, length us, event | category | flops | bytes accessed | tf_op | source)
XLA Modules:
  0.0 180.0 jit_solution(15796791455009656915)
XLA Ops:
  0.0 3.0 %collective-permute-start = (bf16[192,1280]{1,0:T(8,128)(2,1)}, bf16[192,1280]{1,0:T(8,128)(2,1)S(1)}, u32[]{:S(2)}, u32[]{:S(2)}) collective-permute-start(bf16[192,1280]{1,0:T(8,128)(2,1)} %refs_0_.1), channel_id=1, source_target_pairs={{0,4},{4,0},{8,12},{12,8},{1,5},{5,1},{9,13},{13,9},{2,6},{6,2},{1... | collective-permute-start | bytes 1474568 | tf_op jit(solution)/shard_map/ppermute | solution.py:331
  3.7 10.7 %collective-permute-done.refs_0_ = bf16[192,1280]{1,0:T(8,128)(2,1)S(1)} collective-permute-done((bf16[192,1280]{1,0:T(8,128)(2,1)}, bf16[192,1280]{1,0:T(8,128)(2,1)S(1)}, u32[]{:S(2)}, u32[]{:S(2)}) %collective-permute-start) | collective-permute-done | bytes 491552 | tf_op jit(solution)/shard_map/ppermute | solution.py:331
  19.8 1.5 route.1.refs_1_.refs_4_
  21.3 14.7 %collective-permute-start.5 = (f32[64,192]{1,0:T(8,128)}, f32[64,192]{1,0:T(8,128)S(1)}, u32[]{:S(2)}, u32[]{:S(2)}) collective-permute-start(f32[64,192]{1,0:T(8,128)} %route.1.refs_1_.refs_4_), channel_id=1, source_target_pairs={{0,8},{4,12},{8,0},{12,4},{1,9},{5,13},{9,1},{13,5},{2,10},{6,14},... | collective-permute-start | bytes 147464 | tf_op jit(solution)/shard_map/ppermute | solution.py:331
  36.0 1.3 collective-permute-start.4
  40.3 2.1 %collective-permute-done.4 = f32[64,192]{1,0:T(8,128)S(1)} collective-permute-done((f32[64,192]{1,0:T(8,128)}, f32[64,192]{1,0:T(8,128)S(1)}, u32[]{:S(2)}, u32[]{:S(2)}) %collective-permute-start.4) | collective-permute-done | bytes 49184 | tf_op jit(solution)/shard_map/ppermute | solution.py:331
  42.4 4.1 %collective-permute-done.1.refs_1_.refs_5_ = f32[64,192]{1,0:T(8,128)S(1)} collective-permute-done((f32[64,192]{1,0:T(8,128)}, f32[64,192]{1,0:T(8,128)S(1)}, u32[]{:S(2)}, u32[]{:S(2)}) %collective-permute-start.1) | collective-permute-done | bytes 49184 | tf_op jit(solution)/shard_map/ppermute | solution.py:331
  48.6 1.5 place.6.refs_2_
  50.1 1.8 place.7.refs_3_.refs_5_
  51.9 12.0 %gate_up.2 = (bf16[2,512,768]{2,1,0:T(8,128)(2,1)S(1)}, bf16[2,512,768]{2,1,0:T(8,128)(2,1)}) custom-call(s32[3]{0:T(128)S(1)} %add_add_fusion.1.where_ref, bf16[8,48,1280]{2,1,0:T(8,128)(2,1)S(1)} %place.4.refs_0_, bf16[8,48,1280]{2,1,0:T(8,128)(2,1)S(1)} %place.5.refs_1_, bf16[8,48,1280]{2,1,0:T(8,128)(2,1)S(1)} %place.6.refs_2_, ...), custom_call_target="tpu_custom_call" | custom-call | flops 1024 | bytes 1024 | tf_op jit(solution)/shard_map/gate_up/pallas_call | solution.py:145
  63.9 3.4 %collective-permute-done.8.near_ref = bf16[2,512,768]{2,1,0:T(8,128)(2,1)S(1)} collective-permute-done((bf16[2,512,768]{2,1,0:T(8,128)(2,1)S(1)}, bf16[2,512,768]{2,1,0:T(8,128)(2,1)S(1)}, u32[]{:S(2)}, u32[]{:S(2)}) %collective-permute-start.8) | collective-permute-done | bytes 1572896 | tf_op jit(solution)/shard_map/ppermute | solution.py:352
  67.3 2.0 %copy-done.2 = bf16[2,512,768]{2,1,0:T(8,128)(2,1)S(1)} copy-done((bf16[2,512,768]{2,1,0:T(8,128)(2,1)S(1)}, bf16[2,512,768]{2,1,0:T(8,128)(2,1)}, u32[]{:S(2)}) %copy-start.2) | copy-done | bytes 1572888
  70.4 1.5 collective-permute-start.10
  73.2 12.7 %gate_up.3 = (bf16[2,512,768]{2,1,0:T(8,128)(2,1)}, bf16[2,512,768]{2,1,0:T(8,128)(2,1)}) custom-call(s32[3]{0:T(128)S(1)} %add_add_fusion.where_ref, bf16[8,48,1280]{2,1,0:T(8,128)(2,1)S(1)} %place.4.refs_0_, bf16[8,48,1280]{2,1,0:T(8,128)(2,1)S(1)} %place.5.refs_1_, bf16[8,48,1280]{2,1,0:T(8,128)(2,1)S(1)} %copy-done.1, ...), custom_call_target="tpu_custom_call" | custom-call | flops 1024 | bytes 1024 | tf_op jit(solution)/shard_map/gate_up/pallas_call | solution.py:145
  85.9 4.4 %collective-permute-done.10.far_ref = bf16[512,768]{1,0:T(8,128)(2,1)} collective-permute-done((bf16[512,768]{1,0:T(8,128)(2,1)}, bf16[512,768]{1,0:T(8,128)(2,1)}, u32[]{:S(2)}, u32[]{:S(2)}) %collective-permute-start.10) | collective-permute-done | bytes 786464 | tf_op jit(solution)/shard_map/ppermute | solution.py:356
  90.4 1.4 copy-done.4
  91.8 1.8 %hidden.2._.refs_0_ = bf16[768,256]{1,0:T(8,128)(2,1)S(1)} custom-call(bf16[2,512,768]{2,1,0:T(8,128)(2,1)S(1)} %copy-done.3, bf16[2,512,768]{2,1,0:T(8,128)(2,1)S(1)} %copy-done.7, bf16[512,768]{1,0:T(8,128)(2,1)} %collective-permute-done.10.far_ref, bf16[2,512,768]{2,1,0:T(8,128)(2,1)S(1)} %copy-done.4), custom_call_target="tpu_custom_call" | custom-call | flops 20000000000 | bytes 1024 | tf_op jit(solution)/shard_map/hidden/pallas_call | solution.py:178
  93.6 1.6 collective-permute-start.12
  96.0 9.8 %collective-permute-done.12.refs_1_ = bf16[768,256]{1,0:T(8,128)(2,1)S(1)} collective-permute-done((bf16[768,256]{1,0:T(8,128)(2,1)S(1)}, bf16[768,256]{1,0:T(8,128)(2,1)S(1)}, u32[]{:S(2)}, u32[]{:S(2)}) %collective-permute-start.12) | collective-permute-done | bytes 393248 | tf_op jit(solution)/shard_map/ppermute | solution.py:359
  105.7 1.7 collective-permute-done.14.refs_3_
  107.4 6.3 %down.2._.refs_10_ = f32[4,192,1280]{2,1,0:T(8,128)S(1)} custom-call(s32[3]{0:T(128)S(1)} %add_add_fusion.1.where_ref, bf16[768,256]{1,0:T(8,128)(2,1)S(1)} %hidden.2._.refs_0_, bf16[768,256]{1,0:T(8,128)(2,1)S(1)} %collective-permute-done.12.refs_1_, bf16[768,256]{1,0:T(8,128)(2,1)S(1)} %collective-permute-done.13.refs_2_, ...), custom_call_target="tpu_custom_call" | custom-call | flops 1024 | bytes 1024 | tf_op jit(solution)/shard_map/down/pallas_call | solution.py:285
  113.8 7.1 %collective-permute-done.11.far_ref = bf16[512,768]{1,0:T(8,128)(2,1)S(1)} collective-permute-done((bf16[512,768]{1,0:T(8,128)(2,1)S(1)}, bf16[512,768]{1,0:T(8,128)(2,1)S(1)}, u32[]{:S(2)}, u32[]{:S(2)}) %collective-permute-start.11) | collective-permute-done | bytes 786464 | tf_op jit(solution)/shard_map/ppermute | solution.py:356
  121.5 1.6 collective-permute-start.15
  123.1 7.9 %collective-permute-done.15.refs_1_ = bf16[768,256]{1,0:T(8,128)(2,1)S(1)} collective-permute-done((bf16[768,256]{1,0:T(8,128)(2,1)S(1)}, bf16[768,256]{1,0:T(8,128)(2,1)S(1)}, u32[]{:S(2)}, u32[]{:S(2)}) %collective-permute-start.15) | collective-permute-done | bytes 393248 | tf_op jit(solution)/shard_map/ppermute | solution.py:359
  131.0 1.7 collective-permute-done.17.refs_3_
  132.7 6.3 %down.3 = (bf16[192,1280]{1,0:T(8,128)(2,1)S(1)}, bf16[192,1280]{1,0:T(8,128)(2,1)S(1)}, bf16[192,1280]{1,0:T(8,128)(2,1)S(1)}, bf16[192,1280]{1,0:T(8,128)(2,1)S(1)}) custom-call(s32[3]{0:T(128)S(1)} %add_add_fusion.where_ref, bf16[768,256]{1,0:T(8,128)(2,1)S(1)} %hidden.3.refs_0_.refs_9_, bf16[768,256]{1,0:T(8,128)(2,1)S(1)} %collective-permute-done.15.refs_1_, ...), custom_call_target="tpu_custom_call" | custom-call | flops 1024 | bytes 1024 | tf_op jit(solution)/shard_map/down/pallas_call | solution.py:285
  139.1 1.6 collective-permute-start.18
  140.7 10.7 %collective-permute-done.18.b_ref = bf16[192,1280]{1,0:T(8,128)(2,1)S(1)} collective-permute-done((bf16[192,1280]{1,0:T(8,128)(2,1)S(1)}, bf16[192,1280]{1,0:T(8,128)(2,1)S(1)}, u32[]{:S(2)}, u32[]{:S(2)}) %collective-permute-start.18) | collective-permute-done | bytes 491552 | tf_op jit(solution)/shard_map/ppermute | solution.py:331
  152.2 6.6 %collective-permute-start.19 = (bf16[192,1280]{1,0:T(8,128)(2,1)S(1)}, bf16[192,1280]{1,0:T(8,128)(2,1)S(1)}, u32[]{:S(2)}, u32[]{:S(2)}) collective-permute-start(bf16[192,1280]{1,0:T(8,128)(2,1)S(1)} %get-tuple-element.22), channel_id=1, source_target_pairs={{0,4},{12,8},{1,5},{13,9},{2,6},{14,10},{3,7},{15,11},{16,20},{28,... | collective-permute-start | bytes 1474568 | tf_op jit(solution)/shard_map/ppermute | solution.py:331
  159.0 9.5 %collective-permute-start.22 = (bf16[192,1280]{1,0:T(8,128)(2,1)S(1)}, bf16[192,1280]{1,0:T(8,128)(2,1)S(1)}, u32[]{:S(2)}, u32[]{:S(2)}) collective-permute-start(bf16[192,1280]{1,0:T(8,128)(2,1)S(1)} %add_convert_fusion.1), channel_id=1, source_target_pairs={{0,4},{4,0},{8,12},{12,8},{1,5},{5,1},{9,13},{13,9},{2,6},{6,2},{1... | collective-permute-start | bytes 1474568 | tf_op jit(solution)/shard_map/ppermute | solution.py:331
  168.5 1.4 collective-permute-done.19
  170.8 8.3 %collective-permute-done.22 = bf16[192,1280]{1,0:T(8,128)(2,1)S(1)} collective-permute-done((bf16[192,1280]{1,0:T(8,128)(2,1)S(1)}, bf16[192,1280]{1,0:T(8,128)(2,1)S(1)}, u32[]{:S(2)}, u32[]{:S(2)}) %collective-permute-start.22) | collective-permute-done | bytes 491552 | tf_op jit(solution)/shard_map/ppermute | solution.py:331
  (65 shorter events, 17.5 us)
Async XLA Ops:
  0.0 14.5 %collective-permute-start = (bf16[192,1280]{1,0:T(8,128)(2,1)}, bf16[192,1280]{1,0:T(8,128)(2,1)S(1)}, u32[]{:S(2)}, u32[]{:S(2)}) collective-permute-start(bf16[192,1280]{1,0:T(8,128)(2,1)} %refs_0_.1), channel_id=1, source_target_pairs={{0,4},{4,0},{8,12},{12,8},{1,5},{5,1},{9,13},{13,9},{2,6},{6,2},{1... | collective-permute-start | bytes 1474568 | tf_op jit(solution)/shard_map/ppermute | solution.py:331
  3.0 12.9 %collective-permute-start.2 = (bf16[192,1280]{1,0:T(8,128)(2,1)}, bf16[192,1280]{1,0:T(8,128)(2,1)S(1)}, u32[]{:S(2)}, u32[]{:S(2)}) collective-permute-start(bf16[192,1280]{1,0:T(8,128)(2,1)} %refs_0_.1), channel_id=1, source_target_pairs={{4,8},{8,4},{5,9},{9,5},{6,10},{10,6},{7,11},{11,7},{20,24},{24,20... | collective-permute-start | bytes 1474568 | tf_op jit(solution)/shard_map/ppermute | solution.py:331
  14.5 2.8 %collective-permute-start.6 = (bf16[192,1280]{1,0:T(8,128)(2,1)S(1)}, bf16[192,1280]{1,0:T(8,128)(2,1)S(1)}, u32[]{:S(2)}, u32[]{:S(2)}) collective-permute-start(bf16[192,1280]{1,0:T(8,128)(2,1)S(1)} %collective-permute-done.refs_0_), channel_id=1, source_target_pairs={{4,8},{8,4},{5,9},{9,5},{6,10},{10,6},{7,11},{11,7},{20,24},{24,20... | collective-permute-start | bytes 1474568 | tf_op jit(solution)/shard_map/ppermute | solution.py:331
  15.9 32.6 %collective-permute-start.3 = (bf16[192,1280]{1,0:T(8,128)(2,1)S(1)}, bf16[192,1280]{1,0:T(8,128)(2,1)}, u32[]{:S(2)}, u32[]{:S(2)}) collective-permute-start(bf16[192,1280]{1,0:T(8,128)(2,1)S(1)} %collective-permute-done.2.refs_0_), channel_id=1, source_target_pairs={{4,0},{8,12},{5,1},{9,13},{6,2},{10,14},{7,3},{11,15},{20,16},{24,... | collective-permute-start | bytes 1474568 | tf_op jit(solution)/shard_map/ppermute | solution.py:331
  17.2 31.3 %copy-start.11 = (bf16[192,1280]{1,0:T(8,128)(2,1)}, bf16[192,1280]{1,0:T(8,128)(2,1)S(1)}, u32[]{:S(2)}) copy-start(bf16[192,1280]{1,0:T(8,128)(2,1)S(1)} %collective-permute-done.6.refs_0_) | copy-start | bytes 1474564
  17.2 32.8 %collective-permute-start.7 = (bf16[192,1280]{1,0:T(8,128)(2,1)S(1)}, bf16[192,1280]{1,0:T(8,128)(2,1)}, u32[]{:S(2)}, u32[]{:S(2)}) collective-permute-start(bf16[192,1280]{1,0:T(8,128)(2,1)S(1)} %collective-permute-done.6.refs_0_), channel_id=1, source_target_pairs={{4,0},{8,12},{5,1},{9,13},{6,2},{10,14},{7,3},{11,15},{20,16},{24,... | collective-permute-start | bytes 1474568 | tf_op jit(solution)/shard_map/ppermute | solution.py:331
  21.3 19.0 %collective-permute-start.5 = (f32[64,192]{1,0:T(8,128)}, f32[64,192]{1,0:T(8,128)S(1)}, u32[]{:S(2)}, u32[]{:S(2)}) collective-permute-start(f32[64,192]{1,0:T(8,128)} %route.1.refs_1_.refs_4_), channel_id=1, source_target_pairs={{0,8},{4,12},{8,0},{12,4},{1,9},{5,13},{9,1},{13,5},{2,10},{6,14},... | collective-permute-start | bytes 147464 | tf_op jit(solution)/shard_map/ppermute | solution.py:331
  36.0 6.4 %collective-permute-start.4 = (f32[64,192]{1,0:T(8,128)}, f32[64,192]{1,0:T(8,128)S(1)}, u32[]{:S(2)}, u32[]{:S(2)}) collective-permute-start(f32[64,192]{1,0:T(8,128)} %route.1.refs_1_.refs_4_), channel_id=1, source_target_pairs={{0,12},{4,8},{8,4},{12,0},{1,13},{5,9},{9,5},{13,1},{2,14},{6,10},... | collective-permute-start | bytes 147464 | tf_op jit(solution)/shard_map/ppermute | solution.py:331
  37.4 9.1 %collective-permute-start.1 = (f32[64,192]{1,0:T(8,128)}, f32[64,192]{1,0:T(8,128)S(1)}, u32[]{:S(2)}, u32[]{:S(2)}) collective-permute-start(f32[64,192]{1,0:T(8,128)} %route.1.refs_1_.refs_4_), channel_id=1, source_target_pairs={{0,4},{4,0},{8,12},{12,8},{1,5},{5,1},{9,13},{13,9},{2,6},{6,2},{1... | collective-permute-start | bytes 147464 | tf_op jit(solution)/shard_map/ppermute | solution.py:331
  48.5 1.5 copy-start.12
  50.1 13.9 %copy-start = (bf16[8,48,1280]{2,1,0:T(8,128)(2,1)}, bf16[8,48,1280]{2,1,0:T(8,128)(2,1)S(1)}, u32[]{:S(2)}) copy-start(bf16[8,48,1280]{2,1,0:T(8,128)(2,1)S(1)} %place.6.refs_2_) | copy-start | bytes 2949124
  63.9 3.4 %collective-permute-start.8 = (bf16[2,512,768]{2,1,0:T(8,128)(2,1)S(1)}, bf16[2,512,768]{2,1,0:T(8,128)(2,1)S(1)}, u32[]{:S(2)}, u32[]{:S(2)}) collective-permute-start(bf16[2,512,768]{2,1,0:T(8,128)(2,1)S(1)} %get-tuple-element.16), channel_id=1, source_target_pairs={{0,1},{1,0},{2,3},{3,2},{4,5},{5,4},{6,7},{7,6},{8,9},{9,8},{10,11... | collective-permute-start | bytes 4718600 | tf_op jit(solution)/shard_map/ppermute | solution.py:352
  67.3 3.1 %copy-start.6 = (bf16[2,512,768]{2,1,0:T(8,128)(2,1)}, bf16[2,512,768]{2,1,0:T(8,128)(2,1)S(1)}, u32[]{:S(2)}) copy-start(bf16[2,512,768]{2,1,0:T(8,128)(2,1)S(1)} %collective-permute-done.8.near_ref) | copy-start | bytes 4718596
  67.3 2.0 %copy-start.2 = (bf16[2,512,768]{2,1,0:T(8,128)(2,1)S(1)}, bf16[2,512,768]{2,1,0:T(8,128)(2,1)}, u32[]{:S(2)}) copy-start(bf16[2,512,768]{2,1,0:T(8,128)(2,1)} %get-tuple-element.15.keep_ref._) | copy-start | bytes 4718596
  70.4 19.9 %collective-permute-start.10 = (bf16[512,768]{1,0:T(8,128)(2,1)}, bf16[512,768]{1,0:T(8,128)(2,1)}, u32[]{:S(2)}, u32[]{:S(2)}) collective-permute-start(bf16[512,768]{1,0:T(8,128)(2,1)} %chip_sum.2.refs_5_), channel_id=1, source_target_pairs={{0,2},{1,3},{2,0},{3,1},{4,6},{5,7},{6,4},{7,5},{8,10},{9,11},{10,... | collective-permute-start | bytes 2359304 | tf_op jit(solution)/shard_map/ppermute | solution.py:356
  73.2 17.1 %copy-start.3 = (bf16[2,512,768]{2,1,0:T(8,128)(2,1)S(1)}, bf16[2,512,768]{2,1,0:T(8,128)(2,1)}, u32[]{:S(2)}) copy-start(bf16[2,512,768]{2,1,0:T(8,128)(2,1)} %get-tuple-element.15.keep_ref._) | copy-start | bytes 4718596
  73.2 17.1 %copy-start.7 = (bf16[2,512,768]{2,1,0:T(8,128)(2,1)S(1)}, bf16[2,512,768]{2,1,0:T(8,128)(2,1)}, u32[]{:S(2)}) copy-start(bf16[2,512,768]{2,1,0:T(8,128)(2,1)} %copy-done.6) | copy-start | bytes 4718596
  85.9 9.3 %collective-permute-start.9 = (bf16[2,512,768]{2,1,0:T(8,128)(2,1)}, bf16[2,512,768]{2,1,0:T(8,128)(2,1)S(1)}, u32[]{:S(2)}, u32[]{:S(2)}) collective-permute-start(bf16[2,512,768]{2,1,0:T(8,128)(2,1)} %get-tuple-element.18), channel_id=1, source_target_pairs={{0,1},{1,0},{2,3},{3,2},{4,5},{5,4},{6,7},{7,6},{8,9},{9,8},{10,11... | collective-permute-start | bytes 4718600 | tf_op jit(solution)/shard_map/ppermute | solution.py:352
  93.6 13.9 %copy-start.9 = (f32[64,192]{1,0:T(8,128)S(1)}, f32[64,192]{1,0:T(8,128)}, u32[]{:S(2)}) copy-start(f32[64,192]{1,0:T(8,128)} %route.1.refs_1_.refs_4_) | copy-start | bytes 147460
  93.6 12.1 %collective-permute-start.12 = (bf16[768,256]{1,0:T(8,128)(2,1)S(1)}, bf16[768,256]{1,0:T(8,128)(2,1)S(1)}, u32[]{:S(2)}, u32[]{:S(2)}) collective-permute-start(bf16[768,256]{1,0:T(8,128)(2,1)S(1)} %hidden.2._.refs_0_), channel_id=1, source_target_pairs={{0,2},{1,3},{2,0},{3,1},{4,6},{5,7},{6,4},{7,5},{8,10},{9,11},{10,... | collective-permute-start | bytes 1179656 | tf_op jit(solution)/shard_map/ppermute | solution.py:359
  95.3 25.5 %copy-start.5 = (bf16[2,512,768]{2,1,0:T(8,128)(2,1)S(1)}, bf16[2,512,768]{2,1,0:T(8,128)(2,1)}, u32[]{:S(2)}) copy-start(bf16[2,512,768]{2,1,0:T(8,128)(2,1)} %get-tuple-element.17._.keep_ref) | copy-start | bytes 4718596
  95.3 25.5 %collective-permute-start.11 = (bf16[512,768]{1,0:T(8,128)(2,1)S(1)}, bf16[512,768]{1,0:T(8,128)(2,1)S(1)}, u32[]{:S(2)}, u32[]{:S(2)}) collective-permute-start(bf16[512,768]{1,0:T(8,128)(2,1)S(1)} %chip_sum.3.refs_9_), channel_id=1, source_target_pairs={{0,2},{1,3},{2,0},{3,1},{4,6},{5,7},{6,4},{7,5},{8,10},{9,11},{10,... | collective-permute-start | bytes 2359304 | tf_op jit(solution)/shard_map/ppermute | solution.py:356
  95.9 9.8 %collective-permute-start.13 = (bf16[768,256]{1,0:T(8,128)(2,1)S(1)}, bf16[768,256]{1,0:T(8,128)(2,1)S(1)}, u32[]{:S(2)}, u32[]{:S(2)}) collective-permute-start(bf16[768,256]{1,0:T(8,128)(2,1)S(1)} %hidden.2._.refs_0_), channel_id=1, source_target_pairs={{0,1},{1,0},{2,3},{3,2},{4,5},{5,4},{6,7},{7,6},{8,9},{9,8},{10,11... | collective-permute-start | bytes 1179656 | tf_op jit(solution)/shard_map/ppermute | solution.py:360
  105.7 1.7 collective-permute-start.14
  121.5 9.5 %collective-permute-start.15 = (bf16[768,256]{1,0:T(8,128)(2,1)S(1)}, bf16[768,256]{1,0:T(8,128)(2,1)S(1)}, u32[]{:S(2)}, u32[]{:S(2)}) collective-permute-start(bf16[768,256]{1,0:T(8,128)(2,1)S(1)} %hidden.3.refs_0_.refs_9_), channel_id=1, source_target_pairs={{0,2},{1,3},{2,0},{3,1},{4,6},{5,7},{6,4},{7,5},{8,10},{9,11},{10,... | collective-permute-start | bytes 1179656 | tf_op jit(solution)/shard_map/ppermute | solution.py:359
  123.1 7.9 %collective-permute-start.16 = (bf16[768,256]{1,0:T(8,128)(2,1)S(1)}, bf16[768,256]{1,0:T(8,128)(2,1)S(1)}, u32[]{:S(2)}, u32[]{:S(2)}) collective-permute-start(bf16[768,256]{1,0:T(8,128)(2,1)S(1)} %hidden.3.refs_0_.refs_9_), channel_id=1, source_target_pairs={{0,1},{1,0},{2,3},{3,2},{4,5},{5,4},{6,7},{7,6},{8,9},{9,8},{10,11... | collective-permute-start | bytes 1179656 | tf_op jit(solution)/shard_map/ppermute | solution.py:360
  131.0 1.7 collective-permute-start.17
  139.1 12.3 %collective-permute-start.18 = (bf16[192,1280]{1,0:T(8,128)(2,1)S(1)}, bf16[192,1280]{1,0:T(8,128)(2,1)S(1)}, u32[]{:S(2)}, u32[]{:S(2)}) collective-permute-start(bf16[192,1280]{1,0:T(8,128)(2,1)S(1)} %get-tuple-element.20.a_ref), channel_id=1, source_target_pairs={{0,4},{12,8},{1,5},{13,9},{2,6},{14,10},{3,7},{15,11},{16,20},{28,... | collective-permute-start | bytes 1474568 | tf_op jit(solution)/shard_map/ppermute | solution.py:331
  151.5 7.3 %collective-permute-start.21 = (bf16[192,1280]{1,0:T(8,128)(2,1)S(1)}, bf16[192,1280]{1,0:T(8,128)(2,1)S(1)}, u32[]{:S(2)}, u32[]{:S(2)}) collective-permute-start(bf16[192,1280]{1,0:T(8,128)(2,1)S(1)} %get-tuple-element.24), channel_id=1, source_target_pairs={{4,8},{8,4},{5,9},{9,5},{6,10},{10,6},{7,11},{11,7},{20,24},{24,20... | collective-permute-start | bytes 1474568 | tf_op jit(solution)/shard_map/ppermute | solution.py:331
  152.2 17.7 %collective-permute-start.19 = (bf16[192,1280]{1,0:T(8,128)(2,1)S(1)}, bf16[192,1280]{1,0:T(8,128)(2,1)S(1)}, u32[]{:S(2)}, u32[]{:S(2)}) collective-permute-start(bf16[192,1280]{1,0:T(8,128)(2,1)S(1)} %get-tuple-element.22), channel_id=1, source_target_pairs={{0,4},{12,8},{1,5},{13,9},{2,6},{14,10},{3,7},{15,11},{16,20},{28,... | collective-permute-start | bytes 1474568 | tf_op jit(solution)/shard_map/ppermute | solution.py:331
  159.0 20.1 %collective-permute-start.22 = (bf16[192,1280]{1,0:T(8,128)(2,1)S(1)}, bf16[192,1280]{1,0:T(8,128)(2,1)S(1)}, u32[]{:S(2)}, u32[]{:S(2)}) collective-permute-start(bf16[192,1280]{1,0:T(8,128)(2,1)S(1)} %add_convert_fusion.1), channel_id=1, source_target_pairs={{0,4},{4,0},{8,12},{12,8},{1,5},{5,1},{9,13},{13,9},{2,6},{6,2},{1... | collective-permute-start | bytes 1474568 | tf_op jit(solution)/shard_map/ppermute | solution.py:331
  170.1 9.0 %collective-permute-start.20 = (bf16[192,1280]{1,0:T(8,128)(2,1)S(1)}, bf16[192,1280]{1,0:T(8,128)(2,1)S(1)}, u32[]{:S(2)}, u32[]{:S(2)}) collective-permute-start(bf16[192,1280]{1,0:T(8,128)(2,1)S(1)} %add_convert_fusion.2), channel_id=1, source_target_pairs={{4,8},{8,4},{5,9},{9,5},{6,10},{10,6},{7,11},{11,7},{20,24},{24,20... | collective-permute-start | bytes 1474568 | tf_op jit(solution)/shard_map/ppermute | solution.py:331
  (6 other events, 6.3 us)
where the time goes:
time: 183 us; the launch traced here: 180 us
  waiting for transfers between devices  73.4 us (40%)
  Pallas kernels  47.9 us (26%)
  starting transfers between devices  47.4 us (26%)
  local copies, waits for them, and re-layouts  8.31 us (5%)
  other arithmetic  2.63 us (1%)
    ppermute x13, starting transfers between devices, hop(): return lax.ppermute(array, 'ep', pairs)  42.2 us
    ppermute x13, waiting for transfers between devices, hop(): return lax.ppermute(array, 'ep', pairs)  37.4 us
    pallas_call x2, Pallas kernels, gate_up(): pl.pallas_call(functools.partial(gate_up_kernel, n_blocks), grid=(group,)...  24.7 us
    ppermute x2, waiting for transfers between devices, gathered(): own_x = lax.ppermute(own, 'tp', ACROSS_X)  17.7 us
    pallas_call x2, Pallas kernels, down(): pl.pallas_call(functools.partial(down_kernel, group, n_blocks, chunk, car...  12.6 us
    ppermute x2, waiting for transfers between devices, across(): return (total, lax.ppermute(total, 'tp', ACROSS_X))  11.5 us
    unnamed x30, local copies, waits for them, and re-layouts  8.31 us
    pallas_call x4, Pallas kernels, place(): pl.pallas_call(functools.partial(place_kernel, experts), out_shape=jax.Sh...  5.18 us
  transfers between devices with their start and end apart: 23, of which 13 were waited for; matrix products, arithmetic and copies ran while one was open for 1% of the time, Pallas kernels for 14%

commit v1 on v0

--- a/solution.py
+++ b/solution.py
@@ -83,7 +83,7 @@
         out_shape=jax.ShapeDtypeStruct((experts, CAP, tokens[0].shape[1]), BF16),
         in_specs=[pl.BlockSpec(memory_space=pltpu.SMEM)] + [whole] * (len(tokens) + 1),
         out_specs=whole,
-        compiler_params=params(24),
+        compiler_params=params(8),
         cost_estimate=QUICK,
         name="place",
     )(where, *tokens, table)
@@ -155,7 +155,7 @@
             pltpu.VMEM((2, 2 * LANES, width), BF16),
             pltpu.VMEM((2 * units, LANES), F32),
         ],
-        compiler_params=params(48),
+        compiler_params=params(28),
         cost_estimate=QUICK,
         name="gate_up",
     )(where, *placed, gu_weight, after)
@@ -187,7 +187,7 @@
         ],
         out_specs=pl.BlockSpec((columns, doubled // 2), lambda i: (0, 0)),
         scratch_shapes=[pltpu.VMEM((columns // LANES, doubled, LANES), F32)],
-        compiler_params=params(24),
+        compiler_params=params(10),
         cost_estimate=SLOW,
         name="hidden",
     )(keep, near, far, after)
@@ -206,7 +206,7 @@
         out_shape=jax.ShapeDtypeStruct((doubled, columns), BF16),
         in_specs=[other, other, pl.BlockSpec(memory_space=pl.ANY)],
         out_specs=pl.BlockSpec((doubled, columns), lambda i: (0, 0)),
-        compiler_params=params(24),
+        compiler_params=params(8),
         cost_estimate=QUICK,
         name="chip_sum",
     )(keep, near, after)
@@ -295,10 +295,28 @@
             pltpu.VMEM((group, 4 * units, width), BF16),
             pltpu.SemaphoreType.DMA((group, 4)),
         ],
-        compiler_params=params(40),
+        compiler_params=params(28),
         cost_estimate=QUICK,
         name="down",
     )(where, *hidden, *routes, down_weight, after, *carried)
+
+
+def hold_kernel(*_):
+    pass
+
+
+def hold(arrays, until):
+    free = pl.BlockSpec(memory_space=pl.ANY)
+    return pl.pallas_call(
+        hold_kernel,
+        out_shape=tuple(jax.ShapeDtypeStruct(a.shape, a.dtype) for a in arrays),
+        in_specs=[free] * (len(arrays) + len(until)),
+        out_specs=(free,) * len(arrays),
+        input_output_aliases={i: i for i in range(len(arrays))},
+        compiler_params=params(1),
+        cost_estimate=QUICK,
+        name="hold",
+    )(*arrays, *until)
 
 
 def plus_kernel(a_ref, b_ref, _, out_ref, __):
@@ -314,7 +332,7 @@
         in_specs=[whole, whole, free],
         out_specs=(whole, free),
         input_output_aliases={2: 1},
-        compiler_params=params(16),
+        compiler_params=params(4),
         cost_estimate=QUICK,
         name="plus",
     )(a, b, other)
@@ -330,12 +348,13 @@
     def hop(array, pairs):
         return lax.ppermute(array, "ep", pairs)
 
+    neighbour = hop(tokens, PAIR)
+    middle_1 = hop(tokens, MIDDLE)
     table = route(expert_ids, gate_weights)
-    neighbour = hop(tokens, PAIR)
     table_1 = hop(table, PAIR)
-    middle_1 = hop(tokens, MIDDLE)
     table_2 = hop(table, [(i, i ^ 2) for i in range(4)])
     table_3 = hop(table, [(i, i ^ 3) for i in range(4)])
+    neighbour, middle_1 = hold((neighbour, middle_1), (table_1, table_2, table_3))
     inner = (z == 1) | (z == 2)
     table_in = jnp.where(inner, table_3, table_2)
     table_out = jnp.where(inner, table_2, table_3)

time: 183 us -> 178 us (0.973)
  waiting for transfers between devices: 73.4 us -> 84.5 us
  starting transfers between devices: 47.4 us -> 39.6 us
  local copies, waits for them, and re-layouts: 8.31 us -> 2.29 us
  Pallas kernels: 47.9 us -> 45.4 us
    ppermute x13, waiting for transfers between devices: 37.4 us -> 47.1 us  [hop(): return lax.ppermute(array, 'ep', pairs)]
    ppermute x13, starting transfers between devices: 42.2 us -> 34.2 us  [hop(): return lax.ppermute(array, 'ep', pairs)]
    unnamed x30 -> x18, local copies, waits for them, and re-layouts: 8.31 us -> 2.29 us
    pallas_call x2, Pallas kernels: 24.7 us -> 22.3 us  [gate_up(): pl.pallas_call(functools.partial(gate_up_kernel, n_blocks), grid=(group,)...]
  transfers between devices with their start and end apart: 23 -> 23, of which waited for: 13 -> 14; matrix products, arithmetic and copies ran while one was open for 1% -> 1% of each run, Pallas kernels for 14% -> 14%
where the time goes in v1:
time: 178 us; the launch traced here: 175 us
  waiting for transfers between devices  84.5 us (47%)
  Pallas kernels  45.4 us (26%)
  starting transfers between devices  39.6 us (22%)
  other arithmetic  2.63 us (1%)
  local copies, waits for them, and re-layouts  2.29 us (1%)
    ppermute x13, waiting for transfers between devices, hop(): return lax.ppermute(array, 'ep', pairs)  47.1 us
    ppermute x13, starting transfers between devices, hop(): return lax.ppermute(array, 'ep', pairs)  34.2 us
    pallas_call x2, Pallas kernels, gate_up(): pl.pallas_call(functools.partial(gate_up_kernel, n_blocks), grid=(group,)...  22.3 us
    ppermute x2, waiting for transfers between devices, gathered(): own_x = lax.ppermute(own, 'tp', ACROSS_X)  17.7 us
    ppermute x2, waiting for transfers between devices, across(): return (total, lax.ppermute(total, 'tp', ACROSS_X))  12.8 us
    pallas_call x2, Pallas kernels, down(): pl.pallas_call(functools.partial(down_kernel, group, n_blocks, chunk, car...  12.6 us
    pallas_call x4, Pallas kernels, place(): pl.pallas_call(functools.partial(place_kernel, experts), out_shape=jax.Sh...  4.94 us
  transfers between devices with their start and end apart: 23, of which 14 were waited for; matrix products, arithmetic and copies ran while one was open for 1% of the time, Pallas kernels for 14%

profile of v1, /device:TPU:0, one launch (start us, length us, event | category | flops | bytes accessed | tf_op | source)
XLA Modules:
  0.0 174.7 jit_solution(2883220048986862470)
XLA Ops:
  0.8 5.9 %collective-permute-start = (bf16[192,1280]{1,0:T(8,128)(2,1)}, bf16[192,1280]{1,0:T(8,128)(2,1)S(1)}, u32[]{:S(2)}, u32[]{:S(2)}) collective-permute-start(bf16[192,1280]{1,0:T(8,128)(2,1)} %refs_0_.1), channel_id=1, source_target_pairs={{0,4},{4,0},{8,12},{12,8},{1,5},{5,1},{9,13},{13,9},{2,6},{6,2},{1... | collective-permute-start | bytes 1474568 | tf_op jit(solution)/shard_map/ppermute | solution.py:349
  8.0 1.5 route.1.refs_1_.refs_4_
  9.5 1.3 collective-permute-start.4
  10.9 2.9 %collective-permute-start.2 = (f32[64,192]{1,0:T(8,128)}, f32[64,192]{1,0:T(8,128)S(1)}, u32[]{:S(2)}, u32[]{:S(2)}) collective-permute-start(f32[64,192]{1,0:T(8,128)} %route.1.refs_1_.refs_4_), channel_id=1, source_target_pairs={{0,4},{4,0},{8,12},{12,8},{1,5},{5,1},{9,13},{13,9},{2,6},{6,2},{1... | collective-permute-start | bytes 147464 | tf_op jit(solution)/shard_map/ppermute | solution.py:349
  13.9 8.0 %collective-permute-done.4.__4_ = f32[64,192]{1,0:T(8,128)S(1)} collective-permute-done((f32[64,192]{1,0:T(8,128)}, f32[64,192]{1,0:T(8,128)S(1)}, u32[]{:S(2)}, u32[]{:S(2)}) %collective-permute-start.4) | collective-permute-done | bytes 49184 | tf_op jit(solution)/shard_map/ppermute | solution.py:349
  21.8 1.4 collective-permute-done.3.__3_
  23.3 1.4 collective-permute-start.6
  30.2 7.5 %collective-permute-done.5.refs_1_ = bf16[192,1280]{1,0:T(8,128)(2,1)} collective-permute-done((bf16[192,1280]{1,0:T(8,128)(2,1)S(1)}, bf16[192,1280]{1,0:T(8,128)(2,1)}, u32[]{:S(2)}, u32[]{:S(2)}) %collective-permute-start.5) | collective-permute-done | bytes 491552 | tf_op jit(solution)/shard_map/ppermute | solution.py:349
  37.7 1.4 place.6.refs_2_
  39.2 9.1 %collective-permute-done.7.refs_1_ = bf16[192,1280]{1,0:T(8,128)(2,1)} collective-permute-done((bf16[192,1280]{1,0:T(8,128)(2,1)}, bf16[192,1280]{1,0:T(8,128)(2,1)}, u32[]{:S(2)}, u32[]{:S(2)}) %collective-permute-start.7) | collective-permute-done | bytes 491552 | tf_op jit(solution)/shard_map/ppermute | solution.py:349
  48.3 1.6 place.7.refs_3_.refs_5_
  49.9 11.0 %gate_up.2 = (bf16[2,512,768]{2,1,0:T(8,128)(2,1)S(1)}, bf16[2,512,768]{2,1,0:T(8,128)(2,1)S(1)}) custom-call(s32[3]{0:T(128)S(1)} %add_add_fusion.1.where_ref, bf16[8,48,1280]{2,1,0:T(8,128)(2,1)S(1)} %place.4.refs_0_, bf16[8,48,1280]{2,1,0:T(8,128)(2,1)S(1)} %place.5.refs_1_, bf16[8,48,1280]{2,1,0:T(8,128)(2,1)S(1)} %place.6.refs_2_, ...), custom_call_target="tpu_custom_call" | custom-call | flops 1024 | bytes 1024 | tf_op jit(solution)/shard_map/gate_up/pallas_call | solution.py:145
  61.0 3.4 %collective-permute-done.8.near_ref = bf16[2,512,768]{2,1,0:T(8,128)(2,1)S(1)} collective-permute-done((bf16[2,512,768]{2,1,0:T(8,128)(2,1)S(1)}, bf16[2,512,768]{2,1,0:T(8,128)(2,1)S(1)}, u32[]{:S(2)}, u32[]{:S(2)}) %collective-permute-start.8) | collective-permute-done | bytes 1572896 | tf_op jit(solution)/shard_map/ppermute | solution.py:371
  65.9 1.5 collective-permute-start.10
  68.6 11.3 %gate_up.3 = (bf16[2,512,768]{2,1,0:T(8,128)(2,1)S(1)}, bf16[2,512,768]{2,1,0:T(8,128)(2,1)S(1)}) custom-call(s32[3]{0:T(128)S(1)} %add_add_fusion.where_ref, bf16[8,48,1280]{2,1,0:T(8,128)(2,1)S(1)} %place.4.refs_0_, bf16[8,48,1280]{2,1,0:T(8,128)(2,1)S(1)} %place.5.refs_1_, bf16[8,48,1280]{2,1,0:T(8,128)(2,1)S(1)} %copy-done.1, ...), custom_call_target="tpu_custom_call" | custom-call | flops 1024 | bytes 1024 | tf_op jit(solution)/shard_map/gate_up/pallas_call | solution.py:145
  80.0 5.8 %collective-permute-done.10.far_ref = bf16[512,768]{1,0:T(8,128)(2,1)} collective-permute-done((bf16[512,768]{1,0:T(8,128)(2,1)}, bf16[512,768]{1,0:T(8,128)(2,1)}, u32[]{:S(2)}, u32[]{:S(2)}) %collective-permute-start.10) | collective-permute-done | bytes 786464 | tf_op jit(solution)/shard_map/ppermute | solution.py:375
  85.8 1.8 %hidden.2._.refs_0_ = bf16[768,256]{1,0:T(8,128)(2,1)S(1)} custom-call(bf16[2,512,768]{2,1,0:T(8,128)(2,1)S(1)} %copy-done.3, bf16[2,512,768]{2,1,0:T(8,128)(2,1)S(1)} %copy-done.5, bf16[512,768]{1,0:T(8,128)(2,1)} %collective-permute-done.10.far_ref, bf16[2,512,768]{2,1,0:T(8,128)(2,1)S(1)} %get-tuple-element.21._.keep_ref), custom_call_target="tpu_custom_call" | custom-call | flops 20000000000 | bytes 1024 | tf_op jit(solution)/shard_map/hidden/pallas_call | solution.py:178
  87.6 1.6 collective-permute-start.12
  90.0 9.8 %collective-permute-done.12.refs_1_ = bf16[768,256]{1,0:T(8,128)(2,1)S(1)} collective-permute-done((bf16[768,256]{1,0:T(8,128)(2,1)S(1)}, bf16[768,256]{1,0:T(8,128)(2,1)S(1)}, u32[]{:S(2)}, u32[]{:S(2)}) %collective-permute-start.12) | collective-permute-done | bytes 393248 | tf_op jit(solution)/shard_map/ppermute | solution.py:378
  99.7 1.7 collective-permute-done.14.refs_3_
  101.4 6.3 %down.2._.refs_10_ = f32[4,192,1280]{2,1,0:T(8,128)S(1)} custom-call(s32[3]{0:T(128)S(1)} %add_add_fusion.1.where_ref, bf16[768,256]{1,0:T(8,128)(2,1)S(1)} %hidden.2._.refs_0_, bf16[768,256]{1,0:T(8,128)(2,1)S(1)} %collective-permute-done.12.refs_1_, bf16[768,256]{1,0:T(8,128)(2,1)S(1)} %collective-permute-done.13.refs_2_, ...), custom_call_target="tpu_custom_call" | custom-call | flops 1024 | bytes 1024 | tf_op jit(solution)/shard_map/down/pallas_call | solution.py:285
  107.8 7.1 %collective-permute-done.11.far_ref = bf16[512,768]{1,0:T(8,128)(2,1)S(1)} collective-permute-done((bf16[512,768]{1,0:T(8,128)(2,1)S(1)}, bf16[512,768]{1,0:T(8,128)(2,1)S(1)}, u32[]{:S(2)}, u32[]{:S(2)}) %collective-permute-start.11) | collective-permute-done | bytes 786464 | tf_op jit(solution)/shard_map/ppermute | solution.py:375
  115.6 1.6 collective-permute-start.15
  117.1 7.9 %collective-permute-done.15.refs_1_ = bf16[768,256]{1,0:T(8,128)(2,1)S(1)} collective-permute-done((bf16[768,256]{1,0:T(8,128)(2,1)S(1)}, bf16[768,256]{1,0:T(8,128)(2,1)S(1)}, u32[]{:S(2)}, u32[]{:S(2)}) %collective-permute-start.15) | collective-permute-done | bytes 393248 | tf_op jit(solution)/shard_map/ppermute | solution.py:378
  125.0 1.7 collective-permute-done.17.refs_3_
  126.7 6.3 %down.3 = (bf16[192,1280]{1,0:T(8,128)(2,1)S(1)}, bf16[192,1280]{1,0:T(8,128)(2,1)S(1)}, bf16[192,1280]{1,0:T(8,128)(2,1)S(1)}, bf16[192,1280]{1,0:T(8,128)(2,1)S(1)}) custom-call(s32[3]{0:T(128)S(1)} %add_add_fusion.where_ref, bf16[768,256]{1,0:T(8,128)(2,1)S(1)} %hidden.3.refs_0_.refs_9_, bf16[768,256]{1,0:T(8,128)(2,1)S(1)} %collective-permute-done.15.refs_1_, ...), custom_call_target="tpu_custom_call" | custom-call | flops 1024 | bytes 1024 | tf_op jit(solution)/shard_map/down/pallas_call | solution.py:285
  133.1 1.5 collective-permute-start.18
  134.6 10.9 %collective-permute-done.18.b_ref = bf16[192,1280]{1,0:T(8,128)(2,1)S(1)} collective-permute-done((bf16[192,1280]{1,0:T(8,128)(2,1)S(1)}, bf16[192,1280]{1,0:T(8,128)(2,1)S(1)}, u32[]{:S(2)}, u32[]{:S(2)}) %collective-permute-start.18) | collective-permute-done | bytes 491552 | tf_op jit(solution)/shard_map/ppermute | solution.py:349
  146.2 7.2 %collective-permute-start.19 = (bf16[192,1280]{1,0:T(8,128)(2,1)S(1)}, bf16[192,1280]{1,0:T(8,128)(2,1)S(1)}, u32[]{:S(2)}, u32[]{:S(2)}) collective-permute-start(bf16[192,1280]{1,0:T(8,128)(2,1)S(1)} %get-tuple-element.26), channel_id=1, source_target_pairs={{0,4},{12,8},{1,5},{13,9},{2,6},{14,10},{3,7},{15,11},{16,20},{28,... | collective-permute-start | bytes 1474568 | tf_op jit(solution)/shard_map/ppermute | solution.py:349
  153.6 9.1 %collective-permute-start.22 = (bf16[192,1280]{1,0:T(8,128)(2,1)S(1)}, bf16[192,1280]{1,0:T(8,128)(2,1)S(1)}, u32[]{:S(2)}, u32[]{:S(2)}) collective-permute-start(bf16[192,1280]{1,0:T(8,128)(2,1)S(1)} %add_convert_fusion.1), channel_id=1, source_target_pairs={{0,4},{4,0},{8,12},{12,8},{1,5},{5,1},{9,13},{13,9},{2,6},{6,2},{1... | collective-permute-start | bytes 1474568 | tf_op jit(solution)/shard_map/ppermute | solution.py:349
  162.7 2.4 %collective-permute-done.19 = bf16[192,1280]{1,0:T(8,128)(2,1)S(1)} collective-permute-done((bf16[192,1280]{1,0:T(8,128)(2,1)S(1)}, bf16[192,1280]{1,0:T(8,128)(2,1)S(1)}, u32[]{:S(2)}, u32[]{:S(2)}) %collective-permute-start.19) | collective-permute-done | bytes 491552 | tf_op jit(solution)/shard_map/ppermute | solution.py:349
  165.9 7.9 %collective-permute-done.22 = bf16[192,1280]{1,0:T(8,128)(2,1)S(1)} collective-permute-done((bf16[192,1280]{1,0:T(8,128)(2,1)S(1)}, bf16[192,1280]{1,0:T(8,128)(2,1)S(1)}, u32[]{:S(2)}, u32[]{:S(2)}) %collective-permute-start.22) | collective-permute-done | bytes 491552 | tf_op jit(solution)/shard_map/ppermute | solution.py:349
  (54 shorter events, 14.8 us)
Async XLA Ops:
  0.0 27.4 %copy-start.8 = (bf16[192,1280]{1,0:T(8,128)(2,1)S(1)}, bf16[192,1280]{1,0:T(8,128)(2,1)}, u32[]{:S(2)}) copy-start(bf16[192,1280]{1,0:T(8,128)(2,1)} %refs_0_.1) | copy-start | bytes 1474564
  0.0 23.3 %collective-permute-start.1 = (bf16[192,1280]{1,0:T(8,128)(2,1)}, bf16[192,1280]{1,0:T(8,128)(2,1)S(1)}, u32[]{:S(2)}, u32[]{:S(2)}) collective-permute-start(bf16[192,1280]{1,0:T(8,128)(2,1)} %refs_0_.1), channel_id=1, source_target_pairs={{4,8},{8,4},{5,9},{9,5},{6,10},{10,6},{7,11},{11,7},{20,24},{24,20... | collective-permute-start | bytes 1474568 | tf_op jit(solution)/shard_map/ppermute | solution.py:349
  0.8 22.5 %collective-permute-start = (bf16[192,1280]{1,0:T(8,128)(2,1)}, bf16[192,1280]{1,0:T(8,128)(2,1)S(1)}, u32[]{:S(2)}, u32[]{:S(2)}) collective-permute-start(bf16[192,1280]{1,0:T(8,128)(2,1)} %refs_0_.1), channel_id=1, source_target_pairs={{0,4},{4,0},{8,12},{12,8},{1,5},{5,1},{9,13},{13,9},{2,6},{6,2},{1... | collective-permute-start | bytes 1474568 | tf_op jit(solution)/shard_map/ppermute | solution.py:349
  9.5 12.4 %collective-permute-start.4 = (f32[64,192]{1,0:T(8,128)}, f32[64,192]{1,0:T(8,128)S(1)}, u32[]{:S(2)}, u32[]{:S(2)}) collective-permute-start(f32[64,192]{1,0:T(8,128)} %route.1.refs_1_.refs_4_), channel_id=1, source_target_pairs={{0,12},{4,8},{8,4},{12,0},{1,13},{5,9},{9,5},{13,1},{2,14},{6,10},... | collective-permute-start | bytes 147464 | tf_op jit(solution)/shard_map/ppermute | solution.py:349
  10.8 12.4 %collective-permute-start.3 = (f32[64,192]{1,0:T(8,128)}, f32[64,192]{1,0:T(8,128)S(1)}, u32[]{:S(2)}, u32[]{:S(2)}) collective-permute-start(f32[64,192]{1,0:T(8,128)} %route.1.refs_1_.refs_4_), channel_id=1, source_target_pairs={{0,8},{4,12},{8,0},{12,4},{1,9},{5,13},{9,1},{13,5},{2,10},{6,14},... | collective-permute-start | bytes 147464 | tf_op jit(solution)/shard_map/ppermute | solution.py:349
  10.9 12.3 %collective-permute-start.2 = (f32[64,192]{1,0:T(8,128)}, f32[64,192]{1,0:T(8,128)S(1)}, u32[]{:S(2)}, u32[]{:S(2)}) collective-permute-start(f32[64,192]{1,0:T(8,128)} %route.1.refs_1_.refs_4_), channel_id=1, source_target_pairs={{0,4},{4,0},{8,12},{12,8},{1,5},{5,1},{9,13},{13,9},{2,6},{6,2},{1... | collective-permute-start | bytes 147464 | tf_op jit(solution)/shard_map/ppermute | solution.py:349
  23.3 2.7 %collective-permute-start.6 = (bf16[192,1280]{1,0:T(8,128)(2,1)S(1)}, bf16[192,1280]{1,0:T(8,128)(2,1)}, u32[]{:S(2)}, u32[]{:S(2)}) collective-permute-start(bf16[192,1280]{1,0:T(8,128)(2,1)S(1)} %get-tuple-element.17.refs_0_), channel_id=1, source_target_pairs={{4,8},{8,4},{5,9},{9,5},{6,10},{10,6},{7,11},{11,7},{20,24},{24,20... | collective-permute-start | bytes 1474568 | tf_op jit(solution)/shard_map/ppermute | solution.py:349
  24.7 13.0 %collective-permute-start.5 = (bf16[192,1280]{1,0:T(8,128)(2,1)S(1)}, bf16[192,1280]{1,0:T(8,128)(2,1)}, u32[]{:S(2)}, u32[]{:S(2)}) collective-permute-start(bf16[192,1280]{1,0:T(8,128)(2,1)S(1)} %get-tuple-element.18.refs_0_), channel_id=1, source_target_pairs={{4,0},{8,12},{5,1},{9,13},{6,2},{10,14},{7,3},{11,15},{20,16},{24,... | collective-permute-start | bytes 1474568 | tf_op jit(solution)/shard_map/ppermute | solution.py:349
  26.0 22.2 %collective-permute-start.7 = (bf16[192,1280]{1,0:T(8,128)(2,1)}, bf16[192,1280]{1,0:T(8,128)(2,1)}, u32[]{:S(2)}, u32[]{:S(2)}) collective-permute-start(bf16[192,1280]{1,0:T(8,128)(2,1)} %collective-permute-done.6.refs_0_), channel_id=1, source_target_pairs={{4,0},{8,12},{5,1},{9,13},{6,2},{10,14},{7,3},{11,15},{20,16},{24,... | collective-permute-start | bytes 1474568 | tf_op jit(solution)/shard_map/ppermute | solution.py:349
  27.4 0.8 copy-start.6
  39.2 21.7 %copy-start = (bf16[8,48,1280]{2,1,0:T(8,128)(2,1)}, bf16[8,48,1280]{2,1,0:T(8,128)(2,1)S(1)}, u32[]{:S(2)}) copy-start(bf16[8,48,1280]{2,1,0:T(8,128)(2,1)S(1)} %place.6.refs_2_) | copy-start | bytes 2949124
  60.9 4.8 %copy-start.2 = (bf16[2,512,768]{2,1,0:T(8,128)(2,1)}, bf16[2,512,768]{2,1,0:T(8,128)(2,1)S(1)}, u32[]{:S(2)}) copy-start(bf16[2,512,768]{2,1,0:T(8,128)(2,1)S(1)} %get-tuple-element.19.keep_ref._) | copy-start | bytes 4718596
  60.9 3.5 %collective-permute-start.8 = (bf16[2,512,768]{2,1,0:T(8,128)(2,1)S(1)}, bf16[2,512,768]{2,1,0:T(8,128)(2,1)S(1)}, u32[]{:S(2)}, u32[]{:S(2)}) collective-permute-start(bf16[2,512,768]{2,1,0:T(8,128)(2,1)S(1)} %get-tuple-element.20), channel_id=1, source_target_pairs={{0,1},{1,0},{2,3},{3,2},{4,5},{5,4},{6,7},{7,6},{8,9},{9,8},{10,11... | collective-permute-start | bytes 4718600 | tf_op jit(solution)/shard_map/ppermute | solution.py:371
  64.4 1.5 copy-start.4
  65.9 19.9 %collective-permute-start.10 = (bf16[512,768]{1,0:T(8,128)(2,1)}, bf16[512,768]{1,0:T(8,128)(2,1)}, u32[]{:S(2)}, u32[]{:S(2)}) collective-permute-start(bf16[512,768]{1,0:T(8,128)(2,1)} %chip_sum.2.refs_5_), channel_id=1, source_target_pairs={{0,2},{1,3},{2,0},{3,1},{4,6},{5,7},{6,4},{7,5},{8,10},{9,11},{10,... | collective-permute-start | bytes 2359304 | tf_op jit(solution)/shard_map/ppermute | solution.py:375
  67.4 1.2 copy-start.1
  68.6 17.1 %copy-start.3 = (bf16[2,512,768]{2,1,0:T(8,128)(2,1)S(1)}, bf16[2,512,768]{2,1,0:T(8,128)(2,1)}, u32[]{:S(2)}) copy-start(bf16[2,512,768]{2,1,0:T(8,128)(2,1)} %copy-done.2) | copy-start | bytes 4718596
  68.6 17.1 %copy-start.5 = (bf16[2,512,768]{2,1,0:T(8,128)(2,1)S(1)}, bf16[2,512,768]{2,1,0:T(8,128)(2,1)}, u32[]{:S(2)}) copy-start(bf16[2,512,768]{2,1,0:T(8,128)(2,1)} %copy-done.4) | copy-start | bytes 4718596
  79.9 9.2 %collective-permute-start.9 = (bf16[2,512,768]{2,1,0:T(8,128)(2,1)S(1)}, bf16[2,512,768]{2,1,0:T(8,128)(2,1)S(1)}, u32[]{:S(2)}, u32[]{:S(2)}) collective-permute-start(bf16[2,512,768]{2,1,0:T(8,128)(2,1)S(1)} %get-tuple-element.22), channel_id=1, source_target_pairs={{0,1},{1,0},{2,3},{3,2},{4,5},{5,4},{6,7},{7,6},{8,9},{9,8},{10,11... | collective-permute-start | bytes 4718600 | tf_op jit(solution)/shard_map/ppermute | solution.py:371
  87.6 13.9 %copy-start.7 = (f32[64,192]{1,0:T(8,128)S(1)}, f32[64,192]{1,0:T(8,128)}, u32[]{:S(2)}) copy-start(f32[64,192]{1,0:T(8,128)} %route.1.refs_1_.refs_4_) | copy-start | bytes 147460
  87.6 12.1 %collective-permute-start.12 = (bf16[768,256]{1,0:T(8,128)(2,1)S(1)}, bf16[768,256]{1,0:T(8,128)(2,1)S(1)}, u32[]{:S(2)}, u32[]{:S(2)}) collective-permute-start(bf16[768,256]{1,0:T(8,128)(2,1)S(1)} %hidden.2._.refs_0_), channel_id=1, source_target_pairs={{0,2},{1,3},{2,0},{3,1},{4,6},{5,7},{6,4},{7,5},{8,10},{9,11},{10,... | collective-permute-start | bytes 1179656 | tf_op jit(solution)/shard_map/ppermute | solution.py:378
  89.3 25.5 %collective-permute-start.11 = (bf16[512,768]{1,0:T(8,128)(2,1)S(1)}, bf16[512,768]{1,0:T(8,128)(2,1)S(1)}, u32[]{:S(2)}, u32[]{:S(2)}) collective-permute-start(bf16[512,768]{1,0:T(8,128)(2,1)S(1)} %chip_sum.3.refs_9_), channel_id=1, source_target_pairs={{0,2},{1,3},{2,0},{3,1},{4,6},{5,7},{6,4},{7,5},{8,10},{9,11},{10,... | collective-permute-start | bytes 2359304 | tf_op jit(solution)/shard_map/ppermute | solution.py:375
  89.9 9.8 %collective-permute-start.13 = (bf16[768,256]{1,0:T(8,128)(2,1)S(1)}, bf16[768,256]{1,0:T(8,128)(2,1)S(1)}, u32[]{:S(2)}, u32[]{:S(2)}) collective-permute-start(bf16[768,256]{1,0:T(8,128)(2,1)S(1)} %hidden.2._.refs_0_), channel_id=1, source_target_pairs={{0,1},{1,0},{2,3},{3,2},{4,5},{5,4},{6,7},{7,6},{8,9},{9,8},{10,11... | collective-permute-start | bytes 1179656 | tf_op jit(solution)/shard_map/ppermute | solution.py:379
  99.7 1.7 collective-permute-start.14
  115.6 9.5 %collective-permute-start.15 = (bf16[768,256]{1,0:T(8,128)(2,1)S(1)}, bf16[768,256]{1,0:T(8,128)(2,1)S(1)}, u32[]{:S(2)}, u32[]{:S(2)}) collective-permute-start(bf16[768,256]{1,0:T(8,128)(2,1)S(1)} %hidden.3.refs_0_.refs_9_), channel_id=1, source_target_pairs={{0,2},{1,3},{2,0},{3,1},{4,6},{5,7},{6,4},{7,5},{8,10},{9,11},{10,... | collective-permute-start | bytes 1179656 | tf_op jit(solution)/shard_map/ppermute | solution.py:378
  117.1 7.9 %collective-permute-start.16 = (bf16[768,256]{1,0:T(8,128)(2,1)S(1)}, bf16[768,256]{1,0:T(8,128)(2,1)S(1)}, u32[]{:S(2)}, u32[]{:S(2)}) collective-permute-start(bf16[768,256]{1,0:T(8,128)(2,1)S(1)} %hidden.3.refs_0_.refs_9_), channel_id=1, source_target_pairs={{0,1},{1,0},{2,3},{3,2},{4,5},{5,4},{6,7},{7,6},{8,9},{9,8},{10,11... | collective-permute-start | bytes 1179656 | tf_op jit(solution)/shard_map/ppermute | solution.py:379
  125.0 1.7 collective-permute-start.17
  133.1 12.3 %collective-permute-start.18 = (bf16[192,1280]{1,0:T(8,128)(2,1)S(1)}, bf16[192,1280]{1,0:T(8,128)(2,1)S(1)}, u32[]{:S(2)}, u32[]{:S(2)}) collective-permute-start(bf16[192,1280]{1,0:T(8,128)(2,1)S(1)} %get-tuple-element.24.a_ref), channel_id=1, source_target_pairs={{0,4},{12,8},{1,5},{13,9},{2,6},{14,10},{3,7},{15,11},{16,20},{28,... | collective-permute-start | bytes 1474568 | tf_op jit(solution)/shard_map/ppermute | solution.py:349
  145.5 7.9 %collective-permute-start.21 = (bf16[192,1280]{1,0:T(8,128)(2,1)S(1)}, bf16[192,1280]{1,0:T(8,128)(2,1)S(1)}, u32[]{:S(2)}, u32[]{:S(2)}) collective-permute-start(bf16[192,1280]{1,0:T(8,128)(2,1)S(1)} %get-tuple-element.28), channel_id=1, source_target_pairs={{4,8},{8,4},{5,9},{9,5},{6,10},{10,6},{7,11},{11,7},{20,24},{24,20... | collective-permute-start | bytes 1474568 | tf_op jit(solution)/shard_map/ppermute | solution.py:349
  146.2 18.8 %collective-permute-start.19 = (bf16[192,1280]{1,0:T(8,128)(2,1)S(1)}, bf16[192,1280]{1,0:T(8,128)(2,1)S(1)}, u32[]{:S(2)}, u32[]{:S(2)}) collective-permute-start(bf16[192,1280]{1,0:T(8,128)(2,1)S(1)} %get-tuple-element.26), channel_id=1, source_target_pairs={{0,4},{12,8},{1,5},{13,9},{2,6},{14,10},{3,7},{15,11},{16,20},{28,... | collective-permute-start | bytes 1474568 | tf_op jit(solution)/shard_map/ppermute | solution.py:349
  153.6 20.2 %collective-permute-start.22 = (bf16[192,1280]{1,0:T(8,128)(2,1)S(1)}, bf16[192,1280]{1,0:T(8,128)(2,1)S(1)}, u32[]{:S(2)}, u32[]{:S(2)}) collective-permute-start(bf16[192,1280]{1,0:T(8,128)(2,1)S(1)} %add_convert_fusion.1), channel_id=1, source_target_pairs={{0,4},{4,0},{8,12},{12,8},{1,5},{5,1},{9,13},{13,9},{2,6},{6,2},{1... | collective-permute-start | bytes 1474568 | tf_op jit(solution)/shard_map/ppermute | solution.py:349
  165.2 8.6 %collective-permute-start.20 = (bf16[192,1280]{1,0:T(8,128)(2,1)S(1)}, bf16[192,1280]{1,0:T(8,128)(2,1)S(1)}, u32[]{:S(2)}, u32[]{:S(2)}) collective-permute-start(bf16[192,1280]{1,0:T(8,128)(2,1)S(1)} %add_convert_fusion.2), channel_id=1, source_target_pairs={{4,8},{8,4},{5,9},{9,5},{6,10},{10,6},{7,11},{11,7},{20,24},{24,20... | collective-permute-start | bytes 1474568 | tf_op jit(solution)/shard_map/ppermute | solution.py:349

commit v2 on v1

--- a/solution.py
+++ b/solution.py
@@ -136,7 +136,7 @@
         store(out[:, LANES:], 2 * LANES)
 
 
-def gate_up(where, placed, gu_weight, chunk, group, after):
+def gate_up(where, placed, gu_weight, start, group, after):
     _, units, _, width = gu_weight.shape
     n_blocks = len(placed)
     lanes = 2 * n_blocks * CAP
@@ -147,8 +147,8 @@
         grid=(group,),
         out_shape=(half, half),
         in_specs=[pl.BlockSpec(memory_space=pltpu.SMEM)]
-        + [pl.BlockSpec((1, CAP, width), lambda i: (chunk * group + i, 0, 0))] * n_blocks
-        + [pl.BlockSpec((1, units, 2, width), lambda i: (chunk * group + i, 0, 0, 0))]
+        + [pl.BlockSpec((1, CAP, width), lambda i: (start + i, 0, 0))] * n_blocks
+        + [pl.BlockSpec((1, units, 2, width), lambda i: (start + i, 0, 0, 0))]
         + [pl.BlockSpec(memory_space=pl.ANY)],
         out_specs=(pair, pair),
         scratch_shapes=[
@@ -212,7 +212,7 @@
     )(keep, near, after)
 
 
-def down_kernel(group, n_blocks, chunk, has_carry, where_ref, *refs):
+def down_kernel(group, n_blocks, first, has_carry, final, where_ref, *refs):
     hidden_refs, refs = refs[:4], refs[4:]
     route_refs, refs = refs[:n_blocks], refs[n_blocks:]
     w_hbm, refs = refs[0], refs[2:]
@@ -231,7 +231,7 @@
             f0 = pl.multiple_of((order[j][0] * 2 + order[j][1]) * quarter, quarter)
             copies.append(
                 pltpu.make_async_copy(
-                    w_hbm.at[chunk * group + e, pl.ds(f0, quarter)],
+                    w_hbm.at[first + e, pl.ds(f0, quarter)],
                     w_buf.at[e, pl.ds(j * quarter, quarter)],
                     sems.at[e, j],
                 )
@@ -242,8 +242,8 @@
         for copy in fetch(e):
             copy.start()
 
-    start(0)
-    start(1)
+    for e in range(min(2, group)):
+        start(e)
     for e in range(group):
         for copy in fetch(e):
             copy.wait()
@@ -266,24 +266,27 @@
         table = jnp.concatenate(table, axis=0).astype(BF16)
         total = lax.dot_general(table, held[i], TN, preferred_element_type=F32)
         if has_carry:
-            out_refs[i][...] = (total + carry_ref[i]).astype(BF16)
+            total = total + carry_ref[i]
+        if final:
+            out_refs[i][...] = total.astype(BF16)
         else:
             out_refs[0][i] = total
 
 
-def down(where, hidden, routes, down_weight, chunk, group, carry, after):
+def down(where, hidden, routes, down_weight, first, group, carry, after):
     n_blocks = len(routes)
     units = hidden[0].shape[1]
     count = routes[0].shape[1]
     width = down_weight.shape[2]
     whole = pl.BlockSpec(memory_space=pltpu.VMEM)
     carried = [] if carry is None else [carry]
-    if carry is None:
+    final = first + group == down_weight.shape[0]
+    if not final:
         out_shape = (jax.ShapeDtypeStruct((n_blocks, count, width), F32),)
     else:
         out_shape = tuple(jax.ShapeDtypeStruct((count, width), BF16) for _ in routes)
     return pl.pallas_call(
-        functools.partial(down_kernel, group, n_blocks, chunk, carry is not None),
+        functools.partial(down_kernel, group, n_blocks, first, carry is not None, final),
         out_shape=out_shape,
         in_specs=[pl.BlockSpec(memory_space=pltpu.SMEM)]
         + [whole] * (4 + n_blocks)
@@ -342,8 +345,8 @@
     z, t = lax.axis_index("ep"), lax.axis_index("tp")
     x, core = t // 2, t % 2
     local = gu_weight.shape[0]
-    group = local // 2
-    wheres = [jnp.stack([z * local + n * group, x, core]).astype(jnp.int32) for n in range(2)]
+    groups = [(0, local // 4), (local // 4, local // 2), (local * 3 // 4, local // 4)]
+    wheres = [jnp.stack([z * local + first, x, core]).astype(jnp.int32) for first, _ in groups]
 
     def hop(array, pairs):
         return lax.ppermute(array, "ep", pairs)
@@ -354,20 +357,21 @@
     table_1 = hop(table, PAIR)
     table_2 = hop(table, [(i, i ^ 2) for i in range(4)])
     table_3 = hop(table, [(i, i ^ 3) for i in range(4)])
-    neighbour, middle_1 = hold((neighbour, middle_1), (table_1, table_2, table_3))
+    placed = [place(wheres[0], (tokens,), table, local)]
+    neighbour, middle_1 = hold((neighbour, middle_1), placed)
     inner = (z == 1) | (z == 2)
     table_in = jnp.where(inner, table_3, table_2)
     table_out = jnp.where(inner, table_2, table_3)
     middle_2 = hop(neighbour, MIDDLE)
     end_1 = hop(middle_1, OUTWARD)
+    (middle_2,) = hold((middle_2,), (table_1, table_2, table_3))
     end_2 = hop(middle_2, OUTWARD)
-
     tables = [table, table_1, table_in, table_out]
-    blocks = [(tokens,), (neighbour,), (middle_1, end_1), (middle_2, end_2)]
-    placed = [place(wheres[0], b, t, local) for b, t in zip(blocks, tables)]
+    blocks = [(neighbour,), (middle_1, end_1), (middle_2, end_2)]
+    placed += [place(wheres[0], b, t, local) for b, t in zip(blocks, tables[1:])]
 
     def sums(n, after):
-        send, keep = gate_up(wheres[n], placed, gu_weight, n, group, after)
+        send, keep = gate_up(wheres[n], placed, gu_weight, *groups[n], after)
         return keep, lax.ppermute(send, "tp", ACROSS_CORE)
 
     def across(keep, near, after):
@@ -378,6 +382,9 @@
         own_x = lax.ppermute(own, "tp", ACROSS_X)
         own_core = lax.ppermute(own, "tp", ACROSS_CORE)
         return own, own_x, own_core, lax.ppermute(own_x, "tp", ACROSS_CORE)
+
+    def outputs(n, hidden, carry, after):
+        return down(wheres[n], hidden, tables, down_weight, *groups[n], carry, after)
 
     keep_0, near_0 = sums(0, placed[3])
     turn, far_0 = across(keep_0, near_0, keep_0)
@@ -385,12 +392,14 @@
     own_0 = hidden_quarter(keep_0, near_0, far_0, keep_1)
     hidden_0 = gathered(own_0)
     turn, far_1 = across(keep_1, near_1, own_0)
-    (carry,) = down(wheres[0], hidden_0, tables, down_weight, 0, group, None, turn)
+    keep_2, near_2 = sums(2, turn)
+    (carry,) = outputs(0, hidden_0, None, keep_2)
     own_1 = hidden_quarter(keep_1, near_1, far_1, carry)
     hidden_1 = gathered(own_1)
-    own, other, far_in, far_out = down(
-        wheres[1], hidden_1, tables, down_weight, 1, group, carry, own_1
-    )
+    turn, far_2 = across(keep_2, near_2, own_1)
+    (carry,) = outputs(1, hidden_1, carry, turn)
+    own_2 = hidden_quarter(keep_2, near_2, far_2, carry)
+    own, other, far_in, far_out = outputs(2, gathered(own_2), carry, own_2)
 
     def plus(a, b):
         return (a.astype(F32) + b.astype(F32)).astype(BF16)

time: 178 us -> 208 us (1.17); the launches traced: 175 us -> 207 us
  waiting for transfers between devices: 84.5 us -> 105 us
  local copies, waits for them, and re-layouts: 2.29 us -> 13.1 us
  Pallas kernels: 45.4 us -> 51.1 us
  starting transfers between devices: 39.6 us -> 34.4 us
    ppermute x2 -> x3, waiting for transfers between devices: 17.7 us -> 38.4 us  [gathered(): own_x = lax.ppermute(own, 'tp', ACROSS_X)]
    unnamed x18 -> x38, local copies, waits for them, and re-layouts: 2.29 us -> 13.1 us
    ppermute x13, waiting for transfers between devices: 47.1 us -> 56.8 us  [hop(): return lax.ppermute(array, 'ep', pairs)]
    ppermute x2 -> x3, waiting for transfers between devices: 12.8 us -> 3.59 us  [across(): return (total, lax.ppermute(total, 'tp', ACROSS_X))]
    ppermute x13, starting transfers between devices: 34.2 us -> 28.3 us  [hop(): return lax.ppermute(array, 'ep', pairs)]
    pallas_call x2 -> x3, Pallas kernels: 12.6 us -> 15.8 us  [down(): pl.pallas_call(functools.partial(down_kernel, group, n_blocks, first, car...]
    pallas_call x2 -> x3, Pallas kernels: 22.3 us -> 23.5 us  [gate_up(): pl.pallas_call(functools.partial(gate_up_kernel, n_blocks), grid=(group,)...]
  transfers between devices with their start and end apart: 23 -> 28, of which waited for: 14 -> 15; matrix products, arithmetic and copies ran while one was open for 1% -> 1% of each run, Pallas kernels for 14% -> 18%
where the time goes in v2:
time: 208 us; the launch traced here: 207 us
  waiting for transfers between devices  105 us (50%)
  Pallas kernels  51.1 us (25%)
  starting transfers between devices  34.4 us (17%)
  local copies, waits for them, and re-layouts  13.1 us (6%)
  other arithmetic  2.72 us (1%)
    ppermute x13, waiting for transfers between devices, hop(): return lax.ppermute(array, 'ep', pairs)  56.8 us
    ppermute x3, waiting for transfers between devices, gathered(): own_x = lax.ppermute(own, 'tp', ACROSS_X)  38.4 us
    ppermute x13, starting transfers between devices, hop(): return lax.ppermute(array, 'ep', pairs)  28.3 us
    pallas_call x3, Pallas kernels, gate_up(): pl.pallas_call(functools.partial(gate_up_kernel, n_blocks), grid=(group,)...  23.5 us
    pallas_call x3, Pallas kernels, down(): pl.pallas_call(functools.partial(down_kernel, group, n_blocks, first, car...  15.8 us
    unnamed x38, local copies, waits for them, and re-layouts  13.1 us
    pallas_call x4, Pallas kernels, place(): pl.pallas_call(functools.partial(place_kernel, experts), out_shape=jax.Sh...  4.81 us
  transfers between devices with their start and end apart: 28, of which 15 were waited for; matrix products, arithmetic and copies ran while one was open for 1% of the time, Pallas kernels for 18%

profile of v2, /device:TPU:0, one launch (start us, length us, event | category | flops | bytes accessed | tf_op | source)
XLA Modules:
  0.0 206.9 jit_solution(8533434783736307045)
XLA Ops:
  0.0 3.0 %collective-permute-start = (bf16[192,1280]{1,0:T(8,128)(2,1)}, bf16[192,1280]{1,0:T(8,128)(2,1)S(1)}, u32[]{:S(2)}, u32[]{:S(2)}) collective-permute-start(bf16[192,1280]{1,0:T(8,128)(2,1)} %refs_0_.1), channel_id=1, source_target_pairs={{0,4},{4,0},{8,12},{12,8},{1,5},{5,1},{9,13},{13,9},{2,6},{6,2},{1... | collective-permute-start | bytes 1474568 | tf_op jit(solution)/shard_map/ppermute | solution.py:352
  5.1 1.5 route.1.refs_1_.refs_4_
  9.4 5.1 %collective-permute-done.__0_ = bf16[192,1280]{1,0:T(8,128)(2,1)S(1)} collective-permute-done((bf16[192,1280]{1,0:T(8,128)(2,1)}, bf16[192,1280]{1,0:T(8,128)(2,1)S(1)}, u32[]{:S(2)}, u32[]{:S(2)}) %collective-permute-start) | collective-permute-done | bytes 491552 | tf_op jit(solution)/shard_map/ppermute | solution.py:352
  15.1 7.8 %collective-permute-start.2 = (f32[64,192]{1,0:T(8,128)S(1)}, f32[64,192]{1,0:T(8,128)S(1)}, u32[]{:S(2)}, u32[]{:S(2)}) collective-permute-start(f32[64,192]{1,0:T(8,128)S(1)} %copy-done.6), channel_id=1, source_target_pairs={{0,4},{4,0},{8,12},{12,8},{1,5},{5,1},{9,13},{13,9},{2,6},{6,2},{1... | collective-permute-start | bytes 147464 | tf_op jit(solution)/shard_map/ppermute | solution.py:352
  25.8 3.4 %collective-permute-done.4.__3_ = f32[64,192]{1,0:T(8,128)S(1)} collective-permute-done((f32[64,192]{1,0:T(8,128)S(1)}, f32[64,192]{1,0:T(8,128)S(1)}, u32[]{:S(2)}, u32[]{:S(2)}) %collective-permute-start.4) | collective-permute-done | bytes 49184 | tf_op jit(solution)/shard_map/ppermute | solution.py:352
  29.1 9.2 %collective-permute-done.5.__2_ = f32[64,192]{1,0:T(8,128)S(1)} collective-permute-done((f32[64,192]{1,0:T(8,128)S(1)}, f32[64,192]{1,0:T(8,128)S(1)}, u32[]{:S(2)}, u32[]{:S(2)}) %collective-permute-start.5) | collective-permute-done | bytes 49184 | tf_op jit(solution)/shard_map/ppermute | solution.py:352
  40.7 1.5 place.6.refs_2_
  42.1 9.0 %collective-permute-done.7.refs_1_ = bf16[192,1280]{1,0:T(8,128)(2,1)} collective-permute-done((bf16[192,1280]{1,0:T(8,128)(2,1)S(1)}, bf16[192,1280]{1,0:T(8,128)(2,1)}, u32[]{:S(2)}, u32[]{:S(2)}) %collective-permute-start.7) | collective-permute-done | bytes 491552 | tf_op jit(solution)/shard_map/ppermute | solution.py:352
  51.1 1.5 place.7.refs_3_.refs_5_
  52.6 6.2 %gate_up.3 = (bf16[2,512,384]{2,1,0:T(8,128)(2,1)S(1)}, bf16[2,512,384]{2,1,0:T(8,128)(2,1)S(1)}) custom-call(s32[3]{0:T(128)S(1)} %add_add_fusion.1.where_ref, bf16[8,48,1280]{2,1,0:T(8,128)(2,1)S(1)} %place.4.__2_.refs_0_, bf16[8,48,1280]{2,1,0:T(8,128)(2,1)S(1)} %place.5.refs_1_, bf16[8,48,1280]{2,1,0:T(8,128)(2,1)S(1)} %place.6.refs_2_, ...), custom_call_target="tpu_custom_call" | custom-call | flops 1024 | bytes 1024 | tf_op jit(solution)/shard_map/gate_up/pallas_call | solution.py:145
  58.8 2.3 %collective-permute-done.8.near_ref = bf16[2,512,384]{2,1,0:T(8,128)(2,1)S(1)} collective-permute-done((bf16[2,512,384]{2,1,0:T(8,128)(2,1)S(1)}, bf16[2,512,384]{2,1,0:T(8,128)(2,1)S(1)}, u32[]{:S(2)}, u32[]{:S(2)}) %collective-permute-start.8) | collective-permute-done | bytes 786464 | tf_op jit(solution)/shard_map/ppermute | solution.py:375
  62.9 1.5 collective-permute-start.10
  65.6 11.1 %gate_up.4 = (bf16[2,512,768]{2,1,0:T(8,128)(2,1)S(1)}, bf16[2,512,768]{2,1,0:T(8,128)(2,1)S(1)}) custom-call(s32[3]{0:T(128)S(1)} %add_add_fusion.2.where_ref, bf16[8,48,1280]{2,1,0:T(8,128)(2,1)S(1)} %place.4.__2_.refs_0_, bf16[8,48,1280]{2,1,0:T(8,128)(2,1)S(1)} %place.5.refs_1_, bf16[8,48,1280]{2,1,0:T(8,128)(2,1)S(1)} %copy-done.2, ...), custom_call_target="tpu_custom_call" | custom-call | flops 1024 | bytes 1024 | tf_op jit(solution)/shard_map/gate_up/pallas_call | solution.py:145
  76.8 1.7 hidden.3._.refs_0_
  78.5 1.7 collective-permute-done.9.near_ref
  82.2 1.5 collective-permute-start.13
  83.7 21.9 %collective-permute-done.13.refs_1_ = bf16[384,256]{1,0:T(8,128)(2,1)S(1)} collective-permute-done((bf16[384,256]{1,0:T(8,128)(2,1)S(1)}, bf16[384,256]{1,0:T(8,128)(2,1)S(1)}, u32[]{:S(2)}, u32[]{:S(2)}) %collective-permute-start.13) | collective-permute-done | bytes 196640 | tf_op jit(solution)/shard_map/ppermute | solution.py:382
  106.9 6.3 %gate_up.5 = (bf16[2,512,384]{2,1,0:T(8,128)(2,1)S(1)}, bf16[2,512,384]{2,1,0:T(8,128)(2,1)S(1)}) custom-call(s32[3]{0:T(128)S(1)} %add_add_fusion.where_ref, bf16[8,48,1280]{2,1,0:T(8,128)(2,1)S(1)} %place.4.__2_.refs_0_, bf16[8,48,1280]{2,1,0:T(8,128)(2,1)S(1)} %place.5.refs_1_, bf16[8,48,1280]{2,1,0:T(8,128)(2,1)S(1)} %copy-done.3, ...), custom_call_target="tpu_custom_call" | custom-call | flops 1024 | bytes 1024 | tf_op jit(solution)/shard_map/gate_up/pallas_call | solution.py:145
  113.9 7.0 %copy-done = bf16[8,1024,1280]{2,1,0:T(8,128)(2,1)S(1)} copy-done((bf16[8,1024,1280]{2,1,0:T(8,128)(2,1)S(1)}, bf16[8,1024,1280]{2,1,0:T(8,128)(2,1)}, u32[]{:S(2)}) %copy-start) | copy-done | bytes 20971544
  120.8 5.0 %down.3._.refs_10_ = f32[4,192,1280]{2,1,0:T(8,128)S(1)} custom-call(s32[3]{0:T(128)S(1)} %add_add_fusion.1.where_ref, bf16[384,256]{1,0:T(8,128)(2,1)S(1)} %hidden.3._.refs_0_, bf16[384,256]{1,0:T(8,128)(2,1)S(1)} %collective-permute-done.13.refs_1_, bf16[384,256]{1,0:T(8,128)(2,1)} %collective-permute-done.14.refs_2_, ...), custom_call_target="tpu_custom_call" | custom-call | flops 1024 | bytes 1024 | tf_op jit(solution)/shard_map/down/pallas_call | solution.py:288
  125.9 1.8 hidden.4._.refs_0_
  128.3 10.5 %collective-permute-done.17.refs_1_ = bf16[768,256]{1,0:T(8,128)(2,1)S(1)} collective-permute-done((bf16[768,256]{1,0:T(8,128)(2,1)S(1)}, bf16[768,256]{1,0:T(8,128)(2,1)S(1)}, u32[]{:S(2)}, u32[]{:S(2)}) %collective-permute-start.17) | collective-permute-done | bytes 393248 | tf_op jit(solution)/shard_map/ppermute | solution.py:382
  140.5 6.4 %down.4._.refs_10_ = f32[4,192,1280]{2,1,0:T(8,128)S(1)} custom-call(s32[3]{0:T(128)S(1)} %add_add_fusion.2.where_ref, bf16[768,256]{1,0:T(8,128)(2,1)S(1)} %hidden.4._.refs_0_, bf16[768,256]{1,0:T(8,128)(2,1)S(1)} %collective-permute-done.17.refs_1_, bf16[768,256]{1,0:T(8,128)(2,1)S(1)} %collective-permute-done.18.refs_2_, ...), custom_call_target="tpu_custom_call" | custom-call | flops 1024 | bytes 1024 | tf_op jit(solution)/shard_map/down/pallas_call | solution.py:288
  146.9 3.6 %collective-permute-done.16.far_ref = bf16[512,384]{1,0:T(8,128)(2,1)S(1)} collective-permute-done((bf16[512,384]{1,0:T(8,128)(2,1)S(1)}, bf16[512,384]{1,0:T(8,128)(2,1)S(1)}, u32[]{:S(2)}, u32[]{:S(2)}) %collective-permute-start.16) | collective-permute-done | bytes 393248 | tf_op jit(solution)/shard_map/ppermute | solution.py:379
  151.5 6.0 %collective-permute-done.20.refs_1_ = bf16[384,256]{1,0:T(8,128)(2,1)S(1)} collective-permute-done((bf16[384,256]{1,0:T(8,128)(2,1)S(1)}, bf16[384,256]{1,0:T(8,128)(2,1)S(1)}, u32[]{:S(2)}, u32[]{:S(2)}) %collective-permute-start.20) | collective-permute-done | bytes 196640 | tf_op jit(solution)/shard_map/ppermute | solution.py:382
  157.5 1.4 collective-permute-done.22.refs_3_
  159.0 4.4 %down.5 = (bf16[192,1280]{1,0:T(8,128)(2,1)S(1)}, bf16[192,1280]{1,0:T(8,128)(2,1)S(1)}, bf16[192,1280]{1,0:T(8,128)(2,1)S(1)}, bf16[192,1280]{1,0:T(8,128)(2,1)S(1)}) custom-call(s32[3]{0:T(128)S(1)} %add_add_fusion.where_ref, bf16[384,256]{1,0:T(8,128)(2,1)S(1)} %hidden.5.refs_0_.refs_9_, bf16[384,256]{1,0:T(8,128)(2,1)S(1)} %collective-permute-done.20.refs_1_, ...), custom_call_target="tpu_custom_call" | custom-call | flops 1024 | bytes 1024 | tf_op jit(solution)/shard_map/down/pallas_call | solution.py:288
  164.8 11.0 %collective-permute-done.23.b_ref = bf16[192,1280]{1,0:T(8,128)(2,1)S(1)} collective-permute-done((bf16[192,1280]{1,0:T(8,128)(2,1)S(1)}, bf16[192,1280]{1,0:T(8,128)(2,1)S(1)}, u32[]{:S(2)}, u32[]{:S(2)}) %collective-permute-start.23) | collective-permute-done | bytes 491552 | tf_op jit(solution)/shard_map/ppermute | solution.py:352
  175.8 4.4 %collective-permute-start.24 = (bf16[192,1280]{1,0:T(8,128)(2,1)S(1)}, bf16[192,1280]{1,0:T(8,128)(2,1)S(1)}, u32[]{:S(2)}, u32[]{:S(2)}) collective-permute-start(bf16[192,1280]{1,0:T(8,128)(2,1)S(1)} %get-tuple-element.30), channel_id=1, source_target_pairs={{0,4},{12,8},{1,5},{13,9},{2,6},{14,10},{3,7},{15,11},{16,20},{28,... | collective-permute-start | bytes 1474568 | tf_op jit(solution)/shard_map/ppermute | solution.py:352
  181.0 9.5 %collective-permute-done.24 = bf16[192,1280]{1,0:T(8,128)(2,1)S(1)} collective-permute-done((bf16[192,1280]{1,0:T(8,128)(2,1)S(1)}, bf16[192,1280]{1,0:T(8,128)(2,1)S(1)}, u32[]{:S(2)}, u32[]{:S(2)}) %collective-permute-start.24) | collective-permute-done | bytes 491552 | tf_op jit(solution)/shard_map/ppermute | solution.py:352
  191.4 4.8 %collective-permute-start.27 = (bf16[192,1280]{1,0:T(8,128)(2,1)S(1)}, bf16[192,1280]{1,0:T(8,128)(2,1)S(1)}, u32[]{:S(2)}, u32[]{:S(2)}) collective-permute-start(bf16[192,1280]{1,0:T(8,128)(2,1)S(1)} %add_convert_fusion.1), channel_id=1, source_target_pairs={{0,4},{4,0},{8,12},{12,8},{1,5},{5,1},{9,13},{13,9},{2,6},{6,2},{1... | collective-permute-start | bytes 1474568 | tf_op jit(solution)/shard_map/ppermute | solution.py:352
  196.2 9.7 %collective-permute-done.27 = bf16[192,1280]{1,0:T(8,128)(2,1)S(1)} collective-permute-done((bf16[192,1280]{1,0:T(8,128)(2,1)S(1)}, bf16[192,1280]{1,0:T(8,128)(2,1)S(1)}, u32[]{:S(2)}, u32[]{:S(2)}) %collective-permute-start.27) | collective-permute-done | bytes 491552 | tf_op jit(solution)/shard_map/ppermute | solution.py:352
  (90 shorter events, 25.0 us)
Async XLA Ops:
  0.0 14.5 %collective-permute-start = (bf16[192,1280]{1,0:T(8,128)(2,1)}, bf16[192,1280]{1,0:T(8,128)(2,1)S(1)}, u32[]{:S(2)}, u32[]{:S(2)}) collective-permute-start(bf16[192,1280]{1,0:T(8,128)(2,1)} %refs_0_.1), channel_id=1, source_target_pairs={{0,4},{4,0},{8,12},{12,8},{1,5},{5,1},{9,13},{13,9},{2,6},{6,2},{1... | collective-permute-start | bytes 1474568 | tf_op jit(solution)/shard_map/ppermute | solution.py:352
  3.0 11.4 %collective-permute-start.1 = (bf16[192,1280]{1,0:T(8,128)(2,1)}, bf16[192,1280]{1,0:T(8,128)(2,1)S(1)}, u32[]{:S(2)}, u32[]{:S(2)}) collective-permute-start(bf16[192,1280]{1,0:T(8,128)(2,1)} %refs_0_.1), channel_id=1, source_target_pairs={{4,8},{8,4},{5,9},{9,5},{6,10},{10,6},{7,11},{11,7},{20,24},{24,20... | collective-permute-start | bytes 1474568 | tf_op jit(solution)/shard_map/ppermute | solution.py:352
  14.5 23.9 %collective-permute-start.6 = (bf16[192,1280]{1,0:T(8,128)(2,1)S(1)}, bf16[192,1280]{1,0:T(8,128)(2,1)S(1)}, u32[]{:S(2)}, u32[]{:S(2)}) collective-permute-start(bf16[192,1280]{1,0:T(8,128)(2,1)S(1)} %get-tuple-element.19.refs_0_), channel_id=1, source_target_pairs={{4,8},{8,4},{5,9},{9,5},{6,10},{10,6},{7,11},{11,7},{20,24},{24,20... | collective-permute-start | bytes 1474568 | tf_op jit(solution)/shard_map/ppermute | solution.py:352
  15.1 10.6 %collective-permute-start.2 = (f32[64,192]{1,0:T(8,128)S(1)}, f32[64,192]{1,0:T(8,128)S(1)}, u32[]{:S(2)}, u32[]{:S(2)}) collective-permute-start(f32[64,192]{1,0:T(8,128)S(1)} %copy-done.6), channel_id=1, source_target_pairs={{0,4},{4,0},{8,12},{12,8},{1,5},{5,1},{9,13},{13,9},{2,6},{6,2},{1... | collective-permute-start | bytes 147464 | tf_op jit(solution)/shard_map/ppermute | solution.py:352
  22.9 6.2 %collective-permute-start.4 = (f32[64,192]{1,0:T(8,128)S(1)}, f32[64,192]{1,0:T(8,128)S(1)}, u32[]{:S(2)}, u32[]{:S(2)}) collective-permute-start(f32[64,192]{1,0:T(8,128)S(1)} %copy-done.6), channel_id=1, source_target_pairs={{0,12},{4,8},{8,4},{12,0},{1,13},{5,9},{9,5},{13,1},{2,14},{6,10},... | collective-permute-start | bytes 147464 | tf_op jit(solution)/shard_map/ppermute | solution.py:352
  24.1 14.2 %collective-permute-start.5 = (f32[64,192]{1,0:T(8,128)S(1)}, f32[64,192]{1,0:T(8,128)S(1)}, u32[]{:S(2)}, u32[]{:S(2)}) collective-permute-start(f32[64,192]{1,0:T(8,128)S(1)} %copy-done.6), channel_id=1, source_target_pairs={{0,8},{4,12},{8,0},{12,4},{1,9},{5,13},{9,1},{13,5},{2,10},{6,14},... | collective-permute-start | bytes 147464 | tf_op jit(solution)/shard_map/ppermute | solution.py:352
  24.5 16.2 %collective-permute-start.3 = (bf16[192,1280]{1,0:T(8,128)(2,1)S(1)}, bf16[192,1280]{1,0:T(8,128)(2,1)}, u32[]{:S(2)}, u32[]{:S(2)}) collective-permute-start(bf16[192,1280]{1,0:T(8,128)(2,1)S(1)} %get-tuple-element.20.refs_0_), channel_id=1, source_target_pairs={{4,0},{8,12},{5,1},{9,13},{6,2},{10,14},{7,3},{11,15},{20,16},{24,... | collective-permute-start | bytes 1474568 | tf_op jit(solution)/shard_map/ppermute | solution.py:352
  38.4 12.8 %collective-permute-start.7 = (bf16[192,1280]{1,0:T(8,128)(2,1)S(1)}, bf16[192,1280]{1,0:T(8,128)(2,1)}, u32[]{:S(2)}, u32[]{:S(2)}) collective-permute-start(bf16[192,1280]{1,0:T(8,128)(2,1)S(1)} %hold.3.refs_0_), channel_id=1, source_target_pairs={{4,0},{8,12},{5,1},{9,13},{6,2},{10,14},{7,3},{11,15},{20,16},{24,... | collective-permute-start | bytes 1474568 | tf_op jit(solution)/shard_map/ppermute | solution.py:352
  39.7 11.4 %copy-start.8 = (f32[64,192]{1,0:T(8,128)}, f32[64,192]{1,0:T(8,128)S(1)}, u32[]{:S(2)}) copy-start(f32[64,192]{1,0:T(8,128)S(1)} %get-tuple-element.33.refs_2_.refs_7_) | copy-start | bytes 147460
  39.7 11.4 %copy-start.10 = (f32[64,192]{1,0:T(8,128)}, f32[64,192]{1,0:T(8,128)S(1)}, u32[]{:S(2)}) copy-start(f32[64,192]{1,0:T(8,128)S(1)} %get-tuple-element.34.refs_2_.refs_6_) | copy-start | bytes 147460
  42.1 16.6 %copy-start.1 = (bf16[8,48,1280]{2,1,0:T(8,128)(2,1)}, bf16[8,48,1280]{2,1,0:T(8,128)(2,1)S(1)}, u32[]{:S(2)}) copy-start(bf16[8,48,1280]{2,1,0:T(8,128)(2,1)S(1)} %place.6.refs_2_) | copy-start | bytes 2949124
  58.8 2.4 %collective-permute-start.8 = (bf16[2,512,384]{2,1,0:T(8,128)(2,1)S(1)}, bf16[2,512,384]{2,1,0:T(8,128)(2,1)S(1)}, u32[]{:S(2)}, u32[]{:S(2)}) collective-permute-start(bf16[2,512,384]{2,1,0:T(8,128)(2,1)S(1)} %get-tuple-element.22), channel_id=1, source_target_pairs={{0,1},{1,0},{2,3},{3,2},{4,5},{5,4},{6,7},{7,6},{8,9},{9,8},{10,11... | collective-permute-start | bytes 2359304 | tf_op jit(solution)/shard_map/ppermute | solution.py:375
  62.9 13.9 %collective-permute-start.10 = (bf16[512,384]{1,0:T(8,128)(2,1)S(1)}, bf16[512,384]{1,0:T(8,128)(2,1)}, u32[]{:S(2)}, u32[]{:S(2)}) collective-permute-start(bf16[512,384]{1,0:T(8,128)(2,1)S(1)} %chip_sum.3.refs_5_), channel_id=1, source_target_pairs={{0,2},{1,3},{2,0},{3,1},{4,6},{5,7},{6,4},{7,5},{8,10},{9,11},{10,... | collective-permute-start | bytes 1179656 | tf_op jit(solution)/shard_map/ppermute | solution.py:379
  65.6 11.2 %copy-start.17 = (bf16[2,512,384]{2,1,0:T(8,128)(2,1)S(1)}, bf16[2,512,384]{2,1,0:T(8,128)(2,1)}, u32[]{:S(2)}) copy-start(bf16[2,512,384]{2,1,0:T(8,128)(2,1)} %copy-done.16) | copy-start | bytes 2359300
  76.7 3.5 %collective-permute-start.9 = (bf16[2,512,768]{2,1,0:T(8,128)(2,1)S(1)}, bf16[2,512,768]{2,1,0:T(8,128)(2,1)S(1)}, u32[]{:S(2)}, u32[]{:S(2)}) collective-permute-start(bf16[2,512,768]{2,1,0:T(8,128)(2,1)S(1)} %get-tuple-element.24), channel_id=1, source_target_pairs={{0,1},{1,0},{2,3},{3,2},{4,5},{5,4},{6,7},{7,6},{8,9},{9,8},{10,11... | collective-permute-start | bytes 4718600 | tf_op jit(solution)/shard_map/ppermute | solution.py:375
  81.6 44.2 %collective-permute-start.12 = (bf16[512,768]{1,0:T(8,128)(2,1)}, bf16[512,768]{1,0:T(8,128)(2,1)}, u32[]{:S(2)}, u32[]{:S(2)}) collective-permute-start(bf16[512,768]{1,0:T(8,128)(2,1)} %chip_sum.4.refs_5_), channel_id=1, source_target_pairs={{0,2},{1,3},{2,0},{3,1},{4,6},{5,7},{6,4},{7,5},{8,10},{9,11},{10,... | collective-permute-start | bytes 2359304 | tf_op jit(solution)/shard_map/ppermute | solution.py:379
  82.2 23.5 %collective-permute-start.13 = (bf16[384,256]{1,0:T(8,128)(2,1)S(1)}, bf16[384,256]{1,0:T(8,128)(2,1)S(1)}, u32[]{:S(2)}, u32[]{:S(2)}) collective-permute-start(bf16[384,256]{1,0:T(8,128)(2,1)S(1)} %hidden.3._.refs_0_), channel_id=1, source_target_pairs={{0,2},{1,3},{2,0},{3,1},{4,6},{5,7},{6,4},{7,5},{8,10},{9,11},{10,... | collective-permute-start | bytes 589832 | tf_op jit(solution)/shard_map/ppermute | solution.py:382
  83.7 30.1 %collective-permute-start.14 = (bf16[384,256]{1,0:T(8,128)(2,1)S(1)}, bf16[384,256]{1,0:T(8,128)(2,1)}, u32[]{:S(2)}, u32[]{:S(2)}) collective-permute-start(bf16[384,256]{1,0:T(8,128)(2,1)S(1)} %hidden.3._.refs_0_), channel_id=1, source_target_pairs={{0,1},{1,0},{2,3},{3,2},{4,5},{5,4},{6,7},{7,6},{8,9},{9,8},{10,11... | collective-permute-start | bytes 589832 | tf_op jit(solution)/shard_map/ppermute | solution.py:383
  105.6 8.2 %collective-permute-start.15 = (bf16[384,256]{1,0:T(8,128)(2,1)S(1)}, bf16[384,256]{1,0:T(8,128)(2,1)}, u32[]{:S(2)}, u32[]{:S(2)}) collective-permute-start(bf16[384,256]{1,0:T(8,128)(2,1)S(1)} %collective-permute-done.13.refs_1_), channel_id=1, source_target_pairs={{0,1},{1,0},{2,3},{3,2},{4,5},{5,4},{6,7},{7,6},{8,9},{9,8},{10,11... | collective-permute-start | bytes 589832 | tf_op jit(solution)/shard_map/ppermute | solution.py:384
  113.3 25.6 %collective-permute-start.11 = (bf16[2,512,384]{2,1,0:T(8,128)(2,1)S(1)}, bf16[2,512,384]{2,1,0:T(8,128)(2,1)S(1)}, u32[]{:S(2)}, u32[]{:S(2)}) collective-permute-start(bf16[2,512,384]{2,1,0:T(8,128)(2,1)S(1)} %get-tuple-element.26), channel_id=1, source_target_pairs={{0,1},{1,0},{2,3},{3,2},{4,5},{5,4},{6,7},{7,6},{8,9},{9,8},{10,11... | collective-permute-start | bytes 2359304 | tf_op jit(solution)/shard_map/ppermute | solution.py:375
  127.7 11.1 %collective-permute-start.17 = (bf16[768,256]{1,0:T(8,128)(2,1)S(1)}, bf16[768,256]{1,0:T(8,128)(2,1)S(1)}, u32[]{:S(2)}, u32[]{:S(2)}) collective-permute-start(bf16[768,256]{1,0:T(8,128)(2,1)S(1)} %hidden.4._.refs_0_), channel_id=1, source_target_pairs={{0,2},{1,3},{2,0},{3,1},{4,6},{5,7},{6,4},{7,5},{8,10},{9,11},{10,... | collective-permute-start | bytes 1179656 | tf_op jit(solution)/shard_map/ppermute | solution.py:382
  128.3 11.2 %collective-permute-start.18 = (bf16[768,256]{1,0:T(8,128)(2,1)S(1)}, bf16[768,256]{1,0:T(8,128)(2,1)S(1)}, u32[]{:S(2)}, u32[]{:S(2)}) collective-permute-start(bf16[768,256]{1,0:T(8,128)(2,1)S(1)} %hidden.4._.refs_0_), channel_id=1, source_target_pairs={{0,1},{1,0},{2,3},{3,2},{4,5},{5,4},{6,7},{7,6},{8,9},{9,8},{10,11... | collective-permute-start | bytes 1179656 | tf_op jit(solution)/shard_map/ppermute | solution.py:383
  138.8 1.7 collective-permute-start.19
  138.9 11.6 %collective-permute-start.16 = (bf16[512,384]{1,0:T(8,128)(2,1)S(1)}, bf16[512,384]{1,0:T(8,128)(2,1)S(1)}, u32[]{:S(2)}, u32[]{:S(2)}) collective-permute-start(bf16[512,384]{1,0:T(8,128)(2,1)S(1)} %chip_sum.5.refs_9_), channel_id=1, source_target_pairs={{0,2},{1,3},{2,0},{3,1},{4,6},{5,7},{6,4},{7,5},{8,10},{9,11},{10,... | collective-permute-start | bytes 1179656 | tf_op jit(solution)/shard_map/ppermute | solution.py:379
  150.9 6.6 %collective-permute-start.20 = (bf16[384,256]{1,0:T(8,128)(2,1)S(1)}, bf16[384,256]{1,0:T(8,128)(2,1)S(1)}, u32[]{:S(2)}, u32[]{:S(2)}) collective-permute-start(bf16[384,256]{1,0:T(8,128)(2,1)S(1)} %hidden.5.refs_0_.refs_9_), channel_id=1, source_target_pairs={{0,2},{1,3},{2,0},{3,1},{4,6},{5,7},{6,4},{7,5},{8,10},{9,11},{10,... | collective-permute-start | bytes 589832 | tf_op jit(solution)/shard_map/ppermute | solution.py:382
  151.5 6.0 %collective-permute-start.21 = (bf16[384,256]{1,0:T(8,128)(2,1)S(1)}, bf16[384,256]{1,0:T(8,128)(2,1)S(1)}, u32[]{:S(2)}, u32[]{:S(2)}) collective-permute-start(bf16[384,256]{1,0:T(8,128)(2,1)S(1)} %hidden.5.refs_0_.refs_9_), channel_id=1, source_target_pairs={{0,1},{1,0},{2,3},{3,2},{4,5},{5,4},{6,7},{7,6},{8,9},{9,8},{10,11... | collective-permute-start | bytes 589832 | tf_op jit(solution)/shard_map/ppermute | solution.py:383
  157.5 1.4 collective-permute-start.22
  163.4 12.3 %collective-permute-start.23 = (bf16[192,1280]{1,0:T(8,128)(2,1)S(1)}, bf16[192,1280]{1,0:T(8,128)(2,1)S(1)}, u32[]{:S(2)}, u32[]{:S(2)}) collective-permute-start(bf16[192,1280]{1,0:T(8,128)(2,1)S(1)} %get-tuple-element.28.a_ref), channel_id=1, source_target_pairs={{0,4},{12,8},{1,5},{13,9},{2,6},{14,10},{3,7},{15,11},{16,20},{28,... | collective-permute-start | bytes 1474568 | tf_op jit(solution)/shard_map/ppermute | solution.py:352
  175.8 14.6 %collective-permute-start.24 = (bf16[192,1280]{1,0:T(8,128)(2,1)S(1)}, bf16[192,1280]{1,0:T(8,128)(2,1)S(1)}, u32[]{:S(2)}, u32[]{:S(2)}) collective-permute-start(bf16[192,1280]{1,0:T(8,128)(2,1)S(1)} %get-tuple-element.30), channel_id=1, source_target_pairs={{0,4},{12,8},{1,5},{13,9},{2,6},{14,10},{3,7},{15,11},{16,20},{28,... | collective-permute-start | bytes 1474568 | tf_op jit(solution)/shard_map/ppermute | solution.py:352
  180.3 11.0 %collective-permute-start.26 = (bf16[192,1280]{1,0:T(8,128)(2,1)S(1)}, bf16[192,1280]{1,0:T(8,128)(2,1)S(1)}, u32[]{:S(2)}, u32[]{:S(2)}) collective-permute-start(bf16[192,1280]{1,0:T(8,128)(2,1)S(1)} %get-tuple-element.32), channel_id=1, source_target_pairs={{4,8},{8,4},{5,9},{9,5},{6,10},{10,6},{7,11},{11,7},{20,24},{24,20... | collective-permute-start | bytes 1474568 | tf_op jit(solution)/shard_map/ppermute | solution.py:352
  190.6 5.7 %collective-permute-start.25 = (bf16[192,1280]{1,0:T(8,128)(2,1)S(1)}, bf16[192,1280]{1,0:T(8,128)(2,1)S(1)}, u32[]{:S(2)}, u32[]{:S(2)}) collective-permute-start(bf16[192,1280]{1,0:T(8,128)(2,1)S(1)} %add_convert_fusion.2), channel_id=1, source_target_pairs={{4,8},{8,4},{5,9},{9,5},{6,10},{10,6},{7,11},{11,7},{20,24},{24,20... | collective-permute-start | bytes 1474568 | tf_op jit(solution)/shard_map/ppermute | solution.py:352
  191.4 14.6 %collective-permute-start.27 = (bf16[192,1280]{1,0:T(8,128)(2,1)S(1)}, bf16[192,1280]{1,0:T(8,128)(2,1)S(1)}, u32[]{:S(2)}, u32[]{:S(2)}) collective-permute-start(bf16[192,1280]{1,0:T(8,128)(2,1)S(1)} %add_convert_fusion.1), channel_id=1, source_target_pairs={{0,4},{4,0},{8,12},{12,8},{1,5},{5,1},{9,13},{13,9},{2,6},{6,2},{1... | collective-permute-start | bytes 1474568 | tf_op jit(solution)/shard_map/ppermute | solution.py:352
  (15 other events, 59.9 us)

commit v3 on v2

--- a/solution.py
+++ b/solution.py
@@ -364,7 +364,6 @@
     table_out = jnp.where(inner, table_2, table_3)
     middle_2 = hop(neighbour, MIDDLE)
     end_1 = hop(middle_1, OUTWARD)
-    (middle_2,) = hold((middle_2,), (table_1, table_2, table_3))
     end_2 = hop(middle_2, OUTWARD)
     tables = [table, table_1, table_in, table_out]
     blocks = [(neighbour,), (middle_1, end_1), (middle_2, end_2)]
@@ -378,9 +377,11 @@
         total = chip_sum(keep, near, after)
         return total, lax.ppermute(total, "tp", ACROSS_X)
 
-    def gathered(own):
+    def halves(own):
         own_x = lax.ppermute(own, "tp", ACROSS_X)
-        own_core = lax.ppermute(own, "tp", ACROSS_CORE)
+        return own, own_x, lax.ppermute(own, "tp", ACROSS_CORE)
+
+    def gathered(own, own_x, own_core):
         return own, own_x, own_core, lax.ppermute(own_x, "tp", ACROSS_CORE)
 
     def outputs(n, hidden, carry, after):
@@ -390,16 +391,21 @@
     turn, far_0 = across(keep_0, near_0, keep_0)
     keep_1, near_1 = sums(1, turn)
     own_0 = hidden_quarter(keep_0, near_0, far_0, keep_1)
-    hidden_0 = gathered(own_0)
+    halves_0 = halves(own_0)
     turn, far_1 = across(keep_1, near_1, own_0)
     keep_2, near_2 = sums(2, turn)
-    (carry,) = outputs(0, hidden_0, None, keep_2)
-    own_1 = hidden_quarter(keep_1, near_1, far_1, carry)
-    hidden_1 = gathered(own_1)
+    own_1 = hidden_quarter(keep_1, near_1, far_1, keep_2)
+    halves_1 = halves(own_1)
     turn, far_2 = across(keep_2, near_2, own_1)
-    (carry,) = outputs(1, hidden_1, carry, turn)
+    own_0, x_0, core_0 = halves_0
+    (x_0,) = hold((x_0,), (own_1,))
+    (carry,) = outputs(0, gathered(own_0, x_0, core_0), None, turn)
     own_2 = hidden_quarter(keep_2, near_2, far_2, carry)
-    own, other, far_in, far_out = outputs(2, gathered(own_2), carry, own_2)
+    halves_2 = halves(own_2)
+    own_1, x_1, core_1 = halves_1
+    (x_1,) = hold((x_1,), (own_2,))
+    (carry,) = outputs(1, gathered(own_1, x_1, core_1), carry, own_2)
+    own, other, far_in, far_out = outputs(2, gathered(*halves_2), carry, carry)
 
     def plus(a, b):
         return (a.astype(F32) + b.astype(F32)).astype(BF16)

time: 208 us -> 187 us (0.90)
  waiting for transfers between devices: 105 us -> 77.1 us
  starting transfers between devices: 34.4 us -> 46.3 us
  local copies, waits for them, and re-layouts: 13.1 us -> 7.82 us
    ppermute x6, waiting for transfers between devices: 38.5 us -> 12.6 us  [the longest x3 12.6 us: halves(): own_x = lax.ppermute(own, 'tp', ACROSS_X)]
    ppermute x13, starting transfers between devices: 28.3 us -> 39.7 us  [hop(): return lax.ppermute(array, 'ep', pairs)]
    ppermute x3, waiting for transfers between devices: 3.59 us -> 13.3 us  [across(): return (total, lax.ppermute(total, 'tp', ACROSS_X))]
    ppermute x13, waiting for transfers between devices: 56.8 us -> 47.1 us  [hop(): return lax.ppermute(array, 'ep', pairs)]
    unnamed x38 -> x34, local copies, waits for them, and re-layouts: 13.1 us -> 7.82 us
    ppermute x3, waiting for transfers between devices: 2.45 us -> 0.01 us  [gathered(): return (own, own_x, own_core, lax.ppermute(own_x, 'tp', ACROSS_CORE))]
  transfers between devices with their start and end apart: 28 -> 28, of which waited for: 15 -> 13; matrix products, arithmetic and copies ran while one was open for 1% -> 1% of each run, Pallas kernels for 18% -> 20%
where the time goes in v3:
time: 187 us
  waiting for transfers between devices  77.1 us (41%)
  Pallas kernels  52.3 us (28%)
  starting transfers between devices  46.3 us (25%)
  local copies, waits for them, and re-layouts  7.82 us (4%)
  other arithmetic  2.73 us (1%)
    ppermute x13, waiting for transfers between devices, hop(): return lax.ppermute(array, 'ep', pairs)  47.1 us
    ppermute x13, starting transfers between devices, hop(): return lax.ppermute(array, 'ep', pairs)  39.7 us
    pallas_call x3, Pallas kernels, gate_up(): pl.pallas_call(functools.partial(gate_up_kernel, n_blocks), grid=(group,)...  23.5 us
    pallas_call x3, Pallas kernels, down(): pl.pallas_call(functools.partial(down_kernel, group, n_blocks, first, car...  16.1 us
    ppermute x3, waiting for transfers between devices, across(): return (total, lax.ppermute(total, 'tp', ACROSS_X))  13.3 us
    ppermute x3, waiting for transfers between devices, halves(): own_x = lax.ppermute(own, 'tp', ACROSS_X)  12.6 us
    unnamed x34, local copies, waits for them, and re-layouts  7.82 us
    pallas_call x4, Pallas kernels, place(): pl.pallas_call(functools.partial(place_kernel, experts), out_shape=jax.Sh...  5.6 us
  transfers between devices with their start and end apart: 28, of which 13 were waited for; matrix products, arithmetic and copies ran while one was open for 1% of the time, Pallas kernels for 20%

profile of v3, /device:TPU:0, one launch (start us, length us, event | category | flops | bytes accessed | tf_op | source)
XLA Modules:
  0.0 186.6 jit_solution(5974089867755217186)
XLA Ops:
  0.0 3.0 %collective-permute-start = (bf16[192,1280]{1,0:T(8,128)(2,1)}, bf16[192,1280]{1,0:T(8,128)(2,1)S(1)}, u32[]{:S(2)}, u32[]{:S(2)}) collective-permute-start(bf16[192,1280]{1,0:T(8,128)(2,1)} %refs_0_.1), channel_id=1, source_target_pairs={{0,4},{4,0},{8,12},{12,8},{1,5},{5,1},{9,13},{13,9},{2,6},{6,2},{1... | collective-permute-start | bytes 1474568 | tf_op jit(solution)/shard_map/ppermute | solution.py:352
  5.1 1.5 route.1.refs_1_.refs_4_
  8.9 5.6 %collective-permute-done.__0_ = bf16[192,1280]{1,0:T(8,128)(2,1)S(1)} collective-permute-done((bf16[192,1280]{1,0:T(8,128)(2,1)}, bf16[192,1280]{1,0:T(8,128)(2,1)S(1)}, u32[]{:S(2)}, u32[]{:S(2)}) %collective-permute-start) | collective-permute-done | bytes 491552 | tf_op jit(solution)/shard_map/ppermute | solution.py:352
  14.5 1.5 collective-permute-start.6
  18.5 3.8 %collective-permute-start.4 = (f32[64,192]{1,0:T(8,128)}, f32[64,192]{1,0:T(8,128)S(1)}, u32[]{:S(2)}, u32[]{:S(2)}) collective-permute-start(f32[64,192]{1,0:T(8,128)} %route.1.refs_1_.refs_4_), channel_id=1, source_target_pairs={{0,12},{4,8},{8,4},{12,0},{1,13},{5,9},{9,5},{13,1},{2,14},{6,10},... | collective-permute-start | bytes 147464 | tf_op jit(solution)/shard_map/ppermute | solution.py:352
  22.3 15.9 %collective-permute-start.5 = (f32[64,192]{1,0:T(8,128)}, f32[64,192]{1,0:T(8,128)S(1)}, u32[]{:S(2)}, u32[]{:S(2)}) collective-permute-start(f32[64,192]{1,0:T(8,128)} %route.1.refs_1_.refs_4_), channel_id=1, source_target_pairs={{0,8},{4,12},{8,0},{12,4},{1,9},{5,13},{9,1},{13,5},{2,10},{6,14},... | collective-permute-start | bytes 147464 | tf_op jit(solution)/shard_map/ppermute | solution.py:352
  38.3 3.4 %collective-permute-done.5 = f32[64,192]{1,0:T(8,128)S(1)} collective-permute-done((f32[64,192]{1,0:T(8,128)}, f32[64,192]{1,0:T(8,128)S(1)}, u32[]{:S(2)}, u32[]{:S(2)}) %collective-permute-start.5) | collective-permute-done | bytes 49184 | tf_op jit(solution)/shard_map/ppermute | solution.py:352
  41.7 7.4 %collective-permute-done.2.refs_1_.refs_5_ = f32[64,192]{1,0:T(8,128)S(1)} collective-permute-done((f32[64,192]{1,0:T(8,128)}, f32[64,192]{1,0:T(8,128)S(1)}, u32[]{:S(2)}, u32[]{:S(2)}) %collective-permute-start.2) | collective-permute-done | bytes 49184 | tf_op jit(solution)/shard_map/ppermute | solution.py:352
  50.1 1.5 place.6.refs_2_
  51.6 1.9 %place.7.refs_3_.refs_5_ = bf16[8,48,1280]{2,1,0:T(8,128)(2,1)S(1)} custom-call(s32[3]{0:T(128)S(1)} %add_add_fusion.1.where_ref, bf16[192,1280]{1,0:T(8,128)(2,1)} %collective-permute-done.6.refs_0_, bf16[192,1280]{1,0:T(8,128)(2,1)} %collective-permute-done.7.refs_1_, f32[64,192]{1,0:T(8,128)S(1)} %get-tuple-element.33.refs_2_.refs_7_), custom_call_target="tpu_custom_call" | custom-call | flops 1024 | bytes 1024 | tf_op jit(solution)/shard_map/place/pallas_call | solution.py:81
  53.5 6.2 %gate_up.3 = (bf16[2,512,384]{2,1,0:T(8,128)(2,1)S(1)}, bf16[2,512,384]{2,1,0:T(8,128)(2,1)S(1)}) custom-call(s32[3]{0:T(128)S(1)} %add_add_fusion.1.where_ref, bf16[8,48,1280]{2,1,0:T(8,128)(2,1)S(1)} %place.4.__2_.refs_0_, bf16[8,48,1280]{2,1,0:T(8,128)(2,1)S(1)} %place.5.refs_1_, bf16[8,48,1280]{2,1,0:T(8,128)(2,1)S(1)} %place.6.refs_2_, ...), custom_call_target="tpu_custom_call" | custom-call | flops 1024 | bytes 1024 | tf_op jit(solution)/shard_map/gate_up/pallas_call | solution.py:145
  59.8 2.3 %collective-permute-done.8.near_ref = bf16[2,512,384]{2,1,0:T(8,128)(2,1)S(1)} collective-permute-done((bf16[2,512,384]{2,1,0:T(8,128)(2,1)S(1)}, bf16[2,512,384]{2,1,0:T(8,128)(2,1)S(1)}, u32[]{:S(2)}, u32[]{:S(2)}) %collective-permute-start.8) | collective-permute-done | bytes 786464 | tf_op jit(solution)/shard_map/ppermute | solution.py:374
  63.8 1.5 collective-permute-start.10
  66.6 11.1 %gate_up.4 = (bf16[2,512,768]{2,1,0:T(8,128)(2,1)S(1)}, bf16[2,512,768]{2,1,0:T(8,128)(2,1)S(1)}) custom-call(s32[3]{0:T(128)S(1)} %add_add_fusion.2.where_ref, bf16[8,48,1280]{2,1,0:T(8,128)(2,1)S(1)} %place.4.__2_.refs_0_, bf16[8,48,1280]{2,1,0:T(8,128)(2,1)S(1)} %place.5.refs_1_, bf16[8,48,1280]{2,1,0:T(8,128)(2,1)S(1)} %copy-done.1, ...), custom_call_target="tpu_custom_call" | custom-call | flops 1024 | bytes 1024 | tf_op jit(solution)/shard_map/gate_up/pallas_call | solution.py:145
  77.8 1.7 hidden.3._.refs_0_
  79.4 1.7 collective-permute-done.9.near_ref
  83.2 1.5 collective-permute-start.14
  85.9 6.3 %gate_up.5 = (bf16[2,512,384]{2,1,0:T(8,128)(2,1)S(1)}, bf16[2,512,384]{2,1,0:T(8,128)(2,1)S(1)}) custom-call(s32[3]{0:T(128)S(1)} %add_add_fusion.where_ref, bf16[8,48,1280]{2,1,0:T(8,128)(2,1)S(1)} %place.4.__2_.refs_0_, bf16[8,48,1280]{2,1,0:T(8,128)(2,1)S(1)} %place.5.refs_1_, bf16[8,48,1280]{2,1,0:T(8,128)(2,1)S(1)} %copy-done.2, ...), custom_call_target="tpu_custom_call" | custom-call | flops 1024 | bytes 1024 | tf_op jit(solution)/shard_map/gate_up/pallas_call | solution.py:145
  92.3 11.0 %collective-permute-done.12.far_ref = bf16[512,768]{1,0:T(8,128)(2,1)} collective-permute-done((bf16[512,768]{1,0:T(8,128)(2,1)}, bf16[512,768]{1,0:T(8,128)(2,1)}, u32[]{:S(2)}, u32[]{:S(2)}) %collective-permute-start.12) | collective-permute-done | bytes 786464 | tf_op jit(solution)/shard_map/ppermute | solution.py:378
  103.3 2.0 %hidden.4._.__1_.refs_0_ = bf16[768,256]{1,0:T(8,128)(2,1)S(1)} custom-call(bf16[2,512,768]{2,1,0:T(8,128)(2,1)S(1)} %copy-done.6, bf16[2,512,768]{2,1,0:T(8,128)(2,1)S(1)} %copy-done.8, bf16[512,768]{1,0:T(8,128)(2,1)} %collective-permute-done.12.far_ref, bf16[2,512,384]{2,1,0:T(8,128)(2,1)S(1)} %get-tuple-element.25._.keep_ref), custom_call_target="tpu_custom_call" | custom-call | flops 20000000000 | bytes 1024 | tf_op jit(solution)/shard_map/hidden/pallas_call | solution.py:178
  110.6 4.7 %down.3._.refs_10_ = f32[4,192,1280]{2,1,0:T(8,128)S(1)} custom-call(s32[3]{0:T(128)S(1)} %add_add_fusion.1.where_ref, bf16[384,256]{1,0:T(8,128)(2,1)S(1)} %hidden.3._.refs_0_, bf16[384,256]{1,0:T(8,128)(2,1)S(1)} %hold.4.refs_1_, bf16[384,256]{1,0:T(8,128)(2,1)S(1)} %collective-permute-done.15.refs_2_, ...), custom_call_target="tpu_custom_call" | custom-call | flops 1024 | bytes 1024 | tf_op jit(solution)/shard_map/down/pallas_call | solution.py:288
  115.2 2.3 %collective-permute-done.13.far_ref = bf16[512,384]{1,0:T(8,128)(2,1)S(1)} collective-permute-done((bf16[512,384]{1,0:T(8,128)(2,1)S(1)}, bf16[512,384]{1,0:T(8,128)(2,1)S(1)}, u32[]{:S(2)}, u32[]{:S(2)}) %collective-permute-start.13) | collective-permute-done | bytes 393248 | tf_op jit(solution)/shard_map/ppermute | solution.py:378
  117.9 5.5 %collective-permute-done.20.__0_ = bf16[768,256]{1,0:T(8,128)(2,1)S(1)} collective-permute-done((bf16[768,256]{1,0:T(8,128)(2,1)S(1)}, bf16[768,256]{1,0:T(8,128)(2,1)S(1)}, u32[]{:S(2)}, u32[]{:S(2)}) %collective-permute-start.20) | collective-permute-done | bytes 393248 | tf_op jit(solution)/shard_map/ppermute | solution.py:381
  124.2 6.5 %collective-permute-done.17.refs_1_ = bf16[384,256]{1,0:T(8,128)(2,1)S(1)} collective-permute-done((bf16[384,256]{1,0:T(8,128)(2,1)S(1)}, bf16[384,256]{1,0:T(8,128)(2,1)S(1)}, u32[]{:S(2)}, u32[]{:S(2)}) %collective-permute-start.17) | collective-permute-done | bytes 196640 | tf_op jit(solution)/shard_map/ppermute | solution.py:381
  130.8 6.7 %down.4.refs_9_.refs_10_ = f32[4,192,1280]{2,1,0:T(8,128)S(1)} custom-call(s32[3]{0:T(128)S(1)} %add_add_fusion.2.where_ref, bf16[768,256]{1,0:T(8,128)(2,1)S(1)} %hidden.4._.__1_.refs_0_, bf16[768,256]{1,0:T(8,128)(2,1)S(1)} %hold.5.refs_1_, bf16[768,256]{1,0:T(8,128)(2,1)S(1)} %collective-permute-done.21.refs_2_, ...), custom_call_target="tpu_custom_call" | custom-call | flops 1024 | bytes 1024 | tf_op jit(solution)/shard_map/down/pallas_call | solution.py:288
  137.5 4.7 %down.5 = (bf16[192,1280]{1,0:T(8,128)(2,1)S(1)}, bf16[192,1280]{1,0:T(8,128)(2,1)S(1)}, bf16[192,1280]{1,0:T(8,128)(2,1)S(1)}, bf16[192,1280]{1,0:T(8,128)(2,1)S(1)}) custom-call(s32[3]{0:T(128)S(1)} %add_add_fusion.where_ref, bf16[384,256]{1,0:T(8,128)(2,1)S(1)} %hidden.5.__1_.refs_9_.refs_0_, bf16[384,256]{1,0:T(8,128)(2,1)S(1)} %collective-permute-done.17.refs_1_, ...), custom_call_target="tpu_custom_call" | custom-call | flops 1024 | bytes 1024 | tf_op jit(solution)/shard_map/down/pallas_call | solution.py:288
  142.3 1.6 collective-permute-start.23
  143.8 11.1 %collective-permute-done.23.b_ref = bf16[192,1280]{1,0:T(8,128)(2,1)S(1)} collective-permute-done((bf16[192,1280]{1,0:T(8,128)(2,1)S(1)}, bf16[192,1280]{1,0:T(8,128)(2,1)S(1)}, u32[]{:S(2)}, u32[]{:S(2)}) %collective-permute-start.23) | collective-permute-done | bytes 491552 | tf_op jit(solution)/shard_map/ppermute | solution.py:352
  155.1 4.4 %collective-permute-start.24 = (bf16[192,1280]{1,0:T(8,128)(2,1)S(1)}, bf16[192,1280]{1,0:T(8,128)(2,1)S(1)}, u32[]{:S(2)}, u32[]{:S(2)}) collective-permute-start(bf16[192,1280]{1,0:T(8,128)(2,1)S(1)} %get-tuple-element.30), channel_id=1, source_target_pairs={{0,4},{12,8},{1,5},{13,9},{2,6},{14,10},{3,7},{15,11},{16,20},{28,... | collective-permute-start | bytes 1474568 | tf_op jit(solution)/shard_map/ppermute | solution.py:352
  160.2 9.6 %collective-permute-done.24 = bf16[192,1280]{1,0:T(8,128)(2,1)S(1)} collective-permute-done((bf16[192,1280]{1,0:T(8,128)(2,1)S(1)}, bf16[192,1280]{1,0:T(8,128)(2,1)S(1)}, u32[]{:S(2)}, u32[]{:S(2)}) %collective-permute-start.24) | collective-permute-done | bytes 491552 | tf_op jit(solution)/shard_map/ppermute | solution.py:352
  170.8 4.9 %collective-permute-start.27 = (bf16[192,1280]{1,0:T(8,128)(2,1)S(1)}, bf16[192,1280]{1,0:T(8,128)(2,1)S(1)}, u32[]{:S(2)}, u32[]{:S(2)}) collective-permute-start(bf16[192,1280]{1,0:T(8,128)(2,1)S(1)} %add_convert_fusion.1), channel_id=1, source_target_pairs={{0,4},{4,0},{8,12},{12,8},{1,5},{5,1},{9,13},{13,9},{2,6},{6,2},{1... | collective-permute-start | bytes 1474568 | tf_op jit(solution)/shard_map/ppermute | solution.py:352
  175.7 10.0 %collective-permute-done.27 = bf16[192,1280]{1,0:T(8,128)(2,1)S(1)} collective-permute-done((bf16[192,1280]{1,0:T(8,128)(2,1)S(1)}, bf16[192,1280]{1,0:T(8,128)(2,1)S(1)}, u32[]{:S(2)}, u32[]{:S(2)}) %collective-permute-start.27) | collective-permute-done | bytes 491552 | tf_op jit(solution)/shard_map/ppermute | solution.py:352
  (88 shorter events, 23.5 us)
Async XLA Ops:
  0.0 14.5 %collective-permute-start = (bf16[192,1280]{1,0:T(8,128)(2,1)}, bf16[192,1280]{1,0:T(8,128)(2,1)S(1)}, u32[]{:S(2)}, u32[]{:S(2)}) collective-permute-start(bf16[192,1280]{1,0:T(8,128)(2,1)} %refs_0_.1), channel_id=1, source_target_pairs={{0,4},{4,0},{8,12},{12,8},{1,5},{5,1},{9,13},{13,9},{2,6},{6,2},{1... | collective-permute-start | bytes 1474568 | tf_op jit(solution)/shard_map/ppermute | solution.py:352
  3.0 11.4 %collective-permute-start.1 = (bf16[192,1280]{1,0:T(8,128)(2,1)}, bf16[192,1280]{1,0:T(8,128)(2,1)S(1)}, u32[]{:S(2)}, u32[]{:S(2)}) collective-permute-start(bf16[192,1280]{1,0:T(8,128)(2,1)} %refs_0_.1), channel_id=1, source_target_pairs={{4,8},{8,4},{5,9},{9,5},{6,10},{10,6},{7,11},{11,7},{20,24},{24,20... | collective-permute-start | bytes 1474568 | tf_op jit(solution)/shard_map/ppermute | solution.py:352
  14.5 2.7 %collective-permute-start.6 = (bf16[192,1280]{1,0:T(8,128)(2,1)S(1)}, bf16[192,1280]{1,0:T(8,128)(2,1)}, u32[]{:S(2)}, u32[]{:S(2)}) collective-permute-start(bf16[192,1280]{1,0:T(8,128)(2,1)S(1)} %get-tuple-element.19.refs_0_), channel_id=1, source_target_pairs={{4,8},{8,4},{5,9},{9,5},{6,10},{10,6},{7,11},{11,7},{20,24},{24,20... | collective-permute-start | bytes 1474568 | tf_op jit(solution)/shard_map/ppermute | solution.py:352
  15.9 34.2 %collective-permute-start.3 = (bf16[192,1280]{1,0:T(8,128)(2,1)S(1)}, bf16[192,1280]{1,0:T(8,128)(2,1)}, u32[]{:S(2)}, u32[]{:S(2)}) collective-permute-start(bf16[192,1280]{1,0:T(8,128)(2,1)S(1)} %get-tuple-element.20.refs_0_), channel_id=1, source_target_pairs={{4,0},{8,12},{5,1},{9,13},{6,2},{10,14},{7,3},{11,15},{20,16},{24,... | collective-permute-start | bytes 1474568 | tf_op jit(solution)/shard_map/ppermute | solution.py:352
  17.2 34.3 %collective-permute-start.7 = (bf16[192,1280]{1,0:T(8,128)(2,1)}, bf16[192,1280]{1,0:T(8,128)(2,1)}, u32[]{:S(2)}, u32[]{:S(2)}) collective-permute-start(bf16[192,1280]{1,0:T(8,128)(2,1)} %collective-permute-done.6.refs_0_), channel_id=1, source_target_pairs={{4,0},{8,12},{5,1},{9,13},{6,2},{10,14},{7,3},{11,15},{20,16},{24,... | collective-permute-start | bytes 1474568 | tf_op jit(solution)/shard_map/ppermute | solution.py:352
  18.5 19.7 %collective-permute-start.4 = (f32[64,192]{1,0:T(8,128)}, f32[64,192]{1,0:T(8,128)S(1)}, u32[]{:S(2)}, u32[]{:S(2)}) collective-permute-start(f32[64,192]{1,0:T(8,128)} %route.1.refs_1_.refs_4_), channel_id=1, source_target_pairs={{0,12},{4,8},{8,4},{12,0},{1,13},{5,9},{9,5},{13,1},{2,14},{6,10},... | collective-permute-start | bytes 147464 | tf_op jit(solution)/shard_map/ppermute | solution.py:352
  22.3 19.4 %collective-permute-start.5 = (f32[64,192]{1,0:T(8,128)}, f32[64,192]{1,0:T(8,128)S(1)}, u32[]{:S(2)}, u32[]{:S(2)}) collective-permute-start(f32[64,192]{1,0:T(8,128)} %route.1.refs_1_.refs_4_), channel_id=1, source_target_pairs={{0,8},{4,12},{8,0},{12,4},{1,9},{5,13},{9,1},{13,5},{2,10},{6,14},... | collective-permute-start | bytes 147464 | tf_op jit(solution)/shard_map/ppermute | solution.py:352
  38.2 10.9 %collective-permute-start.2 = (f32[64,192]{1,0:T(8,128)}, f32[64,192]{1,0:T(8,128)S(1)}, u32[]{:S(2)}, u32[]{:S(2)}) collective-permute-start(f32[64,192]{1,0:T(8,128)} %route.1.refs_1_.refs_4_), channel_id=1, source_target_pairs={{0,4},{4,0},{8,12},{12,8},{1,5},{5,1},{9,13},{13,9},{2,6},{6,2},{1... | collective-permute-start | bytes 147464 | tf_op jit(solution)/shard_map/ppermute | solution.py:352
  59.7 2.4 %collective-permute-start.8 = (bf16[2,512,384]{2,1,0:T(8,128)(2,1)S(1)}, bf16[2,512,384]{2,1,0:T(8,128)(2,1)S(1)}, u32[]{:S(2)}, u32[]{:S(2)}) collective-permute-start(bf16[2,512,384]{2,1,0:T(8,128)(2,1)S(1)} %get-tuple-element.22), channel_id=1, source_target_pairs={{0,1},{1,0},{2,3},{3,2},{4,5},{5,4},{6,7},{7,6},{8,9},{9,8},{10,11... | collective-permute-start | bytes 2359304 | tf_op jit(solution)/shard_map/ppermute | solution.py:374
  63.8 13.9 %collective-permute-start.10 = (bf16[512,384]{1,0:T(8,128)(2,1)S(1)}, bf16[512,384]{1,0:T(8,128)(2,1)}, u32[]{:S(2)}, u32[]{:S(2)}) collective-permute-start(bf16[512,384]{1,0:T(8,128)(2,1)S(1)} %chip_sum.3.refs_5_), channel_id=1, source_target_pairs={{0,2},{1,3},{2,0},{3,1},{4,6},{5,7},{6,4},{7,5},{8,10},{9,11},{10,... | collective-permute-start | bytes 1179656 | tf_op jit(solution)/shard_map/ppermute | solution.py:378
  66.6 11.2 %copy-start.4 = (bf16[2,512,384]{2,1,0:T(8,128)(2,1)S(1)}, bf16[2,512,384]{2,1,0:T(8,128)(2,1)}, u32[]{:S(2)}) copy-start(bf16[2,512,384]{2,1,0:T(8,128)(2,1)} %copy-done.3) | copy-start | bytes 2359300
  66.6 11.2 %copy-start.10 = (bf16[2,512,384]{2,1,0:T(8,128)(2,1)S(1)}, bf16[2,512,384]{2,1,0:T(8,128)(2,1)}, u32[]{:S(2)}) copy-start(bf16[2,512,384]{2,1,0:T(8,128)(2,1)} %copy-done.9) | copy-start | bytes 2359300
  77.7 3.5 %collective-permute-start.9 = (bf16[2,512,768]{2,1,0:T(8,128)(2,1)S(1)}, bf16[2,512,768]{2,1,0:T(8,128)(2,1)S(1)}, u32[]{:S(2)}, u32[]{:S(2)}) collective-permute-start(bf16[2,512,768]{2,1,0:T(8,128)(2,1)S(1)} %get-tuple-element.24), channel_id=1, source_target_pairs={{0,1},{1,0},{2,3},{3,2},{4,5},{5,4},{6,7},{7,6},{8,9},{9,8},{10,11... | collective-permute-start | bytes 4718600 | tf_op jit(solution)/shard_map/ppermute | solution.py:374
  82.6 20.7 %collective-permute-start.12 = (bf16[512,768]{1,0:T(8,128)(2,1)}, bf16[512,768]{1,0:T(8,128)(2,1)}, u32[]{:S(2)}, u32[]{:S(2)}) collective-permute-start(bf16[512,768]{1,0:T(8,128)(2,1)} %chip_sum.4.refs_5_), channel_id=1, source_target_pairs={{0,2},{1,3},{2,0},{3,1},{4,6},{5,7},{6,4},{7,5},{8,10},{9,11},{10,... | collective-permute-start | bytes 2359304 | tf_op jit(solution)/shard_map/ppermute | solution.py:378
  83.2 23.4 %collective-permute-start.14 = (bf16[384,256]{1,0:T(8,128)(2,1)S(1)}, bf16[384,256]{1,0:T(8,128)(2,1)S(1)}, u32[]{:S(2)}, u32[]{:S(2)}) collective-permute-start(bf16[384,256]{1,0:T(8,128)(2,1)S(1)} %hidden.3._.refs_0_), channel_id=1, source_target_pairs={{0,2},{1,3},{2,0},{3,1},{4,6},{5,7},{6,4},{7,5},{8,10},{9,11},{10,... | collective-permute-start | bytes 589832 | tf_op jit(solution)/shard_map/ppermute | solution.py:381
  85.9 17.4 %copy-start.6 = (bf16[2,512,768]{2,1,0:T(8,128)(2,1)S(1)}, bf16[2,512,768]{2,1,0:T(8,128)(2,1)}, u32[]{:S(2)}) copy-start(bf16[2,512,768]{2,1,0:T(8,128)(2,1)} %copy-done.5) | copy-start | bytes 4718596
  85.9 17.4 %copy-start.8 = (bf16[2,512,768]{2,1,0:T(8,128)(2,1)S(1)}, bf16[2,512,768]{2,1,0:T(8,128)(2,1)}, u32[]{:S(2)}) copy-start(bf16[2,512,768]{2,1,0:T(8,128)(2,1)} %copy-done.7) | copy-start | bytes 4718596
  92.2 13.1 %collective-permute-start.11 = (bf16[2,512,384]{2,1,0:T(8,128)(2,1)S(1)}, bf16[2,512,384]{2,1,0:T(8,128)(2,1)S(1)}, u32[]{:S(2)}, u32[]{:S(2)}) collective-permute-start(bf16[2,512,384]{2,1,0:T(8,128)(2,1)S(1)} %get-tuple-element.26), channel_id=1, source_target_pairs={{0,1},{1,0},{2,3},{3,2},{4,5},{5,4},{6,7},{7,6},{8,9},{9,8},{10,11... | collective-permute-start | bytes 2359304 | tf_op jit(solution)/shard_map/ppermute | solution.py:374
  105.4 12.1 %collective-permute-start.13 = (bf16[512,384]{1,0:T(8,128)(2,1)S(1)}, bf16[512,384]{1,0:T(8,128)(2,1)S(1)}, u32[]{:S(2)}, u32[]{:S(2)}) collective-permute-start(bf16[512,384]{1,0:T(8,128)(2,1)S(1)} %chip_sum.5.refs_9_), channel_id=1, source_target_pairs={{0,2},{1,3},{2,0},{3,1},{4,6},{5,7},{6,4},{7,5},{8,10},{9,11},{10,... | collective-permute-start | bytes 1179656 | tf_op jit(solution)/shard_map/ppermute | solution.py:378
  106.0 2.0 %collective-permute-start.15 = (bf16[384,256]{1,0:T(8,128)(2,1)S(1)}, bf16[384,256]{1,0:T(8,128)(2,1)S(1)}, u32[]{:S(2)}, u32[]{:S(2)}) collective-permute-start(bf16[384,256]{1,0:T(8,128)(2,1)S(1)} %hidden.3._.refs_0_), channel_id=1, source_target_pairs={{0,1},{1,0},{2,3},{3,2},{4,5},{5,4},{6,7},{7,6},{8,9},{9,8},{10,11... | collective-permute-start | bytes 589832 | tf_op jit(solution)/shard_map/ppermute | solution.py:382
  106.6 1.5 collective-permute-start.16
  106.6 16.9 %collective-permute-start.20 = (bf16[768,256]{1,0:T(8,128)(2,1)S(1)}, bf16[768,256]{1,0:T(8,128)(2,1)S(1)}, u32[]{:S(2)}, u32[]{:S(2)}) collective-permute-start(bf16[768,256]{1,0:T(8,128)(2,1)S(1)} %hidden.4._.__1_.refs_0_), channel_id=1, source_target_pairs={{0,2},{1,3},{2,0},{3,1},{4,6},{5,7},{6,4},{7,5},{8,10},{9,11},{10,... | collective-permute-start | bytes 1179656 | tf_op jit(solution)/shard_map/ppermute | solution.py:381
  108.0 22.7 %collective-permute-start.21 = (bf16[768,256]{1,0:T(8,128)(2,1)S(1)}, bf16[768,256]{1,0:T(8,128)(2,1)S(1)}, u32[]{:S(2)}, u32[]{:S(2)}) collective-permute-start(bf16[768,256]{1,0:T(8,128)(2,1)S(1)} %hidden.4._.__1_.refs_0_), channel_id=1, source_target_pairs={{0,1},{1,0},{2,3},{3,2},{4,5},{5,4},{6,7},{7,6},{8,9},{9,8},{10,11... | collective-permute-start | bytes 1179656 | tf_op jit(solution)/shard_map/ppermute | solution.py:382
  123.5 7.3 %collective-permute-start.22 = (bf16[768,256]{1,0:T(8,128)(2,1)S(1)}, bf16[768,256]{1,0:T(8,128)(2,1)S(1)}, u32[]{:S(2)}, u32[]{:S(2)}) collective-permute-start(bf16[768,256]{1,0:T(8,128)(2,1)S(1)} %hold.5.refs_1_), channel_id=1, source_target_pairs={{0,1},{1,0},{2,3},{3,2},{4,5},{5,4},{6,7},{7,6},{8,9},{9,8},{10,11... | collective-permute-start | bytes 1179656 | tf_op jit(solution)/shard_map/ppermute | solution.py:385
  123.5 7.3 %collective-permute-start.17 = (bf16[384,256]{1,0:T(8,128)(2,1)S(1)}, bf16[384,256]{1,0:T(8,128)(2,1)S(1)}, u32[]{:S(2)}, u32[]{:S(2)}) collective-permute-start(bf16[384,256]{1,0:T(8,128)(2,1)S(1)} %hidden.5.__1_.refs_9_.refs_0_), channel_id=1, source_target_pairs={{0,2},{1,3},{2,0},{3,1},{4,6},{5,7},{6,4},{7,5},{8,10},{9,11},{10,... | collective-permute-start | bytes 589832 | tf_op jit(solution)/shard_map/ppermute | solution.py:381
  124.0 13.5 %collective-permute-start.18 = (bf16[384,256]{1,0:T(8,128)(2,1)S(1)}, bf16[384,256]{1,0:T(8,128)(2,1)S(1)}, u32[]{:S(2)}, u32[]{:S(2)}) collective-permute-start(bf16[384,256]{1,0:T(8,128)(2,1)S(1)} %hidden.5.__1_.refs_9_.refs_0_), channel_id=1, source_target_pairs={{0,1},{1,0},{2,3},{3,2},{4,5},{5,4},{6,7},{7,6},{8,9},{9,8},{10,11... | collective-permute-start | bytes 589832 | tf_op jit(solution)/shard_map/ppermute | solution.py:382
  130.8 6.7 %collective-permute-start.19 = (bf16[384,256]{1,0:T(8,128)(2,1)S(1)}, bf16[384,256]{1,0:T(8,128)(2,1)S(1)}, u32[]{:S(2)}, u32[]{:S(2)}) collective-permute-start(bf16[384,256]{1,0:T(8,128)(2,1)S(1)} %collective-permute-done.17.refs_1_), channel_id=1, source_target_pairs={{0,1},{1,0},{2,3},{3,2},{4,5},{5,4},{6,7},{7,6},{8,9},{9,8},{10,11... | collective-permute-start | bytes 589832 | tf_op jit(solution)/shard_map/ppermute | solution.py:385
  142.3 12.7 %collective-permute-start.23 = (bf16[192,1280]{1,0:T(8,128)(2,1)S(1)}, bf16[192,1280]{1,0:T(8,128)(2,1)S(1)}, u32[]{:S(2)}, u32[]{:S(2)}) collective-permute-start(bf16[192,1280]{1,0:T(8,128)(2,1)S(1)} %get-tuple-element.28.a_ref), channel_id=1, source_target_pairs={{0,4},{12,8},{1,5},{13,9},{2,6},{14,10},{3,7},{15,11},{16,20},{28,... | collective-permute-start | bytes 1474568 | tf_op jit(solution)/shard_map/ppermute | solution.py:352
  155.1 14.8 %collective-permute-start.24 = (bf16[192,1280]{1,0:T(8,128)(2,1)S(1)}, bf16[192,1280]{1,0:T(8,128)(2,1)S(1)}, u32[]{:S(2)}, u32[]{:S(2)}) collective-permute-start(bf16[192,1280]{1,0:T(8,128)(2,1)S(1)} %get-tuple-element.30), channel_id=1, source_target_pairs={{0,4},{12,8},{1,5},{13,9},{2,6},{14,10},{3,7},{15,11},{16,20},{28,... | collective-permute-start | bytes 1474568 | tf_op jit(solution)/shard_map/ppermute | solution.py:352
  159.5 11.2 %collective-permute-start.26 = (bf16[192,1280]{1,0:T(8,128)(2,1)S(1)}, bf16[192,1280]{1,0:T(8,128)(2,1)S(1)}, u32[]{:S(2)}, u32[]{:S(2)}) collective-permute-start(bf16[192,1280]{1,0:T(8,128)(2,1)S(1)} %get-tuple-element.32), channel_id=1, source_target_pairs={{4,8},{8,4},{5,9},{9,5},{6,10},{10,6},{7,11},{11,7},{20,24},{24,20... | collective-permute-start | bytes 1474568 | tf_op jit(solution)/shard_map/ppermute | solution.py:352
  170.0 5.7 %collective-permute-start.25 = (bf16[192,1280]{1,0:T(8,128)(2,1)S(1)}, bf16[192,1280]{1,0:T(8,128)(2,1)S(1)}, u32[]{:S(2)}, u32[]{:S(2)}) collective-permute-start(bf16[192,1280]{1,0:T(8,128)(2,1)S(1)} %add_convert_fusion.2), channel_id=1, source_target_pairs={{4,8},{8,4},{5,9},{9,5},{6,10},{10,6},{7,11},{11,7},{20,24},{24,20... | collective-permute-start | bytes 1474568 | tf_op jit(solution)/shard_map/ppermute | solution.py:352
  170.8 14.8 %collective-permute-start.27 = (bf16[192,1280]{1,0:T(8,128)(2,1)S(1)}, bf16[192,1280]{1,0:T(8,128)(2,1)S(1)}, u32[]{:S(2)}, u32[]{:S(2)}) collective-permute-start(bf16[192,1280]{1,0:T(8,128)(2,1)S(1)} %add_convert_fusion.1), channel_id=1, source_target_pairs={{0,4},{4,0},{8,12},{12,8},{1,5},{5,1},{9,13},{13,9},{2,6},{6,2},{1... | collective-permute-start | bytes 1474568 | tf_op jit(solution)/shard_map/ppermute | solution.py:352
  (13 other events, 46.0 us)

commit v4 on v0

--- a/solution.py
+++ b/solution.py
@@ -59,34 +59,79 @@
     )(expert_ids.T, gate_weights.T.astype(F32))
 
 
+EXTRA = 16
+
+
+def pack_kernel(tokens_ref, extra_ref, out_ref):
+    count, lanes = tokens_ref.shape[0], extra_ref.shape[1]
+    out_ref[:count, :] = tokens_ref[...]
+    out_ref[count:, lanes:] = jnp.zeros((EXTRA, out_ref.shape[1] - lanes), BF16)
+    out_ref[count:, :lanes] = extra_ref[...]
+
+
+def pack(tokens, expert_ids, gate_weights):
+    count, width = tokens.shape
+    spare = -count % LANES
+    extra = [
+        jnp.pad(a.T.astype(BF16), ((0, EXTRA - TOPK), (0, spare)))
+        for a in (expert_ids, gate_weights)
+    ]
+    return pl.pallas_call(
+        pack_kernel,
+        out_shape=jax.ShapeDtypeStruct((count + EXTRA, width), BF16),
+        compiler_params=params(8),
+        cost_estimate=QUICK,
+        name="pack",
+    )(tokens, jnp.concatenate(extra, axis=1))
+
+
 def place_kernel(experts, where_ref, *refs):
-    *token_refs, table_ref, out_ref = refs
+    *message_refs, out_ref, table_ref = refs
     count = table_ref.shape[1]
+    lanes = count + -count % LANES
+    message = message_refs[0][...]
+    for more in message_refs[1:]:
+        message = message + more[...]
+    ids = message[count:, :count].astype(F32)
+    gates = message[count:, lanes : lanes + count].astype(F32)
+    expert = lax.broadcasted_iota(jnp.int32, (experts, count), 0) + where_ref[0]
+    expert = expert.astype(F32)
+    weight = jnp.zeros((experts, count), F32)
+    chosen = jnp.zeros((experts, count), F32)
+    for k in range(TOPK):
+        hit = ids[k : k + 1, :] == expert
+        chosen = jnp.where(hit, 1.0, chosen)
+        weight = jnp.where(hit, gates[k : k + 1, :], weight)
+    first = lax.broadcasted_iota(jnp.int32, (count, count), 0)
+    second = lax.broadcasted_iota(jnp.int32, (count, count), 1)
+    before = jnp.where(first < second, 1.0, 0.0).astype(BF16)
+    position = lax.dot_general(chosen.astype(BF16), before, NN, preferred_element_type=F32)
+    position = jnp.where(chosen > 0.0, position, -1.0)
+    table_ref[:experts, :] = position
+    table_ref[experts:, :] = weight
     slot_of = lax.broadcasted_iota(jnp.int32, (CAP, count), 0).astype(F32)
-    table = [
-        jnp.where(table_ref[pl.ds(where_ref[0] + e, 1), :] == slot_of, 1.0, 0.0)
-        for e in range(experts)
-    ]
-    tokens = token_refs[0][...]
-    for extra in token_refs[1:]:
-        tokens = tokens + extra[...]
+    table = [jnp.where(position[e : e + 1, :] == slot_of, 1.0, 0.0) for e in range(experts)]
     table = jnp.concatenate(table, axis=0).astype(BF16)
-    rows = lax.dot_general(table, tokens, NN, preferred_element_type=F32).astype(BF16)
+    rows = lax.dot_general(table, message[:count], NN, preferred_element_type=F32).astype(BF16)
     for e in range(experts):
         out_ref[e] = rows[e * CAP : (e + 1) * CAP]
 
 
-def place(where, tokens, table, experts):
+def place(where, messages, experts):
     whole = pl.BlockSpec(memory_space=pltpu.VMEM)
+    length, width = messages[0].shape
     return pl.pallas_call(
         functools.partial(place_kernel, experts),
-        out_shape=jax.ShapeDtypeStruct((experts, CAP, tokens[0].shape[1]), BF16),
-        in_specs=[pl.BlockSpec(memory_space=pltpu.SMEM)] + [whole] * (len(tokens) + 1),
-        out_specs=whole,
-        compiler_params=params(24),
+        out_shape=(
+            jax.ShapeDtypeStruct((experts, CAP, width), BF16),
+            jax.ShapeDtypeStruct((2 * experts, length - EXTRA), F32),
+        ),
+        in_specs=[pl.BlockSpec(memory_space=pltpu.SMEM)] + [whole] * len(messages),
+        out_specs=(whole, whole),
+        compiler_params=params(12),
         cost_estimate=QUICK,
         name="place",
-    )(where, *tokens, table)
+    )(where, *messages)
 
 
 def gate_up_kernel(n_blocks, where_ref, *refs):
@@ -155,7 +200,7 @@
             pltpu.VMEM((2, 2 * LANES, width), BF16),
             pltpu.VMEM((2 * units, LANES), F32),
         ],
-        compiler_params=params(48),
+        compiler_params=params(28),
         cost_estimate=QUICK,
         name="gate_up",
     )(where, *placed, gu_weight, after)
@@ -187,7 +232,7 @@
         ],
         out_specs=pl.BlockSpec((columns, doubled // 2), lambda i: (0, 0)),
         scratch_shapes=[pltpu.VMEM((columns // LANES, doubled, LANES), F32)],
-        compiler_params=params(24),
+        compiler_params=params(10),
         cost_estimate=SLOW,
         name="hidden",
     )(keep, near, far, after)
@@ -206,7 +251,7 @@
         out_shape=jax.ShapeDtypeStruct((doubled, columns), BF16),
         in_specs=[other, other, pl.BlockSpec(memory_space=pl.ANY)],
         out_specs=pl.BlockSpec((doubled, columns), lambda i: (0, 0)),
-        compiler_params=params(24),
+        compiler_params=params(8),
         cost_estimate=QUICK,
         name="chip_sum",
     )(keep, near, after)
@@ -221,7 +266,7 @@
     rows = n_blocks * CAP
     quarter = w_hbm.shape[1] // 4
     count = route_refs[0].shape[1]
-    expert0 = where_ref[0]
+    local = w_hbm.shape[0]
     x, core = where_ref[1], where_ref[2]
     order = [(x, core), (1 - x, core), (x, 1 - core), (1 - x, 1 - core)]
 
@@ -257,8 +302,8 @@
     for i in range(n_blocks):
         table = [
             jnp.where(
-                route_refs[i][pl.ds(expert0 + e, 1), :] == slot_of,
-                route_refs[i][pl.ds(EXPERTS + expert0 + e, 1), :],
+                route_refs[i][chunk * group + e : chunk * group + e + 1, :] == slot_of,
+                route_refs[i][local + chunk * group + e : local + chunk * group + e + 1, :],
                 0.0,
             )
             for e in range(group)
@@ -295,7 +340,7 @@
             pltpu.VMEM((group, 4 * units, width), BF16),
             pltpu.SemaphoreType.DMA((group, 4)),
         ],
-        compiler_params=params(40),
+        compiler_params=params(28),
         cost_estimate=QUICK,
         name="down",
     )(where, *hidden, *routes, down_weight, after, *carried)
@@ -314,7 +359,7 @@
         in_specs=[whole, whole, free],
         out_specs=(whole, free),
         input_output_aliases={2: 1},
-        compiler_params=params(16),
+        compiler_params=params(4),
         cost_estimate=QUICK,
         name="plus",
     )(a, b, other)
@@ -325,30 +370,22 @@
     x, core = t // 2, t % 2
     local = gu_weight.shape[0]
     group = local // 2
-    wheres = [jnp.stack([z * local + n * group, x, core]).astype(jnp.int32) for n in range(2)]
+    where = jnp.stack([z * local, x, core]).astype(jnp.int32)
 
     def hop(array, pairs):
         return lax.ppermute(array, "ep", pairs)
 
-    table = route(expert_ids, gate_weights)
-    neighbour = hop(tokens, PAIR)
-    table_1 = hop(table, PAIR)
-    middle_1 = hop(tokens, MIDDLE)
-    table_2 = hop(table, [(i, i ^ 2) for i in range(4)])
-    table_3 = hop(table, [(i, i ^ 3) for i in range(4)])
-    inner = (z == 1) | (z == 2)
-    table_in = jnp.where(inner, table_3, table_2)
-    table_out = jnp.where(inner, table_2, table_3)
+    message = pack(tokens, expert_ids, gate_weights)
+    neighbour = hop(message, PAIR)
+    middle_1 = hop(message, MIDDLE)
     middle_2 = hop(neighbour, MIDDLE)
     end_1 = hop(middle_1, OUTWARD)
     end_2 = hop(middle_2, OUTWARD)
-
-    tables = [table, table_1, table_in, table_out]
-    blocks = [(tokens,), (neighbour,), (middle_1, end_1), (middle_2, end_2)]
-    placed = [place(wheres[0], b, t, local) for b, t in zip(blocks, tables)]
+    blocks = [(message,), (neighbour,), (middle_1, end_1), (middle_2, end_2)]
+    placed, tables = zip(*(place(where, b, local) for b in blocks))
 
     def sums(n, after):
-        send, keep = gate_up(wheres[n], placed, gu_weight, n, group, after)
+        send, keep = gate_up(where, placed, gu_weight, n, group, after)
         return keep, lax.ppermute(send, "tp", ACROSS_CORE)
 
     def across(keep, near, after):
@@ -366,11 +403,11 @@
     own_0 = hidden_quarter(keep_0, near_0, far_0, keep_1)
     hidden_0 = gathered(own_0)
     turn, far_1 = across(keep_1, near_1, own_0)
-    (carry,) = down(wheres[0], hidden_0, tables, down_weight, 0, group, None, turn)
+    (carry,) = down(where, hidden_0, tables, down_weight, 0, group, None, turn)
     own_1 = hidden_quarter(keep_1, near_1, far_1, carry)
     hidden_1 = gathered(own_1)
     own, other, far_in, far_out = down(
-        wheres[1], hidden_1, tables, down_weight, 1, group, carry, own_1
+        where, hidden_1, tables, down_weight, 1, group, carry, own_1
     )
 
     def plus(a, b):

time: 183 us -> 172 us (0.940)
  waiting for transfers between devices: 73.4 us -> 92.8 us
  starting transfers between devices: 47.4 us -> 31.6 us
  local copies, waits for them, and re-layouts: 8.31 us -> 1.03 us
  Pallas kernels: 47.9 us -> 41.1 us
    ppermute x13 -> x10, waiting for transfers between devices: 37.4 us -> 54.4 us  [hop(): return lax.ppermute(array, 'ep', pairs)]
    ppermute x13 -> x10, starting transfers between devices: 42.2 us -> 26.2 us  [hop(): return lax.ppermute(array, 'ep', pairs)]
    unnamed x30 -> x2, local copies, waits for them, and re-layouts: 8.31 us -> 1.03 us
    pallas_call x2, Pallas kernels: 24.7 us -> 22.1 us  [gate_up(): pl.pallas_call(functools.partial(gate_up_kernel, n_blocks), grid=(group,)...]
    ppermute x2, waiting for transfers between devices: 11.5 us -> 13.9 us  [across(): return (total, lax.ppermute(total, 'tp', ACROSS_X))]
    pallas_call x5, Pallas kernels: 6.66 us -> 4.39 us  [the longest x4 4.36 us: place(): pl.pallas_call(functools.partial(place_kernel, experts), out_shape=(jax.S...]
  transfers between devices with their start and end apart: 23 -> 20, of which waited for: 13 -> 13; matrix products, arithmetic and copies ran while one was open for 1% -> 0% of each run, Pallas kernels for 14% -> 13%
where the time goes in v4:
time: 172 us; the launch traced here: 169 us
  waiting for transfers between devices  92.8 us (54%)
  Pallas kernels  41.1 us (24%)
  starting transfers between devices  31.6 us (18%)
  other arithmetic  2.67 us (2%)
    ppermute x10, waiting for transfers between devices, hop(): return lax.ppermute(array, 'ep', pairs)  54.4 us
    ppermute x10, starting transfers between devices, hop(): return lax.ppermute(array, 'ep', pairs)  26.2 us
    pallas_call x2, Pallas kernels, gate_up(): pl.pallas_call(functools.partial(gate_up_kernel, n_blocks), grid=(group,)...  22.1 us
    ppermute x2, waiting for transfers between devices, gathered(): own_x = lax.ppermute(own, 'tp', ACROSS_X)  17.7 us
    ppermute x2, waiting for transfers between devices, across(): return (total, lax.ppermute(total, 'tp', ACROSS_X))  13.9 us
    pallas_call x2, Pallas kernels, down(): pl.pallas_call(functools.partial(down_kernel, group, n_blocks, chunk, car...  12.7 us
    pallas_call x4, Pallas kernels, place(): pl.pallas_call(functools.partial(place_kernel, experts), out_shape=(jax.S...  4.36 us
  transfers between devices with their start and end apart: 20, of which 13 were waited for; matrix products, arithmetic and copies ran while one was open for 0% of the time, Pallas kernels for 13%

profile of v4, /device:TPU:0, one launch (start us, length us, event | category | flops | bytes accessed | tf_op | source)
XLA Modules:
  0.0 169.5 jit_solution(14317961656689238536)
XLA Ops:
  1.4 1.0 copy-done
  2.5 3.1 %collective-permute-start = (bf16[208,1280]{1,0:T(8,128)(2,1)S(1)}, bf16[208,1280]{1,0:T(8,128)(2,1)S(1)}, u32[]{:S(2)}, u32[]{:S(2)}) collective-permute-start(bf16[208,1280]{1,0:T(8,128)(2,1)S(1)} %pack.1.refs_0_), channel_id=1, source_target_pairs={{0,4},{4,0},{8,12},{12,8},{1,5},{5,1},{9,13},{13,9},{2,6},{6,2},{1... | collective-permute-start | bytes 1597448 | tf_op jit(solution)/shard_map/ppermute | solution.py:376
  6.2 11.4 %collective-permute-done.refs_0_ = bf16[208,1280]{1,0:T(8,128)(2,1)S(1)} collective-permute-done((bf16[208,1280]{1,0:T(8,128)(2,1)S(1)}, bf16[208,1280]{1,0:T(8,128)(2,1)S(1)}, u32[]{:S(2)}, u32[]{:S(2)}) %collective-permute-start) | collective-permute-done | bytes 532512 | tf_op jit(solution)/shard_map/ppermute | solution.py:376
  18.4 1.3 collective-permute-start.2
  19.7 1.3 collective-permute-start.4
  21.1 1.1 place.4
  22.1 1.1 place.5
  23.2 12.5 %collective-permute-done.2.refs_1_ = bf16[208,1280]{1,0:T(8,128)(2,1)S(1)} collective-permute-done((bf16[208,1280]{1,0:T(8,128)(2,1)S(1)}, bf16[208,1280]{1,0:T(8,128)(2,1)S(1)}, u32[]{:S(2)}, u32[]{:S(2)}) %collective-permute-start.2) | collective-permute-done | bytes 532512 | tf_op jit(solution)/shard_map/ppermute | solution.py:376
  35.7 1.1 place.6
  36.8 9.7 %collective-permute-done.4.refs_1_ = bf16[208,1280]{1,0:T(8,128)(2,1)S(1)} collective-permute-done((bf16[208,1280]{1,0:T(8,128)(2,1)S(1)}, bf16[208,1280]{1,0:T(8,128)(2,1)S(1)}, u32[]{:S(2)}, u32[]{:S(2)}) %collective-permute-start.4) | collective-permute-done | bytes 532512 | tf_op jit(solution)/shard_map/ppermute | solution.py:376
  46.5 1.1 place.7
  47.6 11.0 %gate_up.2 = (bf16[2,512,768]{2,1,0:T(8,128)(2,1)S(1)}, bf16[2,512,768]{2,1,0:T(8,128)(2,1)S(1)}) custom-call(s32[3]{0:T(128)S(1)} %pad_add_fusion.where_ref, bf16[8,48,1280]{2,1,0:T(8,128)(2,1)S(1)} %get-tuple-element.23.refs_0_, bf16[8,48,1280]{2,1,0:T(8,128)(2,1)S(1)} %get-tuple-element.24.refs_1_, bf16[8,48,1280]{2,1,0:T(8,128)(2,1)S(1)} %get-tuple-element.25.refs_2_, ...), custom_call_target="tpu_custom_call" | custom-call | flops 1024 | bytes 1024 | tf_op jit(solution)/shard_map/gate_up/pallas_call | solution.py:190
  58.7 3.4 %collective-permute-done.5.near_ref = bf16[2,512,768]{2,1,0:T(8,128)(2,1)S(1)} collective-permute-done((bf16[2,512,768]{2,1,0:T(8,128)(2,1)S(1)}, bf16[2,512,768]{2,1,0:T(8,128)(2,1)S(1)}, u32[]{:S(2)}, u32[]{:S(2)}) %collective-permute-start.5) | collective-permute-done | bytes 1572896 | tf_op jit(solution)/shard_map/ppermute | solution.py:389
  62.3 1.6 collective-permute-start.7
  63.8 11.1 %gate_up.3 = (bf16[2,512,768]{2,1,0:T(8,128)(2,1)S(1)}, bf16[2,512,768]{2,1,0:T(8,128)(2,1)S(1)}) custom-call(s32[3]{0:T(128)S(1)} %pad_add_fusion.where_ref, bf16[8,48,1280]{2,1,0:T(8,128)(2,1)S(1)} %get-tuple-element.23.refs_0_, bf16[8,48,1280]{2,1,0:T(8,128)(2,1)S(1)} %get-tuple-element.24.refs_1_, bf16[8,48,1280]{2,1,0:T(8,128)(2,1)S(1)} %get-tuple-element.25.refs_2_, ...), custom_call_target="tpu_custom_call" | custom-call | flops 1024 | bytes 1024 | tf_op jit(solution)/shard_map/gate_up/pallas_call | solution.py:190
  75.0 6.9 %collective-permute-done.7.far_ref = bf16[512,768]{1,0:T(8,128)(2,1)S(1)} collective-permute-done((bf16[512,768]{1,0:T(8,128)(2,1)S(1)}, bf16[512,768]{1,0:T(8,128)(2,1)S(1)}, u32[]{:S(2)}, u32[]{:S(2)}) %collective-permute-start.7) | collective-permute-done | bytes 786464 | tf_op jit(solution)/shard_map/ppermute | solution.py:393
  82.6 1.6 collective-permute-start.9
  85.0 9.8 %collective-permute-done.9.refs_1_ = bf16[768,256]{1,0:T(8,128)(2,1)S(1)} collective-permute-done((bf16[768,256]{1,0:T(8,128)(2,1)S(1)}, bf16[768,256]{1,0:T(8,128)(2,1)S(1)}, u32[]{:S(2)}, u32[]{:S(2)}) %collective-permute-start.9) | collective-permute-done | bytes 393248 | tf_op jit(solution)/shard_map/ppermute | solution.py:396
  94.7 1.7 %collective-permute-done.11.refs_3_ = bf16[768,256]{1,0:T(8,128)(2,1)S(1)} collective-permute-done((bf16[768,256]{1,0:T(8,128)(2,1)S(1)}, bf16[768,256]{1,0:T(8,128)(2,1)S(1)}, u32[]{:S(2)}, u32[]{:S(2)}) %collective-permute-start.11) | collective-permute-done | bytes 393248 | tf_op jit(solution)/shard_map/ppermute | solution.py:398
  96.5 6.3 %down.2._.refs_10_ = f32[4,192,1280]{2,1,0:T(8,128)S(1)} custom-call(s32[3]{0:T(128)S(1)} %pad_add_fusion.where_ref, bf16[768,256]{1,0:T(8,128)(2,1)S(1)} %hidden.2._.refs_0_, bf16[768,256]{1,0:T(8,128)(2,1)S(1)} %collective-permute-done.9.refs_1_, bf16[768,256]{1,0:T(8,128)(2,1)S(1)} %collective-permute-done.10.refs_2_, ...), custom_call_target="tpu_custom_call" | custom-call | flops 1024 | bytes 1024 | tf_op jit(solution)/shard_map/down/pallas_call | solution.py:330
  102.8 7.1 %collective-permute-done.8.far_ref = bf16[512,768]{1,0:T(8,128)(2,1)S(1)} collective-permute-done((bf16[512,768]{1,0:T(8,128)(2,1)S(1)}, bf16[512,768]{1,0:T(8,128)(2,1)S(1)}, u32[]{:S(2)}, u32[]{:S(2)}) %collective-permute-start.8) | collective-permute-done | bytes 786464 | tf_op jit(solution)/shard_map/ppermute | solution.py:393
  110.6 1.6 collective-permute-start.12
  112.1 7.9 %collective-permute-done.12.refs_1_ = bf16[768,256]{1,0:T(8,128)(2,1)S(1)} collective-permute-done((bf16[768,256]{1,0:T(8,128)(2,1)S(1)}, bf16[768,256]{1,0:T(8,128)(2,1)S(1)}, u32[]{:S(2)}, u32[]{:S(2)}) %collective-permute-start.12) | collective-permute-done | bytes 393248 | tf_op jit(solution)/shard_map/ppermute | solution.py:396
  120.0 1.7 %collective-permute-done.14.refs_3_ = bf16[768,256]{1,0:T(8,128)(2,1)S(1)} collective-permute-done((bf16[768,256]{1,0:T(8,128)(2,1)S(1)}, bf16[768,256]{1,0:T(8,128)(2,1)S(1)}, u32[]{:S(2)}, u32[]{:S(2)}) %collective-permute-start.14) | collective-permute-done | bytes 393248 | tf_op jit(solution)/shard_map/ppermute | solution.py:398
  121.8 6.4 %down.3 = (bf16[192,1280]{1,0:T(8,128)(2,1)S(1)}, bf16[192,1280]{1,0:T(8,128)(2,1)S(1)}, bf16[192,1280]{1,0:T(8,128)(2,1)S(1)}, bf16[192,1280]{1,0:T(8,128)(2,1)S(1)}) custom-call(s32[3]{0:T(128)S(1)} %pad_add_fusion.where_ref, bf16[768,256]{1,0:T(8,128)(2,1)S(1)} %hidden.3.refs_0_.refs_9_, bf16[768,256]{1,0:T(8,128)(2,1)S(1)} %collective-permute-done.12.refs_1_, ...), custom_call_target="tpu_custom_call" | custom-call | flops 1024 | bytes 1024 | tf_op jit(solution)/shard_map/down/pallas_call | solution.py:330
  128.2 1.5 collective-permute-start.15
  129.7 10.8 %collective-permute-done.15.b_ref = bf16[192,1280]{1,0:T(8,128)(2,1)S(1)} collective-permute-done((bf16[192,1280]{1,0:T(8,128)(2,1)S(1)}, bf16[192,1280]{1,0:T(8,128)(2,1)S(1)}, u32[]{:S(2)}, u32[]{:S(2)}) %collective-permute-start.15) | collective-permute-done | bytes 491552 | tf_op jit(solution)/shard_map/ppermute | solution.py:376
  141.3 6.9 %collective-permute-start.16 = (bf16[192,1280]{1,0:T(8,128)(2,1)S(1)}, bf16[192,1280]{1,0:T(8,128)(2,1)S(1)}, u32[]{:S(2)}, u32[]{:S(2)}) collective-permute-start(bf16[192,1280]{1,0:T(8,128)(2,1)S(1)} %get-tuple-element.38), channel_id=1, source_target_pairs={{0,4},{12,8},{1,5},{13,9},{2,6},{14,10},{3,7},{15,11},{16,20},{28,... | collective-permute-start | bytes 1474568 | tf_op jit(solution)/shard_map/ppermute | solution.py:376
  148.3 9.4 %collective-permute-start.19 = (bf16[192,1280]{1,0:T(8,128)(2,1)S(1)}, bf16[192,1280]{1,0:T(8,128)(2,1)S(1)}, u32[]{:S(2)}, u32[]{:S(2)}) collective-permute-start(bf16[192,1280]{1,0:T(8,128)(2,1)S(1)} %add_convert_fusion.1), channel_id=1, source_target_pairs={{0,4},{4,0},{8,12},{12,8},{1,5},{5,1},{9,13},{13,9},{2,6},{6,2},{1... | collective-permute-start | bytes 1474568 | tf_op jit(solution)/shard_map/ppermute | solution.py:376
  157.7 1.8 %collective-permute-done.16 = bf16[192,1280]{1,0:T(8,128)(2,1)S(1)} collective-permute-done((bf16[192,1280]{1,0:T(8,128)(2,1)S(1)}, bf16[192,1280]{1,0:T(8,128)(2,1)S(1)}, u32[]{:S(2)}, u32[]{:S(2)}) %collective-permute-start.16) | collective-permute-done | bytes 491552 | tf_op jit(solution)/shard_map/ppermute | solution.py:376
  160.3 8.2 %collective-permute-done.19 = bf16[192,1280]{1,0:T(8,128)(2,1)S(1)} collective-permute-done((bf16[192,1280]{1,0:T(8,128)(2,1)S(1)}, bf16[192,1280]{1,0:T(8,128)(2,1)S(1)}, u32[]{:S(2)}, u32[]{:S(2)}) %collective-permute-start.19) | collective-permute-done | bytes 491552 | tf_op jit(solution)/shard_map/ppermute | solution.py:376
  168.5 1.0 add_convert_fusion
  (30 shorter events, 7.1 us)
Async XLA Ops:
  1.4 1.0 copy-start
  2.5 15.2 %collective-permute-start = (bf16[208,1280]{1,0:T(8,128)(2,1)S(1)}, bf16[208,1280]{1,0:T(8,128)(2,1)S(1)}, u32[]{:S(2)}, u32[]{:S(2)}) collective-permute-start(bf16[208,1280]{1,0:T(8,128)(2,1)S(1)} %pack.1.refs_0_), channel_id=1, source_target_pairs={{0,4},{4,0},{8,12},{12,8},{1,5},{5,1},{9,13},{13,9},{2,6},{6,2},{1... | collective-permute-start | bytes 1597448 | tf_op jit(solution)/shard_map/ppermute | solution.py:376
  5.6 12.8 %collective-permute-start.1 = (bf16[208,1280]{1,0:T(8,128)(2,1)S(1)}, bf16[208,1280]{1,0:T(8,128)(2,1)S(1)}, u32[]{:S(2)}, u32[]{:S(2)}) collective-permute-start(bf16[208,1280]{1,0:T(8,128)(2,1)S(1)} %pack.1.refs_0_), channel_id=1, source_target_pairs={{4,8},{8,4},{5,9},{9,5},{6,10},{10,6},{7,11},{11,7},{20,24},{24,20... | collective-permute-start | bytes 1597448 | tf_op jit(solution)/shard_map/ppermute | solution.py:376
  17.7 2.0 %collective-permute-start.3 = (bf16[208,1280]{1,0:T(8,128)(2,1)S(1)}, bf16[208,1280]{1,0:T(8,128)(2,1)S(1)}, u32[]{:S(2)}, u32[]{:S(2)}) collective-permute-start(bf16[208,1280]{1,0:T(8,128)(2,1)S(1)} %collective-permute-done.refs_0_), channel_id=1, source_target_pairs={{4,8},{8,4},{5,9},{9,5},{6,10},{10,6},{7,11},{11,7},{20,24},{24,20... | collective-permute-start | bytes 1597448 | tf_op jit(solution)/shard_map/ppermute | solution.py:376
  18.4 17.4 %collective-permute-start.2 = (bf16[208,1280]{1,0:T(8,128)(2,1)S(1)}, bf16[208,1280]{1,0:T(8,128)(2,1)S(1)}, u32[]{:S(2)}, u32[]{:S(2)}) collective-permute-start(bf16[208,1280]{1,0:T(8,128)(2,1)S(1)} %collective-permute-done.1.refs_0_), channel_id=1, source_target_pairs={{4,0},{8,12},{5,1},{9,13},{6,2},{10,14},{7,3},{11,15},{20,16},{24,... | collective-permute-start | bytes 1597448 | tf_op jit(solution)/shard_map/ppermute | solution.py:376
  19.7 26.9 %collective-permute-start.4 = (bf16[208,1280]{1,0:T(8,128)(2,1)S(1)}, bf16[208,1280]{1,0:T(8,128)(2,1)S(1)}, u32[]{:S(2)}, u32[]{:S(2)}) collective-permute-start(bf16[208,1280]{1,0:T(8,128)(2,1)S(1)} %collective-permute-done.3.refs_0_), channel_id=1, source_target_pairs={{4,0},{8,12},{5,1},{9,13},{6,2},{10,14},{7,3},{11,15},{20,16},{24,... | collective-permute-start | bytes 1597448 | tf_op jit(solution)/shard_map/ppermute | solution.py:376
  58.6 3.5 %collective-permute-start.5 = (bf16[2,512,768]{2,1,0:T(8,128)(2,1)S(1)}, bf16[2,512,768]{2,1,0:T(8,128)(2,1)S(1)}, u32[]{:S(2)}, u32[]{:S(2)}) collective-permute-start(bf16[2,512,768]{2,1,0:T(8,128)(2,1)S(1)} %get-tuple-element.28), channel_id=1, source_target_pairs={{0,1},{1,0},{2,3},{3,2},{4,5},{5,4},{6,7},{7,6},{8,9},{9,8},{10,11... | collective-permute-start | bytes 4718600 | tf_op jit(solution)/shard_map/ppermute | solution.py:389
  62.3 19.6 %collective-permute-start.7 = (bf16[512,768]{1,0:T(8,128)(2,1)S(1)}, bf16[512,768]{1,0:T(8,128)(2,1)S(1)}, u32[]{:S(2)}, u32[]{:S(2)}) collective-permute-start(bf16[512,768]{1,0:T(8,128)(2,1)S(1)} %chip_sum.2.refs_5_), channel_id=1, source_target_pairs={{0,2},{1,3},{2,0},{3,1},{4,6},{5,7},{6,4},{7,5},{8,10},{9,11},{10,... | collective-permute-start | bytes 2359304 | tf_op jit(solution)/shard_map/ppermute | solution.py:393
  75.0 9.2 %collective-permute-start.6 = (bf16[2,512,768]{2,1,0:T(8,128)(2,1)S(1)}, bf16[2,512,768]{2,1,0:T(8,128)(2,1)S(1)}, u32[]{:S(2)}, u32[]{:S(2)}) collective-permute-start(bf16[2,512,768]{2,1,0:T(8,128)(2,1)S(1)} %get-tuple-element.30), channel_id=1, source_target_pairs={{0,1},{1,0},{2,3},{3,2},{4,5},{5,4},{6,7},{7,6},{8,9},{9,8},{10,11... | collective-permute-start | bytes 4718600 | tf_op jit(solution)/shard_map/ppermute | solution.py:389
  82.6 12.1 %collective-permute-start.9 = (bf16[768,256]{1,0:T(8,128)(2,1)S(1)}, bf16[768,256]{1,0:T(8,128)(2,1)S(1)}, u32[]{:S(2)}, u32[]{:S(2)}) collective-permute-start(bf16[768,256]{1,0:T(8,128)(2,1)S(1)} %hidden.2._.refs_0_), channel_id=1, source_target_pairs={{0,2},{1,3},{2,0},{3,1},{4,6},{5,7},{6,4},{7,5},{8,10},{9,11},{10,... | collective-permute-start | bytes 1179656 | tf_op jit(solution)/shard_map/ppermute | solution.py:396
  84.4 25.5 %collective-permute-start.8 = (bf16[512,768]{1,0:T(8,128)(2,1)S(1)}, bf16[512,768]{1,0:T(8,128)(2,1)S(1)}, u32[]{:S(2)}, u32[]{:S(2)}) collective-permute-start(bf16[512,768]{1,0:T(8,128)(2,1)S(1)} %chip_sum.3.refs_9_), channel_id=1, source_target_pairs={{0,2},{1,3},{2,0},{3,1},{4,6},{5,7},{6,4},{7,5},{8,10},{9,11},{10,... | collective-permute-start | bytes 2359304 | tf_op jit(solution)/shard_map/ppermute | solution.py:393
  85.0 9.8 %collective-permute-start.10 = (bf16[768,256]{1,0:T(8,128)(2,1)S(1)}, bf16[768,256]{1,0:T(8,128)(2,1)S(1)}, u32[]{:S(2)}, u32[]{:S(2)}) collective-permute-start(bf16[768,256]{1,0:T(8,128)(2,1)S(1)} %hidden.2._.refs_0_), channel_id=1, source_target_pairs={{0,1},{1,0},{2,3},{3,2},{4,5},{5,4},{6,7},{7,6},{8,9},{9,8},{10,11... | collective-permute-start | bytes 1179656 | tf_op jit(solution)/shard_map/ppermute | solution.py:397
  94.7 1.7 %collective-permute-start.11 = (bf16[768,256]{1,0:T(8,128)(2,1)S(1)}, bf16[768,256]{1,0:T(8,128)(2,1)S(1)}, u32[]{:S(2)}, u32[]{:S(2)}) collective-permute-start(bf16[768,256]{1,0:T(8,128)(2,1)S(1)} %collective-permute-done.9.refs_1_), channel_id=1, source_target_pairs={{0,1},{1,0},{2,3},{3,2},{4,5},{5,4},{6,7},{7,6},{8,9},{9,8},{10,11... | collective-permute-start | bytes 1179656 | tf_op jit(solution)/shard_map/ppermute | solution.py:398
  110.6 9.5 %collective-permute-start.12 = (bf16[768,256]{1,0:T(8,128)(2,1)S(1)}, bf16[768,256]{1,0:T(8,128)(2,1)S(1)}, u32[]{:S(2)}, u32[]{:S(2)}) collective-permute-start(bf16[768,256]{1,0:T(8,128)(2,1)S(1)} %hidden.3.refs_0_.refs_9_), channel_id=1, source_target_pairs={{0,2},{1,3},{2,0},{3,1},{4,6},{5,7},{6,4},{7,5},{8,10},{9,11},{10,... | collective-permute-start | bytes 1179656 | tf_op jit(solution)/shard_map/ppermute | solution.py:396
  112.1 7.9 %collective-permute-start.13 = (bf16[768,256]{1,0:T(8,128)(2,1)S(1)}, bf16[768,256]{1,0:T(8,128)(2,1)S(1)}, u32[]{:S(2)}, u32[]{:S(2)}) collective-permute-start(bf16[768,256]{1,0:T(8,128)(2,1)S(1)} %hidden.3.refs_0_.refs_9_), channel_id=1, source_target_pairs={{0,1},{1,0},{2,3},{3,2},{4,5},{5,4},{6,7},{7,6},{8,9},{9,8},{10,11... | collective-permute-start | bytes 1179656 | tf_op jit(solution)/shard_map/ppermute | solution.py:397
  120.0 1.7 %collective-permute-start.14 = (bf16[768,256]{1,0:T(8,128)(2,1)S(1)}, bf16[768,256]{1,0:T(8,128)(2,1)S(1)}, u32[]{:S(2)}, u32[]{:S(2)}) collective-permute-start(bf16[768,256]{1,0:T(8,128)(2,1)S(1)} %collective-permute-done.12.refs_1_), channel_id=1, source_target_pairs={{0,1},{1,0},{2,3},{3,2},{4,5},{5,4},{6,7},{7,6},{8,9},{9,8},{10,11... | collective-permute-start | bytes 1179656 | tf_op jit(solution)/shard_map/ppermute | solution.py:398
  128.2 12.3 %collective-permute-start.15 = (bf16[192,1280]{1,0:T(8,128)(2,1)S(1)}, bf16[192,1280]{1,0:T(8,128)(2,1)S(1)}, u32[]{:S(2)}, u32[]{:S(2)}) collective-permute-start(bf16[192,1280]{1,0:T(8,128)(2,1)S(1)} %get-tuple-element.36.a_ref), channel_id=1, source_target_pairs={{0,4},{12,8},{1,5},{13,9},{2,6},{14,10},{3,7},{15,11},{16,20},{28,... | collective-permute-start | bytes 1474568 | tf_op jit(solution)/shard_map/ppermute | solution.py:376
  140.6 7.6 %collective-permute-start.18 = (bf16[192,1280]{1,0:T(8,128)(2,1)S(1)}, bf16[192,1280]{1,0:T(8,128)(2,1)S(1)}, u32[]{:S(2)}, u32[]{:S(2)}) collective-permute-start(bf16[192,1280]{1,0:T(8,128)(2,1)S(1)} %get-tuple-element.40), channel_id=1, source_target_pairs={{4,8},{8,4},{5,9},{9,5},{6,10},{10,6},{7,11},{11,7},{20,24},{24,20... | collective-permute-start | bytes 1474568 | tf_op jit(solution)/shard_map/ppermute | solution.py:376
  141.3 18.2 %collective-permute-start.16 = (bf16[192,1280]{1,0:T(8,128)(2,1)S(1)}, bf16[192,1280]{1,0:T(8,128)(2,1)S(1)}, u32[]{:S(2)}, u32[]{:S(2)}) collective-permute-start(bf16[192,1280]{1,0:T(8,128)(2,1)S(1)} %get-tuple-element.38), channel_id=1, source_target_pairs={{0,4},{12,8},{1,5},{13,9},{2,6},{14,10},{3,7},{15,11},{16,20},{28,... | collective-permute-start | bytes 1474568 | tf_op jit(solution)/shard_map/ppermute | solution.py:376
  148.3 20.2 %collective-permute-start.19 = (bf16[192,1280]{1,0:T(8,128)(2,1)S(1)}, bf16[192,1280]{1,0:T(8,128)(2,1)S(1)}, u32[]{:S(2)}, u32[]{:S(2)}) collective-permute-start(bf16[192,1280]{1,0:T(8,128)(2,1)S(1)} %add_convert_fusion.1), channel_id=1, source_target_pairs={{0,4},{4,0},{8,12},{12,8},{1,5},{5,1},{9,13},{13,9},{2,6},{6,2},{1... | collective-permute-start | bytes 1474568 | tf_op jit(solution)/shard_map/ppermute | solution.py:376
  159.6 8.9 %collective-permute-start.17 = (bf16[192,1280]{1,0:T(8,128)(2,1)S(1)}, bf16[192,1280]{1,0:T(8,128)(2,1)S(1)}, u32[]{:S(2)}, u32[]{:S(2)}) collective-permute-start(bf16[192,1280]{1,0:T(8,128)(2,1)S(1)} %add_convert_fusion.2), channel_id=1, source_target_pairs={{4,8},{8,4},{5,9},{9,5},{6,10},{10,6},{7,11},{11,7},{20,24},{24,20... | collective-permute-start | bytes 1474568 | tf_op jit(solution)/shard_map/ppermute | solution.py:376

commit v5 on v4

--- a/solution.py
+++ b/solution.py
@@ -257,28 +257,29 @@
     )(keep, near, after)
 
 
-def down_kernel(group, n_blocks, chunk, has_carry, where_ref, *refs):
-    hidden_refs, refs = refs[:4], refs[4:]
+def down_kernel(group, n_blocks, chunk, quarters, has_carry, has_part, is_part, where_ref, *refs):
+    hidden_refs, refs = refs[: len(quarters)], refs[len(quarters) :]
     route_refs, refs = refs[:n_blocks], refs[n_blocks:]
     w_hbm, refs = refs[0], refs[2:]
     carry_ref, refs = (refs[0], refs[1:]) if has_carry else (None, refs)
+    part_ref, refs = (refs[0], refs[1:]) if has_part else (None, refs)
     out_refs, (held, w_buf, sems) = refs[:-3], refs[-3:]
     rows = n_blocks * CAP
     quarter = w_hbm.shape[1] // 4
     count = route_refs[0].shape[1]
     local = w_hbm.shape[0]
     x, core = where_ref[1], where_ref[2]
-    order = [(x, core), (1 - x, core), (x, 1 - core), (1 - x, 1 - core)]
+    order = [(x, core), (x, 1 - core), (1 - x, core), (1 - x, 1 - core)]
 
     def fetch(e):
         copies = []
-        for j in range(4):
+        for n, j in enumerate(quarters):
             f0 = pl.multiple_of((order[j][0] * 2 + order[j][1]) * quarter, quarter)
             copies.append(
                 pltpu.make_async_copy(
                     w_hbm.at[chunk * group + e, pl.ds(f0, quarter)],
-                    w_buf.at[e, pl.ds(j * quarter, quarter)],
-                    sems.at[e, j],
+                    w_buf.at[e, pl.ds(n * quarter, quarter)],
+                    sems.at[e, n],
                 )
             )
         return copies
@@ -295,9 +296,17 @@
         if e + 2 < group:
             start(e + 2)
         units = jnp.concatenate([h[e * rows : (e + 1) * rows, :] for h in hidden_refs], axis=1)
-        out = lax.dot_general(units, w_buf[e], NN, preferred_element_type=F32).astype(BF16)
+        out = lax.dot_general(units, w_buf[e], NN, preferred_element_type=F32)
+        if is_part:
+            out_refs[0][e] = out
+            continue
+        if has_part:
+            out = out + part_ref[e]
+        out = out.astype(BF16)
         for i in range(n_blocks):
             held[i, e * CAP : (e + 1) * CAP, :] = out[i * CAP : (i + 1) * CAP]
+    if is_part:
+        return
     slot_of = lax.broadcasted_iota(jnp.int32, (CAP, count), 0).astype(F32)
     for i in range(n_blocks):
         table = [
@@ -316,34 +325,57 @@
             out_refs[0][i] = total
 
 
-def down(where, hidden, routes, down_weight, chunk, group, carry, after):
+def down(where, hidden, routes, down_weight, chunk, group, carry, after, part=None, is_part=False):
     n_blocks = len(routes)
-    units = hidden[0].shape[1]
+    quarters = tuple(sorted(hidden))
+    units = hidden[quarters[0]].shape[1]
     count = routes[0].shape[1]
     width = down_weight.shape[2]
     whole = pl.BlockSpec(memory_space=pltpu.VMEM)
-    carried = [] if carry is None else [carry]
-    if carry is None:
+    extra = [a for a in (carry, part) if a is not None]
+    if is_part:
+        out_shape = (jax.ShapeDtypeStruct((group, n_blocks * CAP, width), F32),)
+    elif carry is None:
         out_shape = (jax.ShapeDtypeStruct((n_blocks, count, width), F32),)
     else:
         out_shape = tuple(jax.ShapeDtypeStruct((count, width), BF16) for _ in routes)
     return pl.pallas_call(
-        functools.partial(down_kernel, group, n_blocks, chunk, carry is not None),
+        functools.partial(
+            down_kernel, group, n_blocks, chunk, quarters, carry is not None, part is not None, is_part
+        ),
         out_shape=out_shape,
         in_specs=[pl.BlockSpec(memory_space=pltpu.SMEM)]
-        + [whole] * (4 + n_blocks)
+        + [whole] * (len(quarters) + n_blocks)
         + [pl.BlockSpec(memory_space=pl.ANY)] * 2
-        + [whole] * len(carried),
+        + [whole] * len(extra),
         out_specs=tuple(whole for _ in out_shape),
         scratch_shapes=[
             pltpu.VMEM((n_blocks, group * CAP, width), BF16),
-            pltpu.VMEM((group, 4 * units, width), BF16),
-            pltpu.SemaphoreType.DMA((group, 4)),
+            pltpu.VMEM((group, len(quarters) * units, width), BF16),
+            pltpu.SemaphoreType.DMA((group, len(quarters))),
         ],
         compiler_params=params(28),
         cost_estimate=QUICK,
         name="down",
-    )(where, *hidden, *routes, down_weight, after, *carried)
+    )(where, *(hidden[j] for j in quarters), *routes, down_weight, after, *extra)
+
+
+def hold_kernel(*_):
+    pass
+
+
+def hold(arrays, until):
+    free = pl.BlockSpec(memory_space=pl.ANY)
+    return pl.pallas_call(
+        hold_kernel,
+        out_shape=tuple(jax.ShapeDtypeStruct(a.shape, a.dtype) for a in arrays),
+        in_specs=[free] * (len(arrays) + len(until)),
+        out_specs=(free,) * len(arrays),
+        input_output_aliases={i: i for i in range(len(arrays))},
+        compiler_params=params(1),
+        cost_estimate=QUICK,
+        name="hold",
+    )(*arrays, *until)
 
 
 def plus_kernel(a_ref, b_ref, _, out_ref, __):
@@ -392,22 +424,28 @@
         total = chip_sum(keep, near, after)
         return total, lax.ppermute(total, "tp", ACROSS_X)
 
-    def gathered(own):
+    def halves(own):
         own_x = lax.ppermute(own, "tp", ACROSS_X)
-        own_core = lax.ppermute(own, "tp", ACROSS_CORE)
-        return own, own_x, own_core, lax.ppermute(own_x, "tp", ACROSS_CORE)
+        return own_x, lax.ppermute(own, "tp", ACROSS_CORE)
 
     keep_0, near_0 = sums(0, placed[3])
     turn, far_0 = across(keep_0, near_0, keep_0)
     keep_1, near_1 = sums(1, turn)
     own_0 = hidden_quarter(keep_0, near_0, far_0, keep_1)
-    hidden_0 = gathered(own_0)
+    x_0, core_0 = halves(own_0)
+    both_0 = lax.ppermute(x_0, "tp", ACROSS_CORE)
     turn, far_1 = across(keep_1, near_1, own_0)
+    hidden_0 = {0: own_0, 1: core_0, 2: x_0, 3: both_0}
     (carry,) = down(where, hidden_0, tables, down_weight, 0, group, None, turn)
     own_1 = hidden_quarter(keep_1, near_1, far_1, carry)
-    hidden_1 = gathered(own_1)
+    x_1, core_1 = halves(own_1)
+    (part,) = down(
+        where, {0: own_1, 1: core_1}, tables, down_weight, 1, group, None, own_1, is_part=True
+    )
+    (x_1,) = hold((x_1,), (part,))
+    both_1 = lax.ppermute(x_1, "tp", ACROSS_CORE)
     own, other, far_in, far_out = down(
-        where, hidden_1, tables, down_weight, 1, group, carry, own_1
+        where, {2: x_1, 3: both_1}, tables, down_weight, 1, group, carry, part, part
     )
 
     def plus(a, b):

time: 172 us -> 173 us (level)
  Pallas kernels: 41.1 us -> 45.5 us
  waiting for transfers between devices: 92.8 us -> 88.8 us
    pallas_call x2 -> x4, Pallas kernels: 12.7 us -> 17.2 us  [the longest x3 17.2 us: down(): pl.pallas_call(functools.partial(down_kernel, group, n_blocks, chunk, qua...]
    ppermute x6, waiting for transfers between devices: 21.1 us -> 19 us  [the longest x2 15.4 us: halves(): own_x = lax.ppermute(own, 'tp', ACROSS_X)]
    ppermute x2, waiting for transfers between devices: 13.9 us -> 12.1 us  [across(): return (total, lax.ppermute(total, 'tp', ACROSS_X))]
  transfers between devices with their start and end apart: 20 -> 20, of which waited for: 13 -> 14; matrix products, arithmetic and copies ran while one was open for 0% -> 0% of each run, Pallas kernels for 13% -> 16%
where the time goes in v5:
time: 173 us; the launch traced here: 170 us
  waiting for transfers between devices  88.8 us (51%)
  Pallas kernels  45.5 us (26%)
  starting transfers between devices  31.7 us (18%)
  other arithmetic  2.66 us (2%)
    ppermute x10, waiting for transfers between devices, hop(): return lax.ppermute(array, 'ep', pairs)  54.4 us
    ppermute x10, starting transfers between devices, hop(): return lax.ppermute(array, 'ep', pairs)  26.2 us
    pallas_call x2, Pallas kernels, gate_up(): pl.pallas_call(functools.partial(gate_up_kernel, n_blocks), grid=(group,)...  22.1 us
    pallas_call x3, Pallas kernels, down(): pl.pallas_call(functools.partial(down_kernel, group, n_blocks, chunk, qua...  17.2 us
    ppermute x2, waiting for transfers between devices, halves(): own_x = lax.ppermute(own, 'tp', ACROSS_X)  15.4 us
    ppermute x2, waiting for transfers between devices, across(): return (total, lax.ppermute(total, 'tp', ACROSS_X))  12.1 us
    pallas_call x4, Pallas kernels, place(): pl.pallas_call(functools.partial(place_kernel, experts), out_shape=(jax.S...  4.36 us
  transfers between devices with their start and end apart: 20, of which 14 were waited for; matrix products, arithmetic and copies ran while one was open for 0% of the time, Pallas kernels for 16%

profile of v5, /device:TPU:0, one launch (start us, length us, event | category | flops | bytes accessed | tf_op | source)
XLA Modules:
  0.0 170.0 jit_solution(11495150148165430781)
XLA Ops:
  1.4 1.0 copy-done
  2.5 3.1 %collective-permute-start = (bf16[208,1280]{1,0:T(8,128)(2,1)S(1)}, bf16[208,1280]{1,0:T(8,128)(2,1)S(1)}, u32[]{:S(2)}, u32[]{:S(2)}) collective-permute-start(bf16[208,1280]{1,0:T(8,128)(2,1)S(1)} %pack.1.refs_0_), channel_id=1, source_target_pairs={{0,4},{4,0},{8,12},{12,8},{1,5},{5,1},{9,13},{13,9},{2,6},{6,2},{1... | collective-permute-start | bytes 1597448 | tf_op jit(solution)/shard_map/ppermute | solution.py:408
  6.2 11.4 %collective-permute-done.refs_0_ = bf16[208,1280]{1,0:T(8,128)(2,1)S(1)} collective-permute-done((bf16[208,1280]{1,0:T(8,128)(2,1)S(1)}, bf16[208,1280]{1,0:T(8,128)(2,1)S(1)}, u32[]{:S(2)}, u32[]{:S(2)}) %collective-permute-start) | collective-permute-done | bytes 532512 | tf_op jit(solution)/shard_map/ppermute | solution.py:408
  18.4 1.3 collective-permute-start.2
  19.7 1.3 collective-permute-start.4
  21.1 1.1 place.4
  22.1 1.1 place.5
  23.2 12.5 %collective-permute-done.2.refs_1_ = bf16[208,1280]{1,0:T(8,128)(2,1)S(1)} collective-permute-done((bf16[208,1280]{1,0:T(8,128)(2,1)S(1)}, bf16[208,1280]{1,0:T(8,128)(2,1)S(1)}, u32[]{:S(2)}, u32[]{:S(2)}) %collective-permute-start.2) | collective-permute-done | bytes 532512 | tf_op jit(solution)/shard_map/ppermute | solution.py:408
  35.7 1.1 place.6
  36.8 9.7 %collective-permute-done.4.refs_1_ = bf16[208,1280]{1,0:T(8,128)(2,1)S(1)} collective-permute-done((bf16[208,1280]{1,0:T(8,128)(2,1)S(1)}, bf16[208,1280]{1,0:T(8,128)(2,1)S(1)}, u32[]{:S(2)}, u32[]{:S(2)}) %collective-permute-start.4) | collective-permute-done | bytes 532512 | tf_op jit(solution)/shard_map/ppermute | solution.py:408
  46.5 1.1 place.7
  47.6 11.0 %gate_up.2 = (bf16[2,512,768]{2,1,0:T(8,128)(2,1)S(1)}, bf16[2,512,768]{2,1,0:T(8,128)(2,1)S(1)}) custom-call(s32[3]{0:T(128)S(1)} %pad_add_fusion.where_ref, bf16[8,48,1280]{2,1,0:T(8,128)(2,1)S(1)} %get-tuple-element.23.refs_0_, bf16[8,48,1280]{2,1,0:T(8,128)(2,1)S(1)} %get-tuple-element.24.refs_1_, bf16[8,48,1280]{2,1,0:T(8,128)(2,1)S(1)} %get-tuple-element.25.refs_2_, ...), custom_call_target="tpu_custom_call" | custom-call | flops 1024 | bytes 1024 | tf_op jit(solution)/shard_map/gate_up/pallas_call | solution.py:190
  58.7 3.4 %collective-permute-done.5.near_ref = bf16[2,512,768]{2,1,0:T(8,128)(2,1)S(1)} collective-permute-done((bf16[2,512,768]{2,1,0:T(8,128)(2,1)S(1)}, bf16[2,512,768]{2,1,0:T(8,128)(2,1)S(1)}, u32[]{:S(2)}, u32[]{:S(2)}) %collective-permute-start.5) | collective-permute-done | bytes 1572896 | tf_op jit(solution)/shard_map/ppermute | solution.py:421
  62.3 1.6 collective-permute-start.7
  63.8 11.1 %gate_up.3 = (bf16[2,512,768]{2,1,0:T(8,128)(2,1)S(1)}, bf16[2,512,768]{2,1,0:T(8,128)(2,1)S(1)}) custom-call(s32[3]{0:T(128)S(1)} %pad_add_fusion.where_ref, bf16[8,48,1280]{2,1,0:T(8,128)(2,1)S(1)} %get-tuple-element.23.refs_0_, bf16[8,48,1280]{2,1,0:T(8,128)(2,1)S(1)} %get-tuple-element.24.refs_1_, bf16[8,48,1280]{2,1,0:T(8,128)(2,1)S(1)} %get-tuple-element.25.refs_2_, ...), custom_call_target="tpu_custom_call" | custom-call | flops 1024 | bytes 1024 | tf_op jit(solution)/shard_map/gate_up/pallas_call | solution.py:190
  75.0 6.9 %collective-permute-done.7.far_ref = bf16[512,768]{1,0:T(8,128)(2,1)S(1)} collective-permute-done((bf16[512,768]{1,0:T(8,128)(2,1)S(1)}, bf16[512,768]{1,0:T(8,128)(2,1)S(1)}, u32[]{:S(2)}, u32[]{:S(2)}) %collective-permute-start.7) | collective-permute-done | bytes 786464 | tf_op jit(solution)/shard_map/ppermute | solution.py:425
  82.6 1.6 collective-permute-start.10
  85.0 9.8 %collective-permute-done.10.refs_2_ = bf16[768,256]{1,0:T(8,128)(2,1)S(1)} collective-permute-done((bf16[768,256]{1,0:T(8,128)(2,1)S(1)}, bf16[768,256]{1,0:T(8,128)(2,1)S(1)}, u32[]{:S(2)}, u32[]{:S(2)}) %collective-permute-start.10) | collective-permute-done | bytes 393248 | tf_op jit(solution)/shard_map/ppermute | solution.py:428
  94.7 1.7 %collective-permute-done.11.refs_3_ = bf16[768,256]{1,0:T(8,128)(2,1)S(1)} collective-permute-done((bf16[768,256]{1,0:T(8,128)(2,1)S(1)}, bf16[768,256]{1,0:T(8,128)(2,1)S(1)}, u32[]{:S(2)}, u32[]{:S(2)}) %collective-permute-start.11) | collective-permute-done | bytes 393248 | tf_op jit(solution)/shard_map/ppermute | solution.py:436
  96.5 8.1 %down.3._.refs_8_ = f32[4,192,1280]{2,1,0:T(8,128)S(1)} custom-call(s32[3]{0:T(128)S(1)} %pad_add_fusion.where_ref, bf16[768,256]{1,0:T(8,128)(2,1)S(1)} %hidden.2._.refs_0_, bf16[768,256]{1,0:T(8,128)(2,1)S(1)} %collective-permute-done.9.refs_1_, bf16[768,256]{1,0:T(8,128)(2,1)S(1)} %collective-permute-done.10.refs_2_, ...), custom_call_target="tpu_custom_call" | custom-call | flops 1024 | bytes 1024 | tf_op jit(solution)/shard_map/down/pallas_call | solution.py:342
  104.6 5.2 %collective-permute-done.8.far_ref = bf16[512,768]{1,0:T(8,128)(2,1)S(1)} collective-permute-done((bf16[512,768]{1,0:T(8,128)(2,1)S(1)}, bf16[512,768]{1,0:T(8,128)(2,1)S(1)}, u32[]{:S(2)}, u32[]{:S(2)}) %collective-permute-start.8) | collective-permute-done | bytes 786464 | tf_op jit(solution)/shard_map/ppermute | solution.py:425
  110.6 1.6 collective-permute-start.12
  112.4 4.2 %down.4.__1_.refs_7_.refs_9_ = f32[4,192,1280]{2,1,0:T(8,128)S(1)} custom-call(s32[3]{0:T(128)S(1)} %pad_add_fusion.where_ref, bf16[768,256]{1,0:T(8,128)(2,1)S(1)} %hidden.3.refs_0_.refs_7_, bf16[768,256]{1,0:T(8,128)(2,1)S(1)} %collective-permute-done.13.refs_1_, f32[16,192]{1,0:T(8,128)S(1)} %get-tuple-element.31.refs_4_.refs_2_, ...), custom_call_target="tpu_custom_call" | custom-call | flops 1024 | bytes 1024 | tf_op jit(solution)/shard_map/down/pallas_call | solution.py:342
  116.6 5.6 %collective-permute-done.12.__0_ = bf16[768,256]{1,0:T(8,128)(2,1)S(1)} collective-permute-done((bf16[768,256]{1,0:T(8,128)(2,1)S(1)}, bf16[768,256]{1,0:T(8,128)(2,1)S(1)}, u32[]{:S(2)}, u32[]{:S(2)}) %collective-permute-start.12) | collective-permute-done | bytes 393248 | tf_op jit(solution)/shard_map/ppermute | solution.py:428
  122.2 1.7 %collective-permute-done.14.refs_1_ = bf16[768,256]{1,0:T(8,128)(2,1)S(1)} collective-permute-done((bf16[768,256]{1,0:T(8,128)(2,1)S(1)}, bf16[768,256]{1,0:T(8,128)(2,1)S(1)}, u32[]{:S(2)}, u32[]{:S(2)}) %collective-permute-start.14) | collective-permute-done | bytes 393248 | tf_op jit(solution)/shard_map/ppermute | solution.py:446
  123.9 4.9 %down.5 = (bf16[192,1280]{1,0:T(8,128)(2,1)S(1)}, bf16[192,1280]{1,0:T(8,128)(2,1)S(1)}, bf16[192,1280]{1,0:T(8,128)(2,1)S(1)}, bf16[192,1280]{1,0:T(8,128)(2,1)S(1)}) custom-call(s32[3]{0:T(128)S(1)} %pad_add_fusion.where_ref, bf16[768,256]{1,0:T(8,128)(2,1)S(1)} %hold.1.refs_0_, bf16[768,256]{1,0:T(8,128)(2,1)S(1)} %collective-permute-done.14.refs_1_, ...), custom_call_target="tpu_custom_call" | custom-call | flops 1024 | bytes 1024 | tf_op jit(solution)/shard_map/down/pallas_call | solution.py:342
  128.8 1.5 collective-permute-start.15
  130.3 10.8 %collective-permute-done.15.b_ref = bf16[192,1280]{1,0:T(8,128)(2,1)S(1)} collective-permute-done((bf16[192,1280]{1,0:T(8,128)(2,1)S(1)}, bf16[192,1280]{1,0:T(8,128)(2,1)S(1)}, u32[]{:S(2)}, u32[]{:S(2)}) %collective-permute-start.15) | collective-permute-done | bytes 491552 | tf_op jit(solution)/shard_map/ppermute | solution.py:408
  141.9 6.8 %collective-permute-start.16 = (bf16[192,1280]{1,0:T(8,128)(2,1)S(1)}, bf16[192,1280]{1,0:T(8,128)(2,1)S(1)}, u32[]{:S(2)}, u32[]{:S(2)}) collective-permute-start(bf16[192,1280]{1,0:T(8,128)(2,1)S(1)} %get-tuple-element.38), channel_id=1, source_target_pairs={{0,4},{12,8},{1,5},{13,9},{2,6},{14,10},{3,7},{15,11},{16,20},{28,... | collective-permute-start | bytes 1474568 | tf_op jit(solution)/shard_map/ppermute | solution.py:408
  148.9 9.4 %collective-permute-start.19 = (bf16[192,1280]{1,0:T(8,128)(2,1)S(1)}, bf16[192,1280]{1,0:T(8,128)(2,1)S(1)}, u32[]{:S(2)}, u32[]{:S(2)}) collective-permute-start(bf16[192,1280]{1,0:T(8,128)(2,1)S(1)} %add_convert_fusion.1), channel_id=1, source_target_pairs={{0,4},{4,0},{8,12},{12,8},{1,5},{5,1},{9,13},{13,9},{2,6},{6,2},{1... | collective-permute-start | bytes 1474568 | tf_op jit(solution)/shard_map/ppermute | solution.py:408
  158.3 1.7 %collective-permute-done.16 = bf16[192,1280]{1,0:T(8,128)(2,1)S(1)} collective-permute-done((bf16[192,1280]{1,0:T(8,128)(2,1)S(1)}, bf16[192,1280]{1,0:T(8,128)(2,1)S(1)}, u32[]{:S(2)}, u32[]{:S(2)}) %collective-permute-start.16) | collective-permute-done | bytes 491552 | tf_op jit(solution)/shard_map/ppermute | solution.py:408
  160.9 8.2 %collective-permute-done.19 = bf16[192,1280]{1,0:T(8,128)(2,1)S(1)} collective-permute-done((bf16[192,1280]{1,0:T(8,128)(2,1)S(1)}, bf16[192,1280]{1,0:T(8,128)(2,1)S(1)}, u32[]{:S(2)}, u32[]{:S(2)}) %collective-permute-start.19) | collective-permute-done | bytes 491552 | tf_op jit(solution)/shard_map/ppermute | solution.py:408
  (43 shorter events, 8.3 us)
Async XLA Ops:
  1.4 1.0 copy-start
  2.5 15.2 %collective-permute-start = (bf16[208,1280]{1,0:T(8,128)(2,1)S(1)}, bf16[208,1280]{1,0:T(8,128)(2,1)S(1)}, u32[]{:S(2)}, u32[]{:S(2)}) collective-permute-start(bf16[208,1280]{1,0:T(8,128)(2,1)S(1)} %pack.1.refs_0_), channel_id=1, source_target_pairs={{0,4},{4,0},{8,12},{12,8},{1,5},{5,1},{9,13},{13,9},{2,6},{6,2},{1... | collective-permute-start | bytes 1597448 | tf_op jit(solution)/shard_map/ppermute | solution.py:408
  5.6 12.8 %collective-permute-start.1 = (bf16[208,1280]{1,0:T(8,128)(2,1)S(1)}, bf16[208,1280]{1,0:T(8,128)(2,1)S(1)}, u32[]{:S(2)}, u32[]{:S(2)}) collective-permute-start(bf16[208,1280]{1,0:T(8,128)(2,1)S(1)} %pack.1.refs_0_), channel_id=1, source_target_pairs={{4,8},{8,4},{5,9},{9,5},{6,10},{10,6},{7,11},{11,7},{20,24},{24,20... | collective-permute-start | bytes 1597448 | tf_op jit(solution)/shard_map/ppermute | solution.py:408
  17.7 2.0 %collective-permute-start.3 = (bf16[208,1280]{1,0:T(8,128)(2,1)S(1)}, bf16[208,1280]{1,0:T(8,128)(2,1)S(1)}, u32[]{:S(2)}, u32[]{:S(2)}) collective-permute-start(bf16[208,1280]{1,0:T(8,128)(2,1)S(1)} %collective-permute-done.refs_0_), channel_id=1, source_target_pairs={{4,8},{8,4},{5,9},{9,5},{6,10},{10,6},{7,11},{11,7},{20,24},{24,20... | collective-permute-start | bytes 1597448 | tf_op jit(solution)/shard_map/ppermute | solution.py:408
  18.4 17.4 %collective-permute-start.2 = (bf16[208,1280]{1,0:T(8,128)(2,1)S(1)}, bf16[208,1280]{1,0:T(8,128)(2,1)S(1)}, u32[]{:S(2)}, u32[]{:S(2)}) collective-permute-start(bf16[208,1280]{1,0:T(8,128)(2,1)S(1)} %collective-permute-done.1.refs_0_), channel_id=1, source_target_pairs={{4,0},{8,12},{5,1},{9,13},{6,2},{10,14},{7,3},{11,15},{20,16},{24,... | collective-permute-start | bytes 1597448 | tf_op jit(solution)/shard_map/ppermute | solution.py:408
  19.7 26.9 %collective-permute-start.4 = (bf16[208,1280]{1,0:T(8,128)(2,1)S(1)}, bf16[208,1280]{1,0:T(8,128)(2,1)S(1)}, u32[]{:S(2)}, u32[]{:S(2)}) collective-permute-start(bf16[208,1280]{1,0:T(8,128)(2,1)S(1)} %collective-permute-done.3.refs_0_), channel_id=1, source_target_pairs={{4,0},{8,12},{5,1},{9,13},{6,2},{10,14},{7,3},{11,15},{20,16},{24,... | collective-permute-start | bytes 1597448 | tf_op jit(solution)/shard_map/ppermute | solution.py:408
  58.6 3.5 %collective-permute-start.5 = (bf16[2,512,768]{2,1,0:T(8,128)(2,1)S(1)}, bf16[2,512,768]{2,1,0:T(8,128)(2,1)S(1)}, u32[]{:S(2)}, u32[]{:S(2)}) collective-permute-start(bf16[2,512,768]{2,1,0:T(8,128)(2,1)S(1)} %get-tuple-element.28), channel_id=1, source_target_pairs={{0,1},{1,0},{2,3},{3,2},{4,5},{5,4},{6,7},{7,6},{8,9},{9,8},{10,11... | collective-permute-start | bytes 4718600 | tf_op jit(solution)/shard_map/ppermute | solution.py:421
  62.3 19.6 %collective-permute-start.7 = (bf16[512,768]{1,0:T(8,128)(2,1)S(1)}, bf16[512,768]{1,0:T(8,128)(2,1)S(1)}, u32[]{:S(2)}, u32[]{:S(2)}) collective-permute-start(bf16[512,768]{1,0:T(8,128)(2,1)S(1)} %chip_sum.2.refs_5_), channel_id=1, source_target_pairs={{0,2},{1,3},{2,0},{3,1},{4,6},{5,7},{6,4},{7,5},{8,10},{9,11},{10,... | collective-permute-start | bytes 2359304 | tf_op jit(solution)/shard_map/ppermute | solution.py:425
  75.0 9.2 %collective-permute-start.6 = (bf16[2,512,768]{2,1,0:T(8,128)(2,1)S(1)}, bf16[2,512,768]{2,1,0:T(8,128)(2,1)S(1)}, u32[]{:S(2)}, u32[]{:S(2)}) collective-permute-start(bf16[2,512,768]{2,1,0:T(8,128)(2,1)S(1)} %get-tuple-element.30), channel_id=1, source_target_pairs={{0,1},{1,0},{2,3},{3,2},{4,5},{5,4},{6,7},{7,6},{8,9},{9,8},{10,11... | collective-permute-start | bytes 4718600 | tf_op jit(solution)/shard_map/ppermute | solution.py:421
  82.6 12.1 %collective-permute-start.10 = (bf16[768,256]{1,0:T(8,128)(2,1)S(1)}, bf16[768,256]{1,0:T(8,128)(2,1)S(1)}, u32[]{:S(2)}, u32[]{:S(2)}) collective-permute-start(bf16[768,256]{1,0:T(8,128)(2,1)S(1)} %hidden.2._.refs_0_), channel_id=1, source_target_pairs={{0,2},{1,3},{2,0},{3,1},{4,6},{5,7},{6,4},{7,5},{8,10},{9,11},{10,... | collective-permute-start | bytes 1179656 | tf_op jit(solution)/shard_map/ppermute | solution.py:428
  84.4 25.5 %collective-permute-start.8 = (bf16[512,768]{1,0:T(8,128)(2,1)S(1)}, bf16[512,768]{1,0:T(8,128)(2,1)S(1)}, u32[]{:S(2)}, u32[]{:S(2)}) collective-permute-start(bf16[512,768]{1,0:T(8,128)(2,1)S(1)} %chip_sum.3.refs_9_), channel_id=1, source_target_pairs={{0,2},{1,3},{2,0},{3,1},{4,6},{5,7},{6,4},{7,5},{8,10},{9,11},{10,... | collective-permute-start | bytes 2359304 | tf_op jit(solution)/shard_map/ppermute | solution.py:425
  85.0 9.8 %collective-permute-start.9 = (bf16[768,256]{1,0:T(8,128)(2,1)S(1)}, bf16[768,256]{1,0:T(8,128)(2,1)S(1)}, u32[]{:S(2)}, u32[]{:S(2)}) collective-permute-start(bf16[768,256]{1,0:T(8,128)(2,1)S(1)} %hidden.2._.refs_0_), channel_id=1, source_target_pairs={{0,1},{1,0},{2,3},{3,2},{4,5},{5,4},{6,7},{7,6},{8,9},{9,8},{10,11... | collective-permute-start | bytes 1179656 | tf_op jit(solution)/shard_map/ppermute | solution.py:429
  94.7 1.7 %collective-permute-start.11 = (bf16[768,256]{1,0:T(8,128)(2,1)S(1)}, bf16[768,256]{1,0:T(8,128)(2,1)S(1)}, u32[]{:S(2)}, u32[]{:S(2)}) collective-permute-start(bf16[768,256]{1,0:T(8,128)(2,1)S(1)} %collective-permute-done.10.refs_2_), channel_id=1, source_target_pairs={{0,1},{1,0},{2,3},{3,2},{4,5},{5,4},{6,7},{7,6},{8,9},{9,8},{10,11... | collective-permute-start | bytes 1179656 | tf_op jit(solution)/shard_map/ppermute | solution.py:436
  96.5 15.9 %slice-start = ((s8[20971520]{0:T(1024)(128)(4,1)}), s8[4194304]{0:T(1024)(128)(4,1)S(1)}, s32[]{:S(2)}) async-start(s8[20971520]{0:T(1024)(128)(4,1)} %bitcast.6), calls=%async_computation | async-start | bytes 8388608
  96.5 15.9 %slice-start.1 = ((s8[20971520]{0:T(1024)(128)(4,1)}), s8[4194304]{0:T(1024)(128)(4,1)S(1)}, s32[]{:S(2)}) async-start(s8[20971520]{0:T(1024)(128)(4,1)} %bitcast.6), calls=%async_computation.1 | async-start | bytes 8388608
  104.6 7.8 %slice-start.2 = ((s8[20971520]{0:T(1024)(128)(4,1)}), s8[4194304]{0:T(1024)(128)(4,1)S(1)}, s32[]{:S(2)}) async-start(s8[20971520]{0:T(1024)(128)(4,1)} %bitcast.6), calls=%async_computation.2 | async-start | bytes 8388608
  104.6 7.8 %slice-start.3 = ((s8[20971520]{0:T(1024)(128)(4,1)}), s8[4194304]{0:T(1024)(128)(4,1)S(1)}, s32[]{:S(2)}) async-start(s8[20971520]{0:T(1024)(128)(4,1)} %bitcast.6), calls=%async_computation.3 | async-start | bytes 8388608
  104.6 7.8 %slice-start.4 = ((s8[20971520]{0:T(1024)(128)(4,1)}), s8[4194304]{0:T(1024)(128)(4,1)S(1)}, s32[]{:S(2)}) async-start(s8[20971520]{0:T(1024)(128)(4,1)} %bitcast.6), calls=%async_computation.4 | async-start | bytes 8388608
  110.6 1.8 %collective-permute-start.13 = (bf16[768,256]{1,0:T(8,128)(2,1)S(1)}, bf16[768,256]{1,0:T(8,128)(2,1)S(1)}, u32[]{:S(2)}, u32[]{:S(2)}) collective-permute-start(bf16[768,256]{1,0:T(8,128)(2,1)S(1)} %hidden.3.refs_0_.refs_7_), channel_id=1, source_target_pairs={{0,1},{1,0},{2,3},{3,2},{4,5},{5,4},{6,7},{7,6},{8,9},{9,8},{10,11... | collective-permute-start | bytes 1179656 | tf_op jit(solution)/shard_map/ppermute | solution.py:429
  110.6 11.5 %collective-permute-start.12 = (bf16[768,256]{1,0:T(8,128)(2,1)S(1)}, bf16[768,256]{1,0:T(8,128)(2,1)S(1)}, u32[]{:S(2)}, u32[]{:S(2)}) collective-permute-start(bf16[768,256]{1,0:T(8,128)(2,1)S(1)} %hidden.3.refs_0_.refs_7_), channel_id=1, source_target_pairs={{0,2},{1,3},{2,0},{3,1},{4,6},{5,7},{6,4},{7,5},{8,10},{9,11},{10,... | collective-permute-start | bytes 1179656 | tf_op jit(solution)/shard_map/ppermute | solution.py:428
  122.2 1.7 %collective-permute-start.14 = (bf16[768,256]{1,0:T(8,128)(2,1)S(1)}, bf16[768,256]{1,0:T(8,128)(2,1)S(1)}, u32[]{:S(2)}, u32[]{:S(2)}) collective-permute-start(bf16[768,256]{1,0:T(8,128)(2,1)S(1)} %hold.1.refs_0_), channel_id=1, source_target_pairs={{0,1},{1,0},{2,3},{3,2},{4,5},{5,4},{6,7},{7,6},{8,9},{9,8},{10,11... | collective-permute-start | bytes 1179656 | tf_op jit(solution)/shard_map/ppermute | solution.py:446
  128.8 12.3 %collective-permute-start.15 = (bf16[192,1280]{1,0:T(8,128)(2,1)S(1)}, bf16[192,1280]{1,0:T(8,128)(2,1)S(1)}, u32[]{:S(2)}, u32[]{:S(2)}) collective-permute-start(bf16[192,1280]{1,0:T(8,128)(2,1)S(1)} %get-tuple-element.36.a_ref), channel_id=1, source_target_pairs={{0,4},{12,8},{1,5},{13,9},{2,6},{14,10},{3,7},{15,11},{16,20},{28,... | collective-permute-start | bytes 1474568 | tf_op jit(solution)/shard_map/ppermute | solution.py:408
  141.2 7.6 %collective-permute-start.18 = (bf16[192,1280]{1,0:T(8,128)(2,1)S(1)}, bf16[192,1280]{1,0:T(8,128)(2,1)S(1)}, u32[]{:S(2)}, u32[]{:S(2)}) collective-permute-start(bf16[192,1280]{1,0:T(8,128)(2,1)S(1)} %get-tuple-element.40), channel_id=1, source_target_pairs={{4,8},{8,4},{5,9},{9,5},{6,10},{10,6},{7,11},{11,7},{20,24},{24,20... | collective-permute-start | bytes 1474568 | tf_op jit(solution)/shard_map/ppermute | solution.py:408
  141.9 18.1 %collective-permute-start.16 = (bf16[192,1280]{1,0:T(8,128)(2,1)S(1)}, bf16[192,1280]{1,0:T(8,128)(2,1)S(1)}, u32[]{:S(2)}, u32[]{:S(2)}) collective-permute-start(bf16[192,1280]{1,0:T(8,128)(2,1)S(1)} %get-tuple-element.38), channel_id=1, source_target_pairs={{0,4},{12,8},{1,5},{13,9},{2,6},{14,10},{3,7},{15,11},{16,20},{28,... | collective-permute-start | bytes 1474568 | tf_op jit(solution)/shard_map/ppermute | solution.py:408
  148.9 20.2 %collective-permute-start.19 = (bf16[192,1280]{1,0:T(8,128)(2,1)S(1)}, bf16[192,1280]{1,0:T(8,128)(2,1)S(1)}, u32[]{:S(2)}, u32[]{:S(2)}) collective-permute-start(bf16[192,1280]{1,0:T(8,128)(2,1)S(1)} %add_convert_fusion.1), channel_id=1, source_target_pairs={{0,4},{4,0},{8,12},{12,8},{1,5},{5,1},{9,13},{13,9},{2,6},{6,2},{1... | collective-permute-start | bytes 1474568 | tf_op jit(solution)/shard_map/ppermute | solution.py:408
  160.2 8.9 %collective-permute-start.17 = (bf16[192,1280]{1,0:T(8,128)(2,1)S(1)}, bf16[192,1280]{1,0:T(8,128)(2,1)S(1)}, u32[]{:S(2)}, u32[]{:S(2)}) collective-permute-start(bf16[192,1280]{1,0:T(8,128)(2,1)S(1)} %add_convert_fusion.2), channel_id=1, source_target_pairs={{4,8},{8,4},{5,9},{9,5},{6,10},{10,6},{7,11},{11,7},{20,24},{24,20... | collective-permute-start | bytes 1474568 | tf_op jit(solution)/shard_map/ppermute | solution.py:408

commit v6 on v4

--- a/solution.py
+++ b/solution.py
@@ -62,27 +62,33 @@
 EXTRA = 16
 
 
-def pack_kernel(tokens_ref, extra_ref, out_ref):
-    count, lanes = tokens_ref.shape[0], extra_ref.shape[1]
-    out_ref[:count, :] = tokens_ref[...]
-    out_ref[count:, lanes:] = jnp.zeros((EXTRA, out_ref.shape[1] - lanes), BF16)
-    out_ref[count:, :lanes] = extra_ref[...]
+def pack_kernel(tokens_ref, ids_ref, gates_ref, out_ref, sem):
+    count, width = tokens_ref.shape
+    lanes = count + -count % LANES
+    copy = pltpu.make_async_copy(tokens_ref, out_ref.at[pl.ds(0, count)], sem)
+    copy.start()
+    out_ref[count:, :] = jnp.zeros((EXTRA, width), BF16)
+    none = jnp.zeros((EXTRA - TOPK, count), F32)
+    ids = jnp.concatenate([ids_ref[...].astype(F32), none], axis=0)
+    gates = jnp.concatenate([gates_ref[...].astype(F32), none], axis=0)
+    out_ref[count:, :count] = ids.astype(BF16)
+    out_ref[count:, lanes : lanes + count] = gates.astype(BF16)
+    copy.wait()
 
 
 def pack(tokens, expert_ids, gate_weights):
     count, width = tokens.shape
-    spare = -count % LANES
-    extra = [
-        jnp.pad(a.T.astype(BF16), ((0, EXTRA - TOPK), (0, spare)))
-        for a in (expert_ids, gate_weights)
-    ]
+    whole = pl.BlockSpec(memory_space=pltpu.VMEM)
     return pl.pallas_call(
         pack_kernel,
         out_shape=jax.ShapeDtypeStruct((count + EXTRA, width), BF16),
+        in_specs=[pl.BlockSpec(memory_space=pl.ANY), whole, whole],
+        out_specs=whole,
+        scratch_shapes=[pltpu.SemaphoreType.DMA(())],
         compiler_params=params(8),
         cost_estimate=QUICK,
         name="pack",
-    )(tokens, jnp.concatenate(extra, axis=1))
+    )(tokens, expert_ids.T, gate_weights.T)
 
 
 def place_kernel(experts, where_ref, *refs):

time: 172 us -> 173 us (level)
  no operation moved by 1% of the time
where the time goes in v6:
time: 173 us; the launch traced here: 170 us
  waiting for transfers between devices  92.8 us (54%)
  Pallas kernels  41.4 us (24%)
  starting transfers between devices  31.6 us (18%)
  local copies, waits for them, and re-layouts  2.41 us (1%)
    ppermute x10, waiting for transfers between devices, hop(): return lax.ppermute(array, 'ep', pairs)  54.3 us
    ppermute x10, starting transfers between devices, hop(): return lax.ppermute(array, 'ep', pairs)  26.2 us
    pallas_call x2, Pallas kernels, gate_up(): pl.pallas_call(functools.partial(gate_up_kernel, n_blocks), grid=(group,)...  22.1 us
    ppermute x2, waiting for transfers between devices, gathered(): own_x = lax.ppermute(own, 'tp', ACROSS_X)  17.7 us
    ppermute x2, waiting for transfers between devices, across(): return (total, lax.ppermute(total, 'tp', ACROSS_X))  14 us
    pallas_call x2, Pallas kernels, down(): pl.pallas_call(functools.partial(down_kernel, group, n_blocks, chunk, car...  12.7 us
    pallas_call x4, Pallas kernels, place(): pl.pallas_call(functools.partial(place_kernel, experts), out_shape=(jax.S...  4.36 us
  transfers between devices with their start and end apart: 20, of which 13 were waited for; matrix products, arithmetic and copies ran while one was open for 0% of the time, Pallas kernels for 13%

profile of v6, /device:TPU:0, one launch (start us, length us, event | category | flops | bytes accessed | tf_op | source)
XLA Modules:
  0.0 169.7 jit_solution(13455718030496264840)
XLA Ops:
  0.0 1.0 copy-done
  2.7 3.1 %collective-permute-start = (bf16[208,1280]{1,0:T(8,128)(2,1)S(1)}, bf16[208,1280]{1,0:T(8,128)(2,1)S(1)}, u32[]{:S(2)}, u32[]{:S(2)}) collective-permute-start(bf16[208,1280]{1,0:T(8,128)(2,1)S(1)} %pack.1.refs_0_), channel_id=1, source_target_pairs={{0,4},{4,0},{8,12},{12,8},{1,5},{5,1},{9,13},{13,9},{2,6},{6,2},{1... | collective-permute-start | bytes 1597448 | tf_op jit(solution)/shard_map/ppermute | solution.py:382
  6.5 11.4 %collective-permute-done.refs_0_ = bf16[208,1280]{1,0:T(8,128)(2,1)S(1)} collective-permute-done((bf16[208,1280]{1,0:T(8,128)(2,1)S(1)}, bf16[208,1280]{1,0:T(8,128)(2,1)S(1)}, u32[]{:S(2)}, u32[]{:S(2)}) %collective-permute-start) | collective-permute-done | bytes 532512 | tf_op jit(solution)/shard_map/ppermute | solution.py:382
  18.6 1.3 collective-permute-start.2
  19.9 1.3 collective-permute-start.4
  21.3 1.1 place.4
  22.4 1.1 place.5
  23.5 12.5 %collective-permute-done.2.refs_1_ = bf16[208,1280]{1,0:T(8,128)(2,1)S(1)} collective-permute-done((bf16[208,1280]{1,0:T(8,128)(2,1)S(1)}, bf16[208,1280]{1,0:T(8,128)(2,1)S(1)}, u32[]{:S(2)}, u32[]{:S(2)}) %collective-permute-start.2) | collective-permute-done | bytes 532512 | tf_op jit(solution)/shard_map/ppermute | solution.py:382
  36.0 1.1 place.6
  37.1 9.7 %collective-permute-done.4.refs_1_ = bf16[208,1280]{1,0:T(8,128)(2,1)S(1)} collective-permute-done((bf16[208,1280]{1,0:T(8,128)(2,1)S(1)}, bf16[208,1280]{1,0:T(8,128)(2,1)S(1)}, u32[]{:S(2)}, u32[]{:S(2)}) %collective-permute-start.4) | collective-permute-done | bytes 532512 | tf_op jit(solution)/shard_map/ppermute | solution.py:382
  46.8 1.1 place.7
  47.9 11.0 %gate_up.2 = (bf16[2,512,768]{2,1,0:T(8,128)(2,1)S(1)}, bf16[2,512,768]{2,1,0:T(8,128)(2,1)S(1)}) custom-call(s32[3]{0:T(128)S(1)} %pad_add_fusion.where_ref, bf16[8,48,1280]{2,1,0:T(8,128)(2,1)S(1)} %get-tuple-element.23.refs_0_, bf16[8,48,1280]{2,1,0:T(8,128)(2,1)S(1)} %get-tuple-element.24.refs_1_, bf16[8,48,1280]{2,1,0:T(8,128)(2,1)S(1)} %get-tuple-element.25.refs_2_, ...), custom_call_target="tpu_custom_call" | custom-call | flops 1024 | bytes 1024 | tf_op jit(solution)/shard_map/gate_up/pallas_call | solution.py:196
  59.0 3.4 %collective-permute-done.5.near_ref = bf16[2,512,768]{2,1,0:T(8,128)(2,1)S(1)} collective-permute-done((bf16[2,512,768]{2,1,0:T(8,128)(2,1)S(1)}, bf16[2,512,768]{2,1,0:T(8,128)(2,1)S(1)}, u32[]{:S(2)}, u32[]{:S(2)}) %collective-permute-start.5) | collective-permute-done | bytes 1572896 | tf_op jit(solution)/shard_map/ppermute | solution.py:395
  62.6 1.5 collective-permute-start.7
  64.1 11.1 %gate_up.3 = (bf16[2,512,768]{2,1,0:T(8,128)(2,1)S(1)}, bf16[2,512,768]{2,1,0:T(8,128)(2,1)S(1)}) custom-call(s32[3]{0:T(128)S(1)} %pad_add_fusion.where_ref, bf16[8,48,1280]{2,1,0:T(8,128)(2,1)S(1)} %get-tuple-element.23.refs_0_, bf16[8,48,1280]{2,1,0:T(8,128)(2,1)S(1)} %get-tuple-element.24.refs_1_, bf16[8,48,1280]{2,1,0:T(8,128)(2,1)S(1)} %get-tuple-element.25.refs_2_, ...), custom_call_target="tpu_custom_call" | custom-call | flops 1024 | bytes 1024 | tf_op jit(solution)/shard_map/gate_up/pallas_call | solution.py:196
  75.3 6.9 %collective-permute-done.7.far_ref = bf16[512,768]{1,0:T(8,128)(2,1)S(1)} collective-permute-done((bf16[512,768]{1,0:T(8,128)(2,1)S(1)}, bf16[512,768]{1,0:T(8,128)(2,1)S(1)}, u32[]{:S(2)}, u32[]{:S(2)}) %collective-permute-start.7) | collective-permute-done | bytes 786464 | tf_op jit(solution)/shard_map/ppermute | solution.py:399
  82.9 1.5 collective-permute-start.9
  85.3 9.8 %collective-permute-done.9.refs_1_ = bf16[768,256]{1,0:T(8,128)(2,1)S(1)} collective-permute-done((bf16[768,256]{1,0:T(8,128)(2,1)S(1)}, bf16[768,256]{1,0:T(8,128)(2,1)S(1)}, u32[]{:S(2)}, u32[]{:S(2)}) %collective-permute-start.9) | collective-permute-done | bytes 393248 | tf_op jit(solution)/shard_map/ppermute | solution.py:402
  95.0 1.7 %collective-permute-done.11.refs_3_ = bf16[768,256]{1,0:T(8,128)(2,1)S(1)} collective-permute-done((bf16[768,256]{1,0:T(8,128)(2,1)S(1)}, bf16[768,256]{1,0:T(8,128)(2,1)S(1)}, u32[]{:S(2)}, u32[]{:S(2)}) %collective-permute-start.11) | collective-permute-done | bytes 393248 | tf_op jit(solution)/shard_map/ppermute | solution.py:404
  96.7 6.3 %down.2._.refs_10_ = f32[4,192,1280]{2,1,0:T(8,128)S(1)} custom-call(s32[3]{0:T(128)S(1)} %pad_add_fusion.where_ref, bf16[768,256]{1,0:T(8,128)(2,1)S(1)} %hidden.2._.refs_0_, bf16[768,256]{1,0:T(8,128)(2,1)S(1)} %collective-permute-done.9.refs_1_, bf16[768,256]{1,0:T(8,128)(2,1)S(1)} %collective-permute-done.10.refs_2_, ...), custom_call_target="tpu_custom_call" | custom-call | flops 1024 | bytes 1024 | tf_op jit(solution)/shard_map/down/pallas_call | solution.py:336
  103.1 7.1 %collective-permute-done.8.far_ref = bf16[512,768]{1,0:T(8,128)(2,1)S(1)} collective-permute-done((bf16[512,768]{1,0:T(8,128)(2,1)S(1)}, bf16[512,768]{1,0:T(8,128)(2,1)S(1)}, u32[]{:S(2)}, u32[]{:S(2)}) %collective-permute-start.8) | collective-permute-done | bytes 786464 | tf_op jit(solution)/shard_map/ppermute | solution.py:399
  110.9 1.5 collective-permute-start.12
  112.4 7.9 %collective-permute-done.12.refs_1_ = bf16[768,256]{1,0:T(8,128)(2,1)S(1)} collective-permute-done((bf16[768,256]{1,0:T(8,128)(2,1)S(1)}, bf16[768,256]{1,0:T(8,128)(2,1)S(1)}, u32[]{:S(2)}, u32[]{:S(2)}) %collective-permute-start.12) | collective-permute-done | bytes 393248 | tf_op jit(solution)/shard_map/ppermute | solution.py:402
  120.3 1.7 %collective-permute-done.14.refs_3_ = bf16[768,256]{1,0:T(8,128)(2,1)S(1)} collective-permute-done((bf16[768,256]{1,0:T(8,128)(2,1)S(1)}, bf16[768,256]{1,0:T(8,128)(2,1)S(1)}, u32[]{:S(2)}, u32[]{:S(2)}) %collective-permute-start.14) | collective-permute-done | bytes 393248 | tf_op jit(solution)/shard_map/ppermute | solution.py:404
  122.1 6.4 %down.3 = (bf16[192,1280]{1,0:T(8,128)(2,1)S(1)}, bf16[192,1280]{1,0:T(8,128)(2,1)S(1)}, bf16[192,1280]{1,0:T(8,128)(2,1)S(1)}, bf16[192,1280]{1,0:T(8,128)(2,1)S(1)}) custom-call(s32[3]{0:T(128)S(1)} %pad_add_fusion.where_ref, bf16[768,256]{1,0:T(8,128)(2,1)S(1)} %hidden.3.refs_0_.refs_9_, bf16[768,256]{1,0:T(8,128)(2,1)S(1)} %collective-permute-done.12.refs_1_, ...), custom_call_target="tpu_custom_call" | custom-call | flops 1024 | bytes 1024 | tf_op jit(solution)/shard_map/down/pallas_call | solution.py:336
  128.5 1.5 collective-permute-start.15
  129.9 10.9 %collective-permute-done.15.b_ref = bf16[192,1280]{1,0:T(8,128)(2,1)S(1)} collective-permute-done((bf16[192,1280]{1,0:T(8,128)(2,1)S(1)}, bf16[192,1280]{1,0:T(8,128)(2,1)S(1)}, u32[]{:S(2)}, u32[]{:S(2)}) %collective-permute-start.15) | collective-permute-done | bytes 491552 | tf_op jit(solution)/shard_map/ppermute | solution.py:382
  141.6 6.8 %collective-permute-start.16 = (bf16[192,1280]{1,0:T(8,128)(2,1)S(1)}, bf16[192,1280]{1,0:T(8,128)(2,1)S(1)}, u32[]{:S(2)}, u32[]{:S(2)}) collective-permute-start(bf16[192,1280]{1,0:T(8,128)(2,1)S(1)} %get-tuple-element.38), channel_id=1, source_target_pairs={{0,4},{12,8},{1,5},{13,9},{2,6},{14,10},{3,7},{15,11},{16,20},{28,... | collective-permute-start | bytes 1474568 | tf_op jit(solution)/shard_map/ppermute | solution.py:382
  148.6 9.5 %collective-permute-start.19 = (bf16[192,1280]{1,0:T(8,128)(2,1)S(1)}, bf16[192,1280]{1,0:T(8,128)(2,1)S(1)}, u32[]{:S(2)}, u32[]{:S(2)}) collective-permute-start(bf16[192,1280]{1,0:T(8,128)(2,1)S(1)} %add_convert_fusion.1), channel_id=1, source_target_pairs={{0,4},{4,0},{8,12},{12,8},{1,5},{5,1},{9,13},{13,9},{2,6},{6,2},{1... | collective-permute-start | bytes 1474568 | tf_op jit(solution)/shard_map/ppermute | solution.py:382
  158.1 1.6 collective-permute-done.16
  160.5 8.3 %collective-permute-done.19 = bf16[192,1280]{1,0:T(8,128)(2,1)S(1)} collective-permute-done((bf16[192,1280]{1,0:T(8,128)(2,1)S(1)}, bf16[192,1280]{1,0:T(8,128)(2,1)S(1)}, u32[]{:S(2)}, u32[]{:S(2)}) %collective-permute-start.19) | collective-permute-done | bytes 491552 | tf_op jit(solution)/shard_map/ppermute | solution.py:382
  168.8 1.0 add_convert_fusion
  (32 shorter events, 7.4 us)
Async XLA Ops:
  0.0 1.0 copy-start
  1.0 0.7 copy-start.1
  1.7 0.7 copy-start.2
  2.7 15.2 %collective-permute-start = (bf16[208,1280]{1,0:T(8,128)(2,1)S(1)}, bf16[208,1280]{1,0:T(8,128)(2,1)S(1)}, u32[]{:S(2)}, u32[]{:S(2)}) collective-permute-start(bf16[208,1280]{1,0:T(8,128)(2,1)S(1)} %pack.1.refs_0_), channel_id=1, source_target_pairs={{0,4},{4,0},{8,12},{12,8},{1,5},{5,1},{9,13},{13,9},{2,6},{6,2},{1... | collective-permute-start | bytes 1597448 | tf_op jit(solution)/shard_map/ppermute | solution.py:382
  5.8 12.8 %collective-permute-start.1 = (bf16[208,1280]{1,0:T(8,128)(2,1)S(1)}, bf16[208,1280]{1,0:T(8,128)(2,1)S(1)}, u32[]{:S(2)}, u32[]{:S(2)}) collective-permute-start(bf16[208,1280]{1,0:T(8,128)(2,1)S(1)} %pack.1.refs_0_), channel_id=1, source_target_pairs={{4,8},{8,4},{5,9},{9,5},{6,10},{10,6},{7,11},{11,7},{20,24},{24,20... | collective-permute-start | bytes 1597448 | tf_op jit(solution)/shard_map/ppermute | solution.py:382
  17.9 2.0 %collective-permute-start.3 = (bf16[208,1280]{1,0:T(8,128)(2,1)S(1)}, bf16[208,1280]{1,0:T(8,128)(2,1)S(1)}, u32[]{:S(2)}, u32[]{:S(2)}) collective-permute-start(bf16[208,1280]{1,0:T(8,128)(2,1)S(1)} %collective-permute-done.refs_0_), channel_id=1, source_target_pairs={{4,8},{8,4},{5,9},{9,5},{6,10},{10,6},{7,11},{11,7},{20,24},{24,20... | collective-permute-start | bytes 1597448 | tf_op jit(solution)/shard_map/ppermute | solution.py:382
  18.6 17.4 %collective-permute-start.2 = (bf16[208,1280]{1,0:T(8,128)(2,1)S(1)}, bf16[208,1280]{1,0:T(8,128)(2,1)S(1)}, u32[]{:S(2)}, u32[]{:S(2)}) collective-permute-start(bf16[208,1280]{1,0:T(8,128)(2,1)S(1)} %collective-permute-done.1.refs_0_), channel_id=1, source_target_pairs={{4,0},{8,12},{5,1},{9,13},{6,2},{10,14},{7,3},{11,15},{20,16},{24,... | collective-permute-start | bytes 1597448 | tf_op jit(solution)/shard_map/ppermute | solution.py:382
  19.9 26.9 %collective-permute-start.4 = (bf16[208,1280]{1,0:T(8,128)(2,1)S(1)}, bf16[208,1280]{1,0:T(8,128)(2,1)S(1)}, u32[]{:S(2)}, u32[]{:S(2)}) collective-permute-start(bf16[208,1280]{1,0:T(8,128)(2,1)S(1)} %collective-permute-done.3.refs_0_), channel_id=1, source_target_pairs={{4,0},{8,12},{5,1},{9,13},{6,2},{10,14},{7,3},{11,15},{20,16},{24,... | collective-permute-start | bytes 1597448 | tf_op jit(solution)/shard_map/ppermute | solution.py:382
  58.9 3.5 %collective-permute-start.5 = (bf16[2,512,768]{2,1,0:T(8,128)(2,1)S(1)}, bf16[2,512,768]{2,1,0:T(8,128)(2,1)S(1)}, u32[]{:S(2)}, u32[]{:S(2)}) collective-permute-start(bf16[2,512,768]{2,1,0:T(8,128)(2,1)S(1)} %get-tuple-element.28), channel_id=1, source_target_pairs={{0,1},{1,0},{2,3},{3,2},{4,5},{5,4},{6,7},{7,6},{8,9},{9,8},{10,11... | collective-permute-start | bytes 4718600 | tf_op jit(solution)/shard_map/ppermute | solution.py:395
  62.6 19.6 %collective-permute-start.7 = (bf16[512,768]{1,0:T(8,128)(2,1)S(1)}, bf16[512,768]{1,0:T(8,128)(2,1)S(1)}, u32[]{:S(2)}, u32[]{:S(2)}) collective-permute-start(bf16[512,768]{1,0:T(8,128)(2,1)S(1)} %chip_sum.2.refs_5_), channel_id=1, source_target_pairs={{0,2},{1,3},{2,0},{3,1},{4,6},{5,7},{6,4},{7,5},{8,10},{9,11},{10,... | collective-permute-start | bytes 2359304 | tf_op jit(solution)/shard_map/ppermute | solution.py:399
  75.2 9.2 %collective-permute-start.6 = (bf16[2,512,768]{2,1,0:T(8,128)(2,1)S(1)}, bf16[2,512,768]{2,1,0:T(8,128)(2,1)S(1)}, u32[]{:S(2)}, u32[]{:S(2)}) collective-permute-start(bf16[2,512,768]{2,1,0:T(8,128)(2,1)S(1)} %get-tuple-element.30), channel_id=1, source_target_pairs={{0,1},{1,0},{2,3},{3,2},{4,5},{5,4},{6,7},{7,6},{8,9},{9,8},{10,11... | collective-permute-start | bytes 4718600 | tf_op jit(solution)/shard_map/ppermute | solution.py:395
  82.9 12.1 %collective-permute-start.9 = (bf16[768,256]{1,0:T(8,128)(2,1)S(1)}, bf16[768,256]{1,0:T(8,128)(2,1)S(1)}, u32[]{:S(2)}, u32[]{:S(2)}) collective-permute-start(bf16[768,256]{1,0:T(8,128)(2,1)S(1)} %hidden.2._.refs_0_), channel_id=1, source_target_pairs={{0,2},{1,3},{2,0},{3,1},{4,6},{5,7},{6,4},{7,5},{8,10},{9,11},{10,... | collective-permute-start | bytes 1179656 | tf_op jit(solution)/shard_map/ppermute | solution.py:402
  84.6 25.5 %collective-permute-start.8 = (bf16[512,768]{1,0:T(8,128)(2,1)S(1)}, bf16[512,768]{1,0:T(8,128)(2,1)S(1)}, u32[]{:S(2)}, u32[]{:S(2)}) collective-permute-start(bf16[512,768]{1,0:T(8,128)(2,1)S(1)} %chip_sum.3.refs_9_), channel_id=1, source_target_pairs={{0,2},{1,3},{2,0},{3,1},{4,6},{5,7},{6,4},{7,5},{8,10},{9,11},{10,... | collective-permute-start | bytes 2359304 | tf_op jit(solution)/shard_map/ppermute | solution.py:399
  85.3 9.8 %collective-permute-start.10 = (bf16[768,256]{1,0:T(8,128)(2,1)S(1)}, bf16[768,256]{1,0:T(8,128)(2,1)S(1)}, u32[]{:S(2)}, u32[]{:S(2)}) collective-permute-start(bf16[768,256]{1,0:T(8,128)(2,1)S(1)} %hidden.2._.refs_0_), channel_id=1, source_target_pairs={{0,1},{1,0},{2,3},{3,2},{4,5},{5,4},{6,7},{7,6},{8,9},{9,8},{10,11... | collective-permute-start | bytes 1179656 | tf_op jit(solution)/shard_map/ppermute | solution.py:403
  95.0 1.7 %collective-permute-start.11 = (bf16[768,256]{1,0:T(8,128)(2,1)S(1)}, bf16[768,256]{1,0:T(8,128)(2,1)S(1)}, u32[]{:S(2)}, u32[]{:S(2)}) collective-permute-start(bf16[768,256]{1,0:T(8,128)(2,1)S(1)} %collective-permute-done.9.refs_1_), channel_id=1, source_target_pairs={{0,1},{1,0},{2,3},{3,2},{4,5},{5,4},{6,7},{7,6},{8,9},{9,8},{10,11... | collective-permute-start | bytes 1179656 | tf_op jit(solution)/shard_map/ppermute | solution.py:404
  110.9 9.5 %collective-permute-start.12 = (bf16[768,256]{1,0:T(8,128)(2,1)S(1)}, bf16[768,256]{1,0:T(8,128)(2,1)S(1)}, u32[]{:S(2)}, u32[]{:S(2)}) collective-permute-start(bf16[768,256]{1,0:T(8,128)(2,1)S(1)} %hidden.3.refs_0_.refs_9_), channel_id=1, source_target_pairs={{0,2},{1,3},{2,0},{3,1},{4,6},{5,7},{6,4},{7,5},{8,10},{9,11},{10,... | collective-permute-start | bytes 1179656 | tf_op jit(solution)/shard_map/ppermute | solution.py:402
  112.4 7.9 %collective-permute-start.13 = (bf16[768,256]{1,0:T(8,128)(2,1)S(1)}, bf16[768,256]{1,0:T(8,128)(2,1)S(1)}, u32[]{:S(2)}, u32[]{:S(2)}) collective-permute-start(bf16[768,256]{1,0:T(8,128)(2,1)S(1)} %hidden.3.refs_0_.refs_9_), channel_id=1, source_target_pairs={{0,1},{1,0},{2,3},{3,2},{4,5},{5,4},{6,7},{7,6},{8,9},{9,8},{10,11... | collective-permute-start | bytes 1179656 | tf_op jit(solution)/shard_map/ppermute | solution.py:403
  120.3 1.7 %collective-permute-start.14 = (bf16[768,256]{1,0:T(8,128)(2,1)S(1)}, bf16[768,256]{1,0:T(8,128)(2,1)S(1)}, u32[]{:S(2)}, u32[]{:S(2)}) collective-permute-start(bf16[768,256]{1,0:T(8,128)(2,1)S(1)} %collective-permute-done.12.refs_1_), channel_id=1, source_target_pairs={{0,1},{1,0},{2,3},{3,2},{4,5},{5,4},{6,7},{7,6},{8,9},{9,8},{10,11... | collective-permute-start | bytes 1179656 | tf_op jit(solution)/shard_map/ppermute | solution.py:404
  128.5 12.3 %collective-permute-start.15 = (bf16[192,1280]{1,0:T(8,128)(2,1)S(1)}, bf16[192,1280]{1,0:T(8,128)(2,1)S(1)}, u32[]{:S(2)}, u32[]{:S(2)}) collective-permute-start(bf16[192,1280]{1,0:T(8,128)(2,1)S(1)} %get-tuple-element.36.a_ref), channel_id=1, source_target_pairs={{0,4},{12,8},{1,5},{13,9},{2,6},{14,10},{3,7},{15,11},{16,20},{28,... | collective-permute-start | bytes 1474568 | tf_op jit(solution)/shard_map/ppermute | solution.py:382
  140.9 7.5 %collective-permute-start.18 = (bf16[192,1280]{1,0:T(8,128)(2,1)S(1)}, bf16[192,1280]{1,0:T(8,128)(2,1)S(1)}, u32[]{:S(2)}, u32[]{:S(2)}) collective-permute-start(bf16[192,1280]{1,0:T(8,128)(2,1)S(1)} %get-tuple-element.40), channel_id=1, source_target_pairs={{4,8},{8,4},{5,9},{9,5},{6,10},{10,6},{7,11},{11,7},{20,24},{24,20... | collective-permute-start | bytes 1474568 | tf_op jit(solution)/shard_map/ppermute | solution.py:382
  141.6 18.0 %collective-permute-start.16 = (bf16[192,1280]{1,0:T(8,128)(2,1)S(1)}, bf16[192,1280]{1,0:T(8,128)(2,1)S(1)}, u32[]{:S(2)}, u32[]{:S(2)}) collective-permute-start(bf16[192,1280]{1,0:T(8,128)(2,1)S(1)} %get-tuple-element.38), channel_id=1, source_target_pairs={{0,4},{12,8},{1,5},{13,9},{2,6},{14,10},{3,7},{15,11},{16,20},{28,... | collective-permute-start | bytes 1474568 | tf_op jit(solution)/shard_map/ppermute | solution.py:382
  148.6 20.2 %collective-permute-start.19 = (bf16[192,1280]{1,0:T(8,128)(2,1)S(1)}, bf16[192,1280]{1,0:T(8,128)(2,1)S(1)}, u32[]{:S(2)}, u32[]{:S(2)}) collective-permute-start(bf16[192,1280]{1,0:T(8,128)(2,1)S(1)} %add_convert_fusion.1), channel_id=1, source_target_pairs={{0,4},{4,0},{8,12},{12,8},{1,5},{5,1},{9,13},{13,9},{2,6},{6,2},{1... | collective-permute-start | bytes 1474568 | tf_op jit(solution)/shard_map/ppermute | solution.py:382
  159.8 9.0 %collective-permute-start.17 = (bf16[192,1280]{1,0:T(8,128)(2,1)S(1)}, bf16[192,1280]{1,0:T(8,128)(2,1)S(1)}, u32[]{:S(2)}, u32[]{:S(2)}) collective-permute-start(bf16[192,1280]{1,0:T(8,128)(2,1)S(1)} %add_convert_fusion.2), channel_id=1, source_target_pairs={{4,8},{8,4},{5,9},{9,5},{6,10},{10,6},{7,11},{11,7},{20,24},{24,20... | collective-permute-start | bytes 1474568 | tf_op jit(solution)/shard_map/ppermute | solution.py:382

commit v7 on v4

--- a/solution.py
+++ b/solution.py
@@ -346,25 +346,6 @@
     )(where, *hidden, *routes, down_weight, after, *carried)
 
 
-def plus_kernel(a_ref, b_ref, _, out_ref, __):
-    out_ref[...] = (a_ref[...].astype(F32) + b_ref[...].astype(F32)).astype(BF16)
-
-
-def plus_then(a, b, other):
-    whole = pl.BlockSpec(memory_space=pltpu.VMEM)
-    free = pl.BlockSpec(memory_space=pl.ANY)
-    return pl.pallas_call(
-        plus_kernel,
-        out_shape=(jax.ShapeDtypeStruct(a.shape, a.dtype), jax.ShapeDtypeStruct(a.shape, a.dtype)),
-        in_specs=[whole, whole, free],
-        out_specs=(whole, free),
-        input_output_aliases={2: 1},
-        compiler_params=params(4),
-        cost_estimate=QUICK,
-        name="plus",
-    )(a, b, other)
-
-
 def local_square(tokens, expert_ids, gate_weights, gu_weight, down_weight):
     z, t = lax.axis_index("ep"), lax.axis_index("tp")
     x, core = t // 2, t % 2
@@ -414,9 +395,8 @@
         return (a.astype(F32) + b.astype(F32)).astype(BF16)
 
     out_inner = hop(far_out, INWARD)
-    far_out, far_in = plus_then(far_out, out_inner, far_in)
-    out_mid = hop(far_out, MIDDLE)
     in_inner = hop(far_in, INWARD)
+    out_mid = hop(plus(far_out, out_inner), MIDDLE)
     last = hop(plus(other, out_mid), PAIR)
     in_mid = hop(plus(far_in, in_inner), MIDDLE)
     return (own.astype(F32) + in_mid.astype(F32) + last.astype(F32)).astype(BF16)

time: 172 us -> 169 us (0.983); the launches traced: 169 us -> 168 us
  starting transfers between devices: 31.6 us -> 22.4 us
  waiting for transfers between devices: 92.8 us -> 101 us
    ppermute x10, starting transfers between devices: 26.2 us -> 17 us  [hop(): return lax.ppermute(array, 'ep', pairs)]
    ppermute x10, waiting for transfers between devices: 54.4 us -> 62.6 us  [hop(): return lax.ppermute(array, 'ep', pairs)]
where the time goes in v7:
time: 169 us; the launch traced here: 168 us
  waiting for transfers between devices  101 us (60%)
  Pallas kernels  41 us (24%)
  starting transfers between devices  22.4 us (13%)
  other arithmetic  2.79 us (2%)
    ppermute x10, waiting for transfers between devices, hop(): return lax.ppermute(array, 'ep', pairs)  62.6 us
    pallas_call x2, Pallas kernels, gate_up(): pl.pallas_call(functools.partial(gate_up_kernel, n_blocks), grid=(group,)...  22.1 us
    ppermute x2, waiting for transfers between devices, gathered(): own_x = lax.ppermute(own, 'tp', ACROSS_X)  17.7 us
    ppermute x10, starting transfers between devices, hop(): return lax.ppermute(array, 'ep', pairs)  17 us
    ppermute x2, waiting for transfers between devices, across(): return (total, lax.ppermute(total, 'tp', ACROSS_X))  13.9 us
    pallas_call x2, Pallas kernels, down(): pl.pallas_call(functools.partial(down_kernel, group, n_blocks, chunk, car...  12.7 us
    pallas_call x4, Pallas kernels, place(): pl.pallas_call(functools.partial(place_kernel, experts), out_shape=(jax.S...  4.36 us
    ppermute x2, waiting for transfers between devices, gathered(): return (own, own_x, own_core, lax.ppermute(own_x, 'tp', ACROSS_CORE))  3.43 us
  transfers between devices with their start and end apart: 20, of which 13 were waited for; matrix products, arithmetic and copies ran while one was open for 0% of the time, Pallas kernels for 13%

profile of v7, /device:TPU:0, one launch (start us, length us, event | category | flops | bytes accessed | tf_op | source)
XLA Modules:
  0.0 168.5 jit_solution(7965579173978946685)
XLA Ops:
  1.4 1.0 copy-done
  2.5 3.1 %collective-permute-start = (bf16[208,1280]{1,0:T(8,128)(2,1)S(1)}, bf16[208,1280]{1,0:T(8,128)(2,1)S(1)}, u32[]{:S(2)}, u32[]{:S(2)}) collective-permute-start(bf16[208,1280]{1,0:T(8,128)(2,1)S(1)} %pack.1.refs_0_), channel_id=1, source_target_pairs={{0,4},{4,0},{8,12},{12,8},{1,5},{5,1},{9,13},{13,9},{2,6},{6,2},{1... | collective-permute-start | bytes 1597448 | tf_op jit(solution)/shard_map/ppermute | solution.py:357
  6.2 11.4 %collective-permute-done.refs_0_ = bf16[208,1280]{1,0:T(8,128)(2,1)S(1)} collective-permute-done((bf16[208,1280]{1,0:T(8,128)(2,1)S(1)}, bf16[208,1280]{1,0:T(8,128)(2,1)S(1)}, u32[]{:S(2)}, u32[]{:S(2)}) %collective-permute-start) | collective-permute-done | bytes 532512 | tf_op jit(solution)/shard_map/ppermute | solution.py:357
  18.4 1.3 collective-permute-start.2
  19.7 1.3 collective-permute-start.4
  21.1 1.1 place.4
  22.1 1.1 place.5
  23.2 12.5 %collective-permute-done.2.refs_1_ = bf16[208,1280]{1,0:T(8,128)(2,1)S(1)} collective-permute-done((bf16[208,1280]{1,0:T(8,128)(2,1)S(1)}, bf16[208,1280]{1,0:T(8,128)(2,1)S(1)}, u32[]{:S(2)}, u32[]{:S(2)}) %collective-permute-start.2) | collective-permute-done | bytes 532512 | tf_op jit(solution)/shard_map/ppermute | solution.py:357
  35.7 1.1 place.6
  36.8 9.7 %collective-permute-done.4.refs_1_ = bf16[208,1280]{1,0:T(8,128)(2,1)S(1)} collective-permute-done((bf16[208,1280]{1,0:T(8,128)(2,1)S(1)}, bf16[208,1280]{1,0:T(8,128)(2,1)S(1)}, u32[]{:S(2)}, u32[]{:S(2)}) %collective-permute-start.4) | collective-permute-done | bytes 532512 | tf_op jit(solution)/shard_map/ppermute | solution.py:357
  46.5 1.1 place.7
  47.6 11.0 %gate_up.2 = (bf16[2,512,768]{2,1,0:T(8,128)(2,1)S(1)}, bf16[2,512,768]{2,1,0:T(8,128)(2,1)S(1)}) custom-call(s32[3]{0:T(128)S(1)} %pad_add_fusion.where_ref, bf16[8,48,1280]{2,1,0:T(8,128)(2,1)S(1)} %get-tuple-element.21.refs_0_, bf16[8,48,1280]{2,1,0:T(8,128)(2,1)S(1)} %get-tuple-element.22.refs_1_, bf16[8,48,1280]{2,1,0:T(8,128)(2,1)S(1)} %get-tuple-element.23.refs_2_, ...), custom_call_target="tpu_custom_call" | custom-call | flops 1024 | bytes 1024 | tf_op jit(solution)/shard_map/gate_up/pallas_call | solution.py:190
  58.7 3.4 %collective-permute-done.5.near_ref = bf16[2,512,768]{2,1,0:T(8,128)(2,1)S(1)} collective-permute-done((bf16[2,512,768]{2,1,0:T(8,128)(2,1)S(1)}, bf16[2,512,768]{2,1,0:T(8,128)(2,1)S(1)}, u32[]{:S(2)}, u32[]{:S(2)}) %collective-permute-start.5) | collective-permute-done | bytes 1572896 | tf_op jit(solution)/shard_map/ppermute | solution.py:370
  62.3 1.6 collective-permute-start.7
  63.8 11.1 %gate_up.3 = (bf16[2,512,768]{2,1,0:T(8,128)(2,1)S(1)}, bf16[2,512,768]{2,1,0:T(8,128)(2,1)S(1)}) custom-call(s32[3]{0:T(128)S(1)} %pad_add_fusion.where_ref, bf16[8,48,1280]{2,1,0:T(8,128)(2,1)S(1)} %get-tuple-element.21.refs_0_, bf16[8,48,1280]{2,1,0:T(8,128)(2,1)S(1)} %get-tuple-element.22.refs_1_, bf16[8,48,1280]{2,1,0:T(8,128)(2,1)S(1)} %get-tuple-element.23.refs_2_, ...), custom_call_target="tpu_custom_call" | custom-call | flops 1024 | bytes 1024 | tf_op jit(solution)/shard_map/gate_up/pallas_call | solution.py:190
  75.0 6.9 %collective-permute-done.7.far_ref = bf16[512,768]{1,0:T(8,128)(2,1)S(1)} collective-permute-done((bf16[512,768]{1,0:T(8,128)(2,1)S(1)}, bf16[512,768]{1,0:T(8,128)(2,1)S(1)}, u32[]{:S(2)}, u32[]{:S(2)}) %collective-permute-start.7) | collective-permute-done | bytes 786464 | tf_op jit(solution)/shard_map/ppermute | solution.py:374
  82.6 1.6 collective-permute-start.9
  85.0 9.8 %collective-permute-done.9.refs_1_ = bf16[768,256]{1,0:T(8,128)(2,1)S(1)} collective-permute-done((bf16[768,256]{1,0:T(8,128)(2,1)S(1)}, bf16[768,256]{1,0:T(8,128)(2,1)S(1)}, u32[]{:S(2)}, u32[]{:S(2)}) %collective-permute-start.9) | collective-permute-done | bytes 393248 | tf_op jit(solution)/shard_map/ppermute | solution.py:377
  94.7 1.7 %collective-permute-done.11.refs_3_ = bf16[768,256]{1,0:T(8,128)(2,1)S(1)} collective-permute-done((bf16[768,256]{1,0:T(8,128)(2,1)S(1)}, bf16[768,256]{1,0:T(8,128)(2,1)S(1)}, u32[]{:S(2)}, u32[]{:S(2)}) %collective-permute-start.11) | collective-permute-done | bytes 393248 | tf_op jit(solution)/shard_map/ppermute | solution.py:379
  96.5 6.3 %down.2._.refs_10_ = f32[4,192,1280]{2,1,0:T(8,128)S(1)} custom-call(s32[3]{0:T(128)S(1)} %pad_add_fusion.where_ref, bf16[768,256]{1,0:T(8,128)(2,1)S(1)} %hidden.2._.refs_0_, bf16[768,256]{1,0:T(8,128)(2,1)S(1)} %collective-permute-done.9.refs_1_, bf16[768,256]{1,0:T(8,128)(2,1)S(1)} %collective-permute-done.10.refs_2_, ...), custom_call_target="tpu_custom_call" | custom-call | flops 1024 | bytes 1024 | tf_op jit(solution)/shard_map/down/pallas_call | solution.py:330
  102.8 7.1 %collective-permute-done.8.far_ref = bf16[512,768]{1,0:T(8,128)(2,1)S(1)} collective-permute-done((bf16[512,768]{1,0:T(8,128)(2,1)S(1)}, bf16[512,768]{1,0:T(8,128)(2,1)S(1)}, u32[]{:S(2)}, u32[]{:S(2)}) %collective-permute-start.8) | collective-permute-done | bytes 786464 | tf_op jit(solution)/shard_map/ppermute | solution.py:374
  110.6 1.6 collective-permute-start.12
  112.1 7.9 %collective-permute-done.12.refs_1_ = bf16[768,256]{1,0:T(8,128)(2,1)S(1)} collective-permute-done((bf16[768,256]{1,0:T(8,128)(2,1)S(1)}, bf16[768,256]{1,0:T(8,128)(2,1)S(1)}, u32[]{:S(2)}, u32[]{:S(2)}) %collective-permute-start.12) | collective-permute-done | bytes 393248 | tf_op jit(solution)/shard_map/ppermute | solution.py:377
  120.0 1.7 %collective-permute-done.14.refs_3_ = bf16[768,256]{1,0:T(8,128)(2,1)S(1)} collective-permute-done((bf16[768,256]{1,0:T(8,128)(2,1)S(1)}, bf16[768,256]{1,0:T(8,128)(2,1)S(1)}, u32[]{:S(2)}, u32[]{:S(2)}) %collective-permute-start.14) | collective-permute-done | bytes 393248 | tf_op jit(solution)/shard_map/ppermute | solution.py:379
  121.8 6.4 %down.3 = (bf16[192,1280]{1,0:T(8,128)(2,1)S(1)}, bf16[192,1280]{1,0:T(8,128)(2,1)S(1)}, bf16[192,1280]{1,0:T(8,128)(2,1)S(1)}, bf16[192,1280]{1,0:T(8,128)(2,1)S(1)}) custom-call(s32[3]{0:T(128)S(1)} %pad_add_fusion.where_ref, bf16[768,256]{1,0:T(8,128)(2,1)S(1)} %hidden.3.refs_0_.refs_9_, bf16[768,256]{1,0:T(8,128)(2,1)S(1)} %collective-permute-done.12.refs_1_, ...), custom_call_target="tpu_custom_call" | custom-call | flops 1024 | bytes 1024 | tf_op jit(solution)/shard_map/down/pallas_call | solution.py:330
  128.2 1.5 collective-permute-start.17
  129.7 1.3 collective-permute-start.15
  131.0 10.2 %collective-permute-done.17 = bf16[192,1280]{1,0:T(8,128)(2,1)S(1)} collective-permute-done((bf16[192,1280]{1,0:T(8,128)(2,1)S(1)}, bf16[192,1280]{1,0:T(8,128)(2,1)S(1)}, u32[]{:S(2)}, u32[]{:S(2)}) %collective-permute-start.17) | collective-permute-done | bytes 491552 | tf_op jit(solution)/shard_map/ppermute | solution.py:357
  142.0 9.0 %collective-permute-done.15 = bf16[192,1280]{1,0:T(8,128)(2,1)S(1)} collective-permute-done((bf16[192,1280]{1,0:T(8,128)(2,1)S(1)}, bf16[192,1280]{1,0:T(8,128)(2,1)S(1)}, u32[]{:S(2)}, u32[]{:S(2)}) %collective-permute-start.15) | collective-permute-done | bytes 491552 | tf_op jit(solution)/shard_map/ppermute | solution.py:357
  152.0 5.7 %collective-permute-start.19 = (bf16[192,1280]{1,0:T(8,128)(2,1)S(1)}, bf16[192,1280]{1,0:T(8,128)(2,1)S(1)}, u32[]{:S(2)}, u32[]{:S(2)}) collective-permute-start(bf16[192,1280]{1,0:T(8,128)(2,1)S(1)} %add_convert_fusion.1), channel_id=1, source_target_pairs={{0,4},{4,0},{8,12},{12,8},{1,5},{5,1},{9,13},{13,9},{2,6},{6,2},{1... | collective-permute-start | bytes 1474568 | tf_op jit(solution)/shard_map/ppermute | solution.py:357
  157.7 9.8 %collective-permute-done.19 = bf16[192,1280]{1,0:T(8,128)(2,1)S(1)} collective-permute-done((bf16[192,1280]{1,0:T(8,128)(2,1)S(1)}, bf16[192,1280]{1,0:T(8,128)(2,1)S(1)}, u32[]{:S(2)}, u32[]{:S(2)}) %collective-permute-start.19) | collective-permute-done | bytes 491552 | tf_op jit(solution)/shard_map/ppermute | solution.py:357
  167.5 1.0 add_convert_fusion
  (30 shorter events, 7.1 us)
Async XLA Ops:
  1.4 1.0 copy-start
  2.5 15.2 %collective-permute-start = (bf16[208,1280]{1,0:T(8,128)(2,1)S(1)}, bf16[208,1280]{1,0:T(8,128)(2,1)S(1)}, u32[]{:S(2)}, u32[]{:S(2)}) collective-permute-start(bf16[208,1280]{1,0:T(8,128)(2,1)S(1)} %pack.1.refs_0_), channel_id=1, source_target_pairs={{0,4},{4,0},{8,12},{12,8},{1,5},{5,1},{9,13},{13,9},{2,6},{6,2},{1... | collective-permute-start | bytes 1597448 | tf_op jit(solution)/shard_map/ppermute | solution.py:357
  5.6 12.8 %collective-permute-start.1 = (bf16[208,1280]{1,0:T(8,128)(2,1)S(1)}, bf16[208,1280]{1,0:T(8,128)(2,1)S(1)}, u32[]{:S(2)}, u32[]{:S(2)}) collective-permute-start(bf16[208,1280]{1,0:T(8,128)(2,1)S(1)} %pack.1.refs_0_), channel_id=1, source_target_pairs={{4,8},{8,4},{5,9},{9,5},{6,10},{10,6},{7,11},{11,7},{20,24},{24,20... | collective-permute-start | bytes 1597448 | tf_op jit(solution)/shard_map/ppermute | solution.py:357
  17.7 2.0 %collective-permute-start.3 = (bf16[208,1280]{1,0:T(8,128)(2,1)S(1)}, bf16[208,1280]{1,0:T(8,128)(2,1)S(1)}, u32[]{:S(2)}, u32[]{:S(2)}) collective-permute-start(bf16[208,1280]{1,0:T(8,128)(2,1)S(1)} %collective-permute-done.refs_0_), channel_id=1, source_target_pairs={{4,8},{8,4},{5,9},{9,5},{6,10},{10,6},{7,11},{11,7},{20,24},{24,20... | collective-permute-start | bytes 1597448 | tf_op jit(solution)/shard_map/ppermute | solution.py:357
  18.4 17.4 %collective-permute-start.2 = (bf16[208,1280]{1,0:T(8,128)(2,1)S(1)}, bf16[208,1280]{1,0:T(8,128)(2,1)S(1)}, u32[]{:S(2)}, u32[]{:S(2)}) collective-permute-start(bf16[208,1280]{1,0:T(8,128)(2,1)S(1)} %collective-permute-done.1.refs_0_), channel_id=1, source_target_pairs={{4,0},{8,12},{5,1},{9,13},{6,2},{10,14},{7,3},{11,15},{20,16},{24,... | collective-permute-start | bytes 1597448 | tf_op jit(solution)/shard_map/ppermute | solution.py:357
  19.7 26.9 %collective-permute-start.4 = (bf16[208,1280]{1,0:T(8,128)(2,1)S(1)}, bf16[208,1280]{1,0:T(8,128)(2,1)S(1)}, u32[]{:S(2)}, u32[]{:S(2)}) collective-permute-start(bf16[208,1280]{1,0:T(8,128)(2,1)S(1)} %collective-permute-done.3.refs_0_), channel_id=1, source_target_pairs={{4,0},{8,12},{5,1},{9,13},{6,2},{10,14},{7,3},{11,15},{20,16},{24,... | collective-permute-start | bytes 1597448 | tf_op jit(solution)/shard_map/ppermute | solution.py:357
  58.6 3.5 %collective-permute-start.5 = (bf16[2,512,768]{2,1,0:T(8,128)(2,1)S(1)}, bf16[2,512,768]{2,1,0:T(8,128)(2,1)S(1)}, u32[]{:S(2)}, u32[]{:S(2)}) collective-permute-start(bf16[2,512,768]{2,1,0:T(8,128)(2,1)S(1)} %get-tuple-element.26), channel_id=1, source_target_pairs={{0,1},{1,0},{2,3},{3,2},{4,5},{5,4},{6,7},{7,6},{8,9},{9,8},{10,11... | collective-permute-start | bytes 4718600 | tf_op jit(solution)/shard_map/ppermute | solution.py:370
  62.3 19.6 %collective-permute-start.7 = (bf16[512,768]{1,0:T(8,128)(2,1)S(1)}, bf16[512,768]{1,0:T(8,128)(2,1)S(1)}, u32[]{:S(2)}, u32[]{:S(2)}) collective-permute-start(bf16[512,768]{1,0:T(8,128)(2,1)S(1)} %chip_sum.2.refs_5_), channel_id=1, source_target_pairs={{0,2},{1,3},{2,0},{3,1},{4,6},{5,7},{6,4},{7,5},{8,10},{9,11},{10,... | collective-permute-start | bytes 2359304 | tf_op jit(solution)/shard_map/ppermute | solution.py:374
  75.0 9.2 %collective-permute-start.6 = (bf16[2,512,768]{2,1,0:T(8,128)(2,1)S(1)}, bf16[2,512,768]{2,1,0:T(8,128)(2,1)S(1)}, u32[]{:S(2)}, u32[]{:S(2)}) collective-permute-start(bf16[2,512,768]{2,1,0:T(8,128)(2,1)S(1)} %get-tuple-element.28), channel_id=1, source_target_pairs={{0,1},{1,0},{2,3},{3,2},{4,5},{5,4},{6,7},{7,6},{8,9},{9,8},{10,11... | collective-permute-start | bytes 4718600 | tf_op jit(solution)/shard_map/ppermute | solution.py:370
  82.6 12.1 %collective-permute-start.9 = (bf16[768,256]{1,0:T(8,128)(2,1)S(1)}, bf16[768,256]{1,0:T(8,128)(2,1)S(1)}, u32[]{:S(2)}, u32[]{:S(2)}) collective-permute-start(bf16[768,256]{1,0:T(8,128)(2,1)S(1)} %hidden.2._.refs_0_), channel_id=1, source_target_pairs={{0,2},{1,3},{2,0},{3,1},{4,6},{5,7},{6,4},{7,5},{8,10},{9,11},{10,... | collective-permute-start | bytes 1179656 | tf_op jit(solution)/shard_map/ppermute | solution.py:377
  84.4 25.5 %collective-permute-start.8 = (bf16[512,768]{1,0:T(8,128)(2,1)S(1)}, bf16[512,768]{1,0:T(8,128)(2,1)S(1)}, u32[]{:S(2)}, u32[]{:S(2)}) collective-permute-start(bf16[512,768]{1,0:T(8,128)(2,1)S(1)} %chip_sum.3.refs_9_), channel_id=1, source_target_pairs={{0,2},{1,3},{2,0},{3,1},{4,6},{5,7},{6,4},{7,5},{8,10},{9,11},{10,... | collective-permute-start | bytes 2359304 | tf_op jit(solution)/shard_map/ppermute | solution.py:374
  85.0 9.8 %collective-permute-start.10 = (bf16[768,256]{1,0:T(8,128)(2,1)S(1)}, bf16[768,256]{1,0:T(8,128)(2,1)S(1)}, u32[]{:S(2)}, u32[]{:S(2)}) collective-permute-start(bf16[768,256]{1,0:T(8,128)(2,1)S(1)} %hidden.2._.refs_0_), channel_id=1, source_target_pairs={{0,1},{1,0},{2,3},{3,2},{4,5},{5,4},{6,7},{7,6},{8,9},{9,8},{10,11... | collective-permute-start | bytes 1179656 | tf_op jit(solution)/shard_map/ppermute | solution.py:378
  94.7 1.7 %collective-permute-start.11 = (bf16[768,256]{1,0:T(8,128)(2,1)S(1)}, bf16[768,256]{1,0:T(8,128)(2,1)S(1)}, u32[]{:S(2)}, u32[]{:S(2)}) collective-permute-start(bf16[768,256]{1,0:T(8,128)(2,1)S(1)} %collective-permute-done.9.refs_1_), channel_id=1, source_target_pairs={{0,1},{1,0},{2,3},{3,2},{4,5},{5,4},{6,7},{7,6},{8,9},{9,8},{10,11... | collective-permute-start | bytes 1179656 | tf_op jit(solution)/shard_map/ppermute | solution.py:379
  110.6 9.5 %collective-permute-start.12 = (bf16[768,256]{1,0:T(8,128)(2,1)S(1)}, bf16[768,256]{1,0:T(8,128)(2,1)S(1)}, u32[]{:S(2)}, u32[]{:S(2)}) collective-permute-start(bf16[768,256]{1,0:T(8,128)(2,1)S(1)} %hidden.3.refs_0_.refs_9_), channel_id=1, source_target_pairs={{0,2},{1,3},{2,0},{3,1},{4,6},{5,7},{6,4},{7,5},{8,10},{9,11},{10,... | collective-permute-start | bytes 1179656 | tf_op jit(solution)/shard_map/ppermute | solution.py:377
  112.1 7.9 %collective-permute-start.13 = (bf16[768,256]{1,0:T(8,128)(2,1)S(1)}, bf16[768,256]{1,0:T(8,128)(2,1)S(1)}, u32[]{:S(2)}, u32[]{:S(2)}) collective-permute-start(bf16[768,256]{1,0:T(8,128)(2,1)S(1)} %hidden.3.refs_0_.refs_9_), channel_id=1, source_target_pairs={{0,1},{1,0},{2,3},{3,2},{4,5},{5,4},{6,7},{7,6},{8,9},{9,8},{10,11... | collective-permute-start | bytes 1179656 | tf_op jit(solution)/shard_map/ppermute | solution.py:378
  120.0 1.7 %collective-permute-start.14 = (bf16[768,256]{1,0:T(8,128)(2,1)S(1)}, bf16[768,256]{1,0:T(8,128)(2,1)S(1)}, u32[]{:S(2)}, u32[]{:S(2)}) collective-permute-start(bf16[768,256]{1,0:T(8,128)(2,1)S(1)} %collective-permute-done.12.refs_1_), channel_id=1, source_target_pairs={{0,1},{1,0},{2,3},{3,2},{4,5},{5,4},{6,7},{7,6},{8,9},{9,8},{10,11... | collective-permute-start | bytes 1179656 | tf_op jit(solution)/shard_map/ppermute | solution.py:379
  128.2 13.0 %collective-permute-start.17 = (bf16[192,1280]{1,0:T(8,128)(2,1)S(1)}, bf16[192,1280]{1,0:T(8,128)(2,1)S(1)}, u32[]{:S(2)}, u32[]{:S(2)}) collective-permute-start(bf16[192,1280]{1,0:T(8,128)(2,1)S(1)} %get-tuple-element.36), channel_id=1, source_target_pairs={{0,4},{12,8},{1,5},{13,9},{2,6},{14,10},{3,7},{15,11},{16,20},{28,... | collective-permute-start | bytes 1474568 | tf_op jit(solution)/shard_map/ppermute | solution.py:357
  129.7 21.4 %collective-permute-start.15 = (bf16[192,1280]{1,0:T(8,128)(2,1)S(1)}, bf16[192,1280]{1,0:T(8,128)(2,1)S(1)}, u32[]{:S(2)}, u32[]{:S(2)}) collective-permute-start(bf16[192,1280]{1,0:T(8,128)(2,1)S(1)} %get-tuple-element.34), channel_id=1, source_target_pairs={{0,4},{12,8},{1,5},{13,9},{2,6},{14,10},{3,7},{15,11},{16,20},{28,... | collective-permute-start | bytes 1474568 | tf_op jit(solution)/shard_map/ppermute | solution.py:357
  141.3 10.5 %collective-permute-start.18 = (bf16[192,1280]{1,0:T(8,128)(2,1)S(1)}, bf16[192,1280]{1,0:T(8,128)(2,1)S(1)}, u32[]{:S(2)}, u32[]{:S(2)}) collective-permute-start(bf16[192,1280]{1,0:T(8,128)(2,1)S(1)} %add_convert_fusion.2), channel_id=1, source_target_pairs={{4,8},{8,4},{5,9},{9,5},{6,10},{10,6},{7,11},{11,7},{20,24},{24,20... | collective-permute-start | bytes 1474568 | tf_op jit(solution)/shard_map/ppermute | solution.py:357
  151.2 6.6 %collective-permute-start.16 = (bf16[192,1280]{1,0:T(8,128)(2,1)S(1)}, bf16[192,1280]{1,0:T(8,128)(2,1)S(1)}, u32[]{:S(2)}, u32[]{:S(2)}) collective-permute-start(bf16[192,1280]{1,0:T(8,128)(2,1)S(1)} %add_convert_fusion.3), channel_id=1, source_target_pairs={{4,8},{8,4},{5,9},{9,5},{6,10},{10,6},{7,11},{11,7},{20,24},{24,20... | collective-permute-start | bytes 1474568 | tf_op jit(solution)/shard_map/ppermute | solution.py:357
  152.0 15.5 %collective-permute-start.19 = (bf16[192,1280]{1,0:T(8,128)(2,1)S(1)}, bf16[192,1280]{1,0:T(8,128)(2,1)S(1)}, u32[]{:S(2)}, u32[]{:S(2)}) collective-permute-start(bf16[192,1280]{1,0:T(8,128)(2,1)S(1)} %add_convert_fusion.1), channel_id=1, source_target_pairs={{0,4},{4,0},{8,12},{12,8},{1,5},{5,1},{9,13},{13,9},{2,6},{6,2},{1... | collective-permute-start | bytes 1474568 | tf_op jit(solution)/shard_map/ppermute | solution.py:357

commit v8 on v6

--- a/solution.py
+++ b/solution.py
@@ -352,25 +352,6 @@
     )(where, *hidden, *routes, down_weight, after, *carried)
 
 
-def plus_kernel(a_ref, b_ref, _, out_ref, __):
-    out_ref[...] = (a_ref[...].astype(F32) + b_ref[...].astype(F32)).astype(BF16)
-
-
-def plus_then(a, b, other):
-    whole = pl.BlockSpec(memory_space=pltpu.VMEM)
-    free = pl.BlockSpec(memory_space=pl.ANY)
-    return pl.pallas_call(
-        plus_kernel,
-        out_shape=(jax.ShapeDtypeStruct(a.shape, a.dtype), jax.ShapeDtypeStruct(a.shape, a.dtype)),
-        in_specs=[whole, whole, free],
-        out_specs=(whole, free),
-        input_output_aliases={2: 1},
-        compiler_params=params(4),
-        cost_estimate=QUICK,
-        name="plus",
-    )(a, b, other)
-
-
 def local_square(tokens, expert_ids, gate_weights, gu_weight, down_weight):
     z, t = lax.axis_index("ep"), lax.axis_index("tp")
     x, core = t // 2, t % 2
@@ -420,9 +401,8 @@
         return (a.astype(F32) + b.astype(F32)).astype(BF16)
 
     out_inner = hop(far_out, INWARD)
-    far_out, far_in = plus_then(far_out, out_inner, far_in)
-    out_mid = hop(far_out, MIDDLE)
     in_inner = hop(far_in, INWARD)
+    out_mid = hop(plus(far_out, out_inner), MIDDLE)
     last = hop(plus(other, out_mid), PAIR)
     in_mid = hop(plus(far_in, in_inner), MIDDLE)
     return (own.astype(F32) + in_mid.astype(F32) + last.astype(F32)).astype(BF16)

time: 173 us -> 169 us (0.977); the launches traced: 170 us -> 169 us
  starting transfers between devices: 31.6 us -> 22.4 us
  waiting for transfers between devices: 92.8 us -> 101 us
    ppermute x10, starting transfers between devices: 26.2 us -> 17 us  [hop(): return lax.ppermute(array, 'ep', pairs)]
    ppermute x10, waiting for transfers between devices: 54.3 us -> 62.6 us  [hop(): return lax.ppermute(array, 'ep', pairs)]
where the time goes in v8:
time: 169 us
  waiting for transfers between devices  101 us (60%)
  Pallas kernels  41.3 us (24%)
  starting transfers between devices  22.4 us (13%)
  local copies, waits for them, and re-layouts  2.41 us (1%)
    ppermute x10, waiting for transfers between devices, hop(): return lax.ppermute(array, 'ep', pairs)  62.6 us
    pallas_call x2, Pallas kernels, gate_up(): pl.pallas_call(functools.partial(gate_up_kernel, n_blocks), grid=(group,)...  22.1 us
    ppermute x2, waiting for transfers between devices, gathered(): own_x = lax.ppermute(own, 'tp', ACROSS_X)  17.7 us
    ppermute x10, starting transfers between devices, hop(): return lax.ppermute(array, 'ep', pairs)  17 us
    ppermute x2, waiting for transfers between devices, across(): return (total, lax.ppermute(total, 'tp', ACROSS_X))  14 us
    pallas_call x2, Pallas kernels, down(): pl.pallas_call(functools.partial(down_kernel, group, n_blocks, chunk, car...  12.7 us
    pallas_call x4, Pallas kernels, place(): pl.pallas_call(functools.partial(place_kernel, experts), out_shape=(jax.S...  4.36 us
    ppermute x2, waiting for transfers between devices, gathered(): return (own, own_x, own_core, lax.ppermute(own_x, 'tp', ACROSS_CORE))  3.43 us
  transfers between devices with their start and end apart: 20, of which 13 were waited for; matrix products, arithmetic and copies ran while one was open for 0% of the time, Pallas kernels for 13%

profile of v8, /device:TPU:0, one launch (start us, length us, event | category | flops | bytes accessed | tf_op | source)
XLA Modules:
  0.0 168.8 jit_solution(16845047148318749248)
XLA Ops:
  0.0 1.0 copy-done
  2.7 3.1 %collective-permute-start = (bf16[208,1280]{1,0:T(8,128)(2,1)S(1)}, bf16[208,1280]{1,0:T(8,128)(2,1)S(1)}, u32[]{:S(2)}, u32[]{:S(2)}) collective-permute-start(bf16[208,1280]{1,0:T(8,128)(2,1)S(1)} %pack.1.refs_0_), channel_id=1, source_target_pairs={{0,4},{4,0},{8,12},{12,8},{1,5},{5,1},{9,13},{13,9},{2,6},{6,2},{1... | collective-permute-start | bytes 1597448 | tf_op jit(solution)/shard_map/ppermute | solution.py:363
  6.5 11.4 %collective-permute-done.refs_0_ = bf16[208,1280]{1,0:T(8,128)(2,1)S(1)} collective-permute-done((bf16[208,1280]{1,0:T(8,128)(2,1)S(1)}, bf16[208,1280]{1,0:T(8,128)(2,1)S(1)}, u32[]{:S(2)}, u32[]{:S(2)}) %collective-permute-start) | collective-permute-done | bytes 532512 | tf_op jit(solution)/shard_map/ppermute | solution.py:363
  18.6 1.3 collective-permute-start.2
  19.9 1.3 collective-permute-start.4
  21.3 1.1 place.4
  22.4 1.1 place.5
  23.5 12.5 %collective-permute-done.2.refs_1_ = bf16[208,1280]{1,0:T(8,128)(2,1)S(1)} collective-permute-done((bf16[208,1280]{1,0:T(8,128)(2,1)S(1)}, bf16[208,1280]{1,0:T(8,128)(2,1)S(1)}, u32[]{:S(2)}, u32[]{:S(2)}) %collective-permute-start.2) | collective-permute-done | bytes 532512 | tf_op jit(solution)/shard_map/ppermute | solution.py:363
  36.0 1.1 place.6
  37.1 9.7 %collective-permute-done.4.refs_1_ = bf16[208,1280]{1,0:T(8,128)(2,1)S(1)} collective-permute-done((bf16[208,1280]{1,0:T(8,128)(2,1)S(1)}, bf16[208,1280]{1,0:T(8,128)(2,1)S(1)}, u32[]{:S(2)}, u32[]{:S(2)}) %collective-permute-start.4) | collective-permute-done | bytes 532512 | tf_op jit(solution)/shard_map/ppermute | solution.py:363
  46.8 1.1 place.7
  47.9 11.0 %gate_up.2 = (bf16[2,512,768]{2,1,0:T(8,128)(2,1)S(1)}, bf16[2,512,768]{2,1,0:T(8,128)(2,1)S(1)}) custom-call(s32[3]{0:T(128)S(1)} %pad_add_fusion.where_ref, bf16[8,48,1280]{2,1,0:T(8,128)(2,1)S(1)} %get-tuple-element.21.refs_0_, bf16[8,48,1280]{2,1,0:T(8,128)(2,1)S(1)} %get-tuple-element.22.refs_1_, bf16[8,48,1280]{2,1,0:T(8,128)(2,1)S(1)} %get-tuple-element.23.refs_2_, ...), custom_call_target="tpu_custom_call" | custom-call | flops 1024 | bytes 1024 | tf_op jit(solution)/shard_map/gate_up/pallas_call | solution.py:196
  59.0 3.4 %collective-permute-done.5.near_ref = bf16[2,512,768]{2,1,0:T(8,128)(2,1)S(1)} collective-permute-done((bf16[2,512,768]{2,1,0:T(8,128)(2,1)S(1)}, bf16[2,512,768]{2,1,0:T(8,128)(2,1)S(1)}, u32[]{:S(2)}, u32[]{:S(2)}) %collective-permute-start.5) | collective-permute-done | bytes 1572896 | tf_op jit(solution)/shard_map/ppermute | solution.py:376
  62.6 1.5 collective-permute-start.7
  64.1 11.1 %gate_up.3 = (bf16[2,512,768]{2,1,0:T(8,128)(2,1)S(1)}, bf16[2,512,768]{2,1,0:T(8,128)(2,1)S(1)}) custom-call(s32[3]{0:T(128)S(1)} %pad_add_fusion.where_ref, bf16[8,48,1280]{2,1,0:T(8,128)(2,1)S(1)} %get-tuple-element.21.refs_0_, bf16[8,48,1280]{2,1,0:T(8,128)(2,1)S(1)} %get-tuple-element.22.refs_1_, bf16[8,48,1280]{2,1,0:T(8,128)(2,1)S(1)} %get-tuple-element.23.refs_2_, ...), custom_call_target="tpu_custom_call" | custom-call | flops 1024 | bytes 1024 | tf_op jit(solution)/shard_map/gate_up/pallas_call | solution.py:196
  75.3 6.9 %collective-permute-done.7.far_ref = bf16[512,768]{1,0:T(8,128)(2,1)S(1)} collective-permute-done((bf16[512,768]{1,0:T(8,128)(2,1)S(1)}, bf16[512,768]{1,0:T(8,128)(2,1)S(1)}, u32[]{:S(2)}, u32[]{:S(2)}) %collective-permute-start.7) | collective-permute-done | bytes 786464 | tf_op jit(solution)/shard_map/ppermute | solution.py:380
  82.9 1.5 collective-permute-start.9
  85.3 9.8 %collective-permute-done.9.refs_1_ = bf16[768,256]{1,0:T(8,128)(2,1)S(1)} collective-permute-done((bf16[768,256]{1,0:T(8,128)(2,1)S(1)}, bf16[768,256]{1,0:T(8,128)(2,1)S(1)}, u32[]{:S(2)}, u32[]{:S(2)}) %collective-permute-start.9) | collective-permute-done | bytes 393248 | tf_op jit(solution)/shard_map/ppermute | solution.py:383
  95.0 1.7 %collective-permute-done.11.refs_3_ = bf16[768,256]{1,0:T(8,128)(2,1)S(1)} collective-permute-done((bf16[768,256]{1,0:T(8,128)(2,1)S(1)}, bf16[768,256]{1,0:T(8,128)(2,1)S(1)}, u32[]{:S(2)}, u32[]{:S(2)}) %collective-permute-start.11) | collective-permute-done | bytes 393248 | tf_op jit(solution)/shard_map/ppermute | solution.py:385
  96.7 6.3 %down.2._.refs_10_ = f32[4,192,1280]{2,1,0:T(8,128)S(1)} custom-call(s32[3]{0:T(128)S(1)} %pad_add_fusion.where_ref, bf16[768,256]{1,0:T(8,128)(2,1)S(1)} %hidden.2._.refs_0_, bf16[768,256]{1,0:T(8,128)(2,1)S(1)} %collective-permute-done.9.refs_1_, bf16[768,256]{1,0:T(8,128)(2,1)S(1)} %collective-permute-done.10.refs_2_, ...), custom_call_target="tpu_custom_call" | custom-call | flops 1024 | bytes 1024 | tf_op jit(solution)/shard_map/down/pallas_call | solution.py:336
  103.1 7.1 %collective-permute-done.8.far_ref = bf16[512,768]{1,0:T(8,128)(2,1)S(1)} collective-permute-done((bf16[512,768]{1,0:T(8,128)(2,1)S(1)}, bf16[512,768]{1,0:T(8,128)(2,1)S(1)}, u32[]{:S(2)}, u32[]{:S(2)}) %collective-permute-start.8) | collective-permute-done | bytes 786464 | tf_op jit(solution)/shard_map/ppermute | solution.py:380
  110.9 1.5 collective-permute-start.12
  112.4 7.9 %collective-permute-done.12.refs_1_ = bf16[768,256]{1,0:T(8,128)(2,1)S(1)} collective-permute-done((bf16[768,256]{1,0:T(8,128)(2,1)S(1)}, bf16[768,256]{1,0:T(8,128)(2,1)S(1)}, u32[]{:S(2)}, u32[]{:S(2)}) %collective-permute-start.12) | collective-permute-done | bytes 393248 | tf_op jit(solution)/shard_map/ppermute | solution.py:383
  120.3 1.7 %collective-permute-done.14.refs_3_ = bf16[768,256]{1,0:T(8,128)(2,1)S(1)} collective-permute-done((bf16[768,256]{1,0:T(8,128)(2,1)S(1)}, bf16[768,256]{1,0:T(8,128)(2,1)S(1)}, u32[]{:S(2)}, u32[]{:S(2)}) %collective-permute-start.14) | collective-permute-done | bytes 393248 | tf_op jit(solution)/shard_map/ppermute | solution.py:385
  122.1 6.4 %down.3 = (bf16[192,1280]{1,0:T(8,128)(2,1)S(1)}, bf16[192,1280]{1,0:T(8,128)(2,1)S(1)}, bf16[192,1280]{1,0:T(8,128)(2,1)S(1)}, bf16[192,1280]{1,0:T(8,128)(2,1)S(1)}) custom-call(s32[3]{0:T(128)S(1)} %pad_add_fusion.where_ref, bf16[768,256]{1,0:T(8,128)(2,1)S(1)} %hidden.3.refs_0_.refs_9_, bf16[768,256]{1,0:T(8,128)(2,1)S(1)} %collective-permute-done.12.refs_1_, ...), custom_call_target="tpu_custom_call" | custom-call | flops 1024 | bytes 1024 | tf_op jit(solution)/shard_map/down/pallas_call | solution.py:336
  128.5 1.5 collective-permute-start.17
  129.9 1.3 collective-permute-start.15
  131.3 10.2 %collective-permute-done.17 = bf16[192,1280]{1,0:T(8,128)(2,1)S(1)} collective-permute-done((bf16[192,1280]{1,0:T(8,128)(2,1)S(1)}, bf16[192,1280]{1,0:T(8,128)(2,1)S(1)}, u32[]{:S(2)}, u32[]{:S(2)}) %collective-permute-start.17) | collective-permute-done | bytes 491552 | tf_op jit(solution)/shard_map/ppermute | solution.py:363
  142.3 9.1 %collective-permute-done.15 = bf16[192,1280]{1,0:T(8,128)(2,1)S(1)} collective-permute-done((bf16[192,1280]{1,0:T(8,128)(2,1)S(1)}, bf16[192,1280]{1,0:T(8,128)(2,1)S(1)}, u32[]{:S(2)}, u32[]{:S(2)}) %collective-permute-start.15) | collective-permute-done | bytes 491552 | tf_op jit(solution)/shard_map/ppermute | solution.py:363
  152.3 5.8 %collective-permute-start.19 = (bf16[192,1280]{1,0:T(8,128)(2,1)S(1)}, bf16[192,1280]{1,0:T(8,128)(2,1)S(1)}, u32[]{:S(2)}, u32[]{:S(2)}) collective-permute-start(bf16[192,1280]{1,0:T(8,128)(2,1)S(1)} %add_convert_fusion.1), channel_id=1, source_target_pairs={{0,4},{4,0},{8,12},{12,8},{1,5},{5,1},{9,13},{13,9},{2,6},{6,2},{1... | collective-permute-start | bytes 1474568 | tf_op jit(solution)/shard_map/ppermute | solution.py:363
  158.1 9.7 %collective-permute-done.19 = bf16[192,1280]{1,0:T(8,128)(2,1)S(1)} collective-permute-done((bf16[192,1280]{1,0:T(8,128)(2,1)S(1)}, bf16[192,1280]{1,0:T(8,128)(2,1)S(1)}, u32[]{:S(2)}, u32[]{:S(2)}) %collective-permute-start.19) | collective-permute-done | bytes 491552 | tf_op jit(solution)/shard_map/ppermute | solution.py:363
  167.8 1.0 add_convert_fusion
  (32 shorter events, 7.4 us)
Async XLA Ops:
  0.0 1.0 copy-start
  1.0 0.7 copy-start.1
  1.7 0.7 copy-start.2
  2.7 15.2 %collective-permute-start = (bf16[208,1280]{1,0:T(8,128)(2,1)S(1)}, bf16[208,1280]{1,0:T(8,128)(2,1)S(1)}, u32[]{:S(2)}, u32[]{:S(2)}) collective-permute-start(bf16[208,1280]{1,0:T(8,128)(2,1)S(1)} %pack.1.refs_0_), channel_id=1, source_target_pairs={{0,4},{4,0},{8,12},{12,8},{1,5},{5,1},{9,13},{13,9},{2,6},{6,2},{1... | collective-permute-start | bytes 1597448 | tf_op jit(solution)/shard_map/ppermute | solution.py:363
  5.8 12.8 %collective-permute-start.1 = (bf16[208,1280]{1,0:T(8,128)(2,1)S(1)}, bf16[208,1280]{1,0:T(8,128)(2,1)S(1)}, u32[]{:S(2)}, u32[]{:S(2)}) collective-permute-start(bf16[208,1280]{1,0:T(8,128)(2,1)S(1)} %pack.1.refs_0_), channel_id=1, source_target_pairs={{4,8},{8,4},{5,9},{9,5},{6,10},{10,6},{7,11},{11,7},{20,24},{24,20... | collective-permute-start | bytes 1597448 | tf_op jit(solution)/shard_map/ppermute | solution.py:363
  17.9 2.0 %collective-permute-start.3 = (bf16[208,1280]{1,0:T(8,128)(2,1)S(1)}, bf16[208,1280]{1,0:T(8,128)(2,1)S(1)}, u32[]{:S(2)}, u32[]{:S(2)}) collective-permute-start(bf16[208,1280]{1,0:T(8,128)(2,1)S(1)} %collective-permute-done.refs_0_), channel_id=1, source_target_pairs={{4,8},{8,4},{5,9},{9,5},{6,10},{10,6},{7,11},{11,7},{20,24},{24,20... | collective-permute-start | bytes 1597448 | tf_op jit(solution)/shard_map/ppermute | solution.py:363
  18.6 17.4 %collective-permute-start.2 = (bf16[208,1280]{1,0:T(8,128)(2,1)S(1)}, bf16[208,1280]{1,0:T(8,128)(2,1)S(1)}, u32[]{:S(2)}, u32[]{:S(2)}) collective-permute-start(bf16[208,1280]{1,0:T(8,128)(2,1)S(1)} %collective-permute-done.1.refs_0_), channel_id=1, source_target_pairs={{4,0},{8,12},{5,1},{9,13},{6,2},{10,14},{7,3},{11,15},{20,16},{24,... | collective-permute-start | bytes 1597448 | tf_op jit(solution)/shard_map/ppermute | solution.py:363
  19.9 26.9 %collective-permute-start.4 = (bf16[208,1280]{1,0:T(8,128)(2,1)S(1)}, bf16[208,1280]{1,0:T(8,128)(2,1)S(1)}, u32[]{:S(2)}, u32[]{:S(2)}) collective-permute-start(bf16[208,1280]{1,0:T(8,128)(2,1)S(1)} %collective-permute-done.3.refs_0_), channel_id=1, source_target_pairs={{4,0},{8,12},{5,1},{9,13},{6,2},{10,14},{7,3},{11,15},{20,16},{24,... | collective-permute-start | bytes 1597448 | tf_op jit(solution)/shard_map/ppermute | solution.py:363
  58.9 3.5 %collective-permute-start.5 = (bf16[2,512,768]{2,1,0:T(8,128)(2,1)S(1)}, bf16[2,512,768]{2,1,0:T(8,128)(2,1)S(1)}, u32[]{:S(2)}, u32[]{:S(2)}) collective-permute-start(bf16[2,512,768]{2,1,0:T(8,128)(2,1)S(1)} %get-tuple-element.26), channel_id=1, source_target_pairs={{0,1},{1,0},{2,3},{3,2},{4,5},{5,4},{6,7},{7,6},{8,9},{9,8},{10,11... | collective-permute-start | bytes 4718600 | tf_op jit(solution)/shard_map/ppermute | solution.py:376
  62.6 19.6 %collective-permute-start.7 = (bf16[512,768]{1,0:T(8,128)(2,1)S(1)}, bf16[512,768]{1,0:T(8,128)(2,1)S(1)}, u32[]{:S(2)}, u32[]{:S(2)}) collective-permute-start(bf16[512,768]{1,0:T(8,128)(2,1)S(1)} %chip_sum.2.refs_5_), channel_id=1, source_target_pairs={{0,2},{1,3},{2,0},{3,1},{4,6},{5,7},{6,4},{7,5},{8,10},{9,11},{10,... | collective-permute-start | bytes 2359304 | tf_op jit(solution)/shard_map/ppermute | solution.py:380
  75.2 9.2 %collective-permute-start.6 = (bf16[2,512,768]{2,1,0:T(8,128)(2,1)S(1)}, bf16[2,512,768]{2,1,0:T(8,128)(2,1)S(1)}, u32[]{:S(2)}, u32[]{:S(2)}) collective-permute-start(bf16[2,512,768]{2,1,0:T(8,128)(2,1)S(1)} %get-tuple-element.28), channel_id=1, source_target_pairs={{0,1},{1,0},{2,3},{3,2},{4,5},{5,4},{6,7},{7,6},{8,9},{9,8},{10,11... | collective-permute-start | bytes 4718600 | tf_op jit(solution)/shard_map/ppermute | solution.py:376
  82.9 12.1 %collective-permute-start.9 = (bf16[768,256]{1,0:T(8,128)(2,1)S(1)}, bf16[768,256]{1,0:T(8,128)(2,1)S(1)}, u32[]{:S(2)}, u32[]{:S(2)}) collective-permute-start(bf16[768,256]{1,0:T(8,128)(2,1)S(1)} %hidden.2._.refs_0_), channel_id=1, source_target_pairs={{0,2},{1,3},{2,0},{3,1},{4,6},{5,7},{6,4},{7,5},{8,10},{9,11},{10,... | collective-permute-start | bytes 1179656 | tf_op jit(solution)/shard_map/ppermute | solution.py:383
  84.6 25.5 %collective-permute-start.8 = (bf16[512,768]{1,0:T(8,128)(2,1)S(1)}, bf16[512,768]{1,0:T(8,128)(2,1)S(1)}, u32[]{:S(2)}, u32[]{:S(2)}) collective-permute-start(bf16[512,768]{1,0:T(8,128)(2,1)S(1)} %chip_sum.3.refs_9_), channel_id=1, source_target_pairs={{0,2},{1,3},{2,0},{3,1},{4,6},{5,7},{6,4},{7,5},{8,10},{9,11},{10,... | collective-permute-start | bytes 2359304 | tf_op jit(solution)/shard_map/ppermute | solution.py:380
  85.3 9.8 %collective-permute-start.10 = (bf16[768,256]{1,0:T(8,128)(2,1)S(1)}, bf16[768,256]{1,0:T(8,128)(2,1)S(1)}, u32[]{:S(2)}, u32[]{:S(2)}) collective-permute-start(bf16[768,256]{1,0:T(8,128)(2,1)S(1)} %hidden.2._.refs_0_), channel_id=1, source_target_pairs={{0,1},{1,0},{2,3},{3,2},{4,5},{5,4},{6,7},{7,6},{8,9},{9,8},{10,11... | collective-permute-start | bytes 1179656 | tf_op jit(solution)/shard_map/ppermute | solution.py:384
  95.0 1.7 %collective-permute-start.11 = (bf16[768,256]{1,0:T(8,128)(2,1)S(1)}, bf16[768,256]{1,0:T(8,128)(2,1)S(1)}, u32[]{:S(2)}, u32[]{:S(2)}) collective-permute-start(bf16[768,256]{1,0:T(8,128)(2,1)S(1)} %collective-permute-done.9.refs_1_), channel_id=1, source_target_pairs={{0,1},{1,0},{2,3},{3,2},{4,5},{5,4},{6,7},{7,6},{8,9},{9,8},{10,11... | collective-permute-start | bytes 1179656 | tf_op jit(solution)/shard_map/ppermute | solution.py:385
  110.9 9.5 %collective-permute-start.12 = (bf16[768,256]{1,0:T(8,128)(2,1)S(1)}, bf16[768,256]{1,0:T(8,128)(2,1)S(1)}, u32[]{:S(2)}, u32[]{:S(2)}) collective-permute-start(bf16[768,256]{1,0:T(8,128)(2,1)S(1)} %hidden.3.refs_0_.refs_9_), channel_id=1, source_target_pairs={{0,2},{1,3},{2,0},{3,1},{4,6},{5,7},{6,4},{7,5},{8,10},{9,11},{10,... | collective-permute-start | bytes 1179656 | tf_op jit(solution)/shard_map/ppermute | solution.py:383
  112.4 7.9 %collective-permute-start.13 = (bf16[768,256]{1,0:T(8,128)(2,1)S(1)}, bf16[768,256]{1,0:T(8,128)(2,1)S(1)}, u32[]{:S(2)}, u32[]{:S(2)}) collective-permute-start(bf16[768,256]{1,0:T(8,128)(2,1)S(1)} %hidden.3.refs_0_.refs_9_), channel_id=1, source_target_pairs={{0,1},{1,0},{2,3},{3,2},{4,5},{5,4},{6,7},{7,6},{8,9},{9,8},{10,11... | collective-permute-start | bytes 1179656 | tf_op jit(solution)/shard_map/ppermute | solution.py:384
  120.3 1.7 %collective-permute-start.14 = (bf16[768,256]{1,0:T(8,128)(2,1)S(1)}, bf16[768,256]{1,0:T(8,128)(2,1)S(1)}, u32[]{:S(2)}, u32[]{:S(2)}) collective-permute-start(bf16[768,256]{1,0:T(8,128)(2,1)S(1)} %collective-permute-done.12.refs_1_), channel_id=1, source_target_pairs={{0,1},{1,0},{2,3},{3,2},{4,5},{5,4},{6,7},{7,6},{8,9},{9,8},{10,11... | collective-permute-start | bytes 1179656 | tf_op jit(solution)/shard_map/ppermute | solution.py:385
  128.5 13.0 %collective-permute-start.17 = (bf16[192,1280]{1,0:T(8,128)(2,1)S(1)}, bf16[192,1280]{1,0:T(8,128)(2,1)S(1)}, u32[]{:S(2)}, u32[]{:S(2)}) collective-permute-start(bf16[192,1280]{1,0:T(8,128)(2,1)S(1)} %get-tuple-element.36), channel_id=1, source_target_pairs={{0,4},{12,8},{1,5},{13,9},{2,6},{14,10},{3,7},{15,11},{16,20},{28,... | collective-permute-start | bytes 1474568 | tf_op jit(solution)/shard_map/ppermute | solution.py:363
  129.9 21.4 %collective-permute-start.15 = (bf16[192,1280]{1,0:T(8,128)(2,1)S(1)}, bf16[192,1280]{1,0:T(8,128)(2,1)S(1)}, u32[]{:S(2)}, u32[]{:S(2)}) collective-permute-start(bf16[192,1280]{1,0:T(8,128)(2,1)S(1)} %get-tuple-element.34), channel_id=1, source_target_pairs={{0,4},{12,8},{1,5},{13,9},{2,6},{14,10},{3,7},{15,11},{16,20},{28,... | collective-permute-start | bytes 1474568 | tf_op jit(solution)/shard_map/ppermute | solution.py:363
  141.6 10.6 %collective-permute-start.18 = (bf16[192,1280]{1,0:T(8,128)(2,1)S(1)}, bf16[192,1280]{1,0:T(8,128)(2,1)S(1)}, u32[]{:S(2)}, u32[]{:S(2)}) collective-permute-start(bf16[192,1280]{1,0:T(8,128)(2,1)S(1)} %add_convert_fusion.2), channel_id=1, source_target_pairs={{4,8},{8,4},{5,9},{9,5},{6,10},{10,6},{7,11},{11,7},{20,24},{24,20... | collective-permute-start | bytes 1474568 | tf_op jit(solution)/shard_map/ppermute | solution.py:363
  151.5 6.6 %collective-permute-start.16 = (bf16[192,1280]{1,0:T(8,128)(2,1)S(1)}, bf16[192,1280]{1,0:T(8,128)(2,1)S(1)}, u32[]{:S(2)}, u32[]{:S(2)}) collective-permute-start(bf16[192,1280]{1,0:T(8,128)(2,1)S(1)} %add_convert_fusion.3), channel_id=1, source_target_pairs={{4,8},{8,4},{5,9},{9,5},{6,10},{10,6},{7,11},{11,7},{20,24},{24,20... | collective-permute-start | bytes 1474568 | tf_op jit(solution)/shard_map/ppermute | solution.py:363
  152.3 15.5 %collective-permute-start.19 = (bf16[192,1280]{1,0:T(8,128)(2,1)S(1)}, bf16[192,1280]{1,0:T(8,128)(2,1)S(1)}, u32[]{:S(2)}, u32[]{:S(2)}) collective-permute-start(bf16[192,1280]{1,0:T(8,128)(2,1)S(1)} %add_convert_fusion.1), channel_id=1, source_target_pairs={{0,4},{4,0},{8,12},{12,8},{1,5},{5,1},{9,13},{13,9},{2,6},{6,2},{1... | collective-permute-start | bytes 1474568 | tf_op jit(solution)/shard_map/ppermute | solution.py:363
